TPU v7x, 32 devices: a whole 2x2x4 slice. The times are simulated.
32 devices in a mesh: groups: 2 (over y), tok: 16 (over z, x, core).
Axes of the slice: x: 2, y: 2, z: 4, core: 2. Of those that a mesh axis runs over, the one named last changes fastest.
Arguments:
- query_rows: bfloat16 [8192, 768], P(('groups', 'tok')), parts along dimension 0, may hold values from -6 to 6
- key_rows: bfloat16 [8192, 768], P(('groups', 'tok')), parts along dimension 0, may hold values from -6 to 6
- value_rows: bfloat16 [8192, 768], P(('groups', 'tok')), parts along dimension 0, may hold values from -6 to 6
- out_rows: bfloat16 [8192, 768], P(('groups', 'tok')), parts along dimension 0, may hold values from -6 to 6
- grad_out: bfloat16 [8192, 768], P(('groups', 'tok')), parts along dimension 0, may hold values from -6 to 6
- normalizer: float32 [16, 8192], P(None, ('groups', 'tok')), parts along dimension 1, may hold values from 3 to 5
- keep_tasks: int32 [32, 5], P('groups'), parts along dimension 0, may hold values from 0 to 1, as said below
Outputs:
- grad_query: bfloat16 [8192, 768], P(('groups', 'tok')), parts along dimension 0
- grad_key: bfloat16 [8192, 768], P(('groups', 'tok')), parts along dimension 0
- grad_value: bfloat16 [8192, 768], P(('groups', 'tok')), parts along dimension 0
There are 2 independent parts, one for each index of `groups`. A program takes and returns all parts, laid end to end along the dimension named above; each array names one. Nothing has to cross between parts.
Inputs may be any that keep to these rules, and one draw needn't show every extreme that they name: keep_tasks[a, 2] = 1 for every block a; entries naming a key block outside 0 to 15 are ignored.
All inputs are finite; a program needn't handle non-finite values.
Results may differ from a plain program's by a relative error of at most 0.0053.
Values may be sent and summed in bfloat16 or wider, within the bound.
No kernel may reach another device: no remote copies, remote signals or barrier semaphores. Data moves between devices by JAX's collectives and lax.ppermute only.
A program may use at most 128 MiB of HBM per device.

v0:
```python
import jax
import jax.numpy as jnp
from jax import lax
from jax.sharding import PartitionSpec as P

HEADS = 16
RADIUS = 2
WIN = 5


def shifted(value, axis, steps):
    count = lax.axis_size(axis)
    first, last = (max(0, -steps), min(count, count - steps))
    return lax.ppermute(value, axis, [(source, source + steps) for source in range(first, last)])


def split_heads(rows_in):
    return rows_in.reshape(rows_in.shape[0], HEADS, rows_in.shape[1] // HEADS)


def block_delta(dout_rows, out_rows):
    product = split_heads(dout_rows).astype(jnp.float32) * split_heads(out_rows).astype(jnp.float32)
    return jnp.transpose(jnp.sum(product, axis=2))


def scores_grads(query_rows, dout_rows, lse_rows, delta_rows, key_block, value_block, scale):
    q_heads = split_heads(query_rows)
    dout_heads = split_heads(dout_rows)
    k_heads = split_heads(key_block)
    v_heads = split_heads(value_block)
    scores = (
        jnp.einsum("qhe,khe->hqk", q_heads, k_heads, preferred_element_type=jnp.float32) * scale
    )
    probs = jnp.exp(scores - lse_rows[:, :, None])
    prob_grad = jnp.einsum("qhe,khe->hqk", dout_heads, v_heads, preferred_element_type=jnp.float32)
    score_grad = (probs * (prob_grad - delta_rows[:, :, None])).astype(jnp.bfloat16)
    probs_low = probs.astype(jnp.bfloat16)
    return (q_heads, dout_heads, k_heads, probs_low, score_grad)


def grad_of_query(parts, scale):
    q_heads, dout_heads, k_heads, probs_low, score_grad = parts
    term = (
        jnp.einsum("hqk,khe->qhe", score_grad, k_heads, preferred_element_type=jnp.float32) * scale
    )
    return term.reshape(term.shape[0], term.shape[1] * term.shape[2])


def grads_of_keys(parts, scale):
    q_heads, dout_heads, k_heads, probs_low, score_grad = parts
    term_k = (
        jnp.einsum("hqk,qhe->khe", score_grad, q_heads, preferred_element_type=jnp.float32) * scale
    )
    term_v = jnp.einsum("hqk,qhe->khe", probs_low, dout_heads, preferred_element_type=jnp.float32)
    stacked = jnp.stack([term_k, term_v])
    return stacked.reshape(2, term_k.shape[0], term_k.shape[1] * term_k.shape[2])


def task_flag(keep_tasks, block, offset_index, count):
    target = block - RADIUS + offset_index
    inside = (block >= 0) & (block < count) & (target >= 0) & (target < count)
    return jnp.where(inside, keep_tasks[jnp.clip(block, 0, count - 1), offset_index], 0)


def per_device(query_rows, key_rows, value_rows, out_rows, grad_out, normalizer, keep_tasks):
    rows, width = query_rows.shape
    scale = (width // HEADS) ** (-0.5)
    count = lax.axis_size("tok")
    place = lax.axis_index("tok")
    delta = block_delta(grad_out, out_rows)
    pairs = jnp.stack([key_rows, value_rows])
    zero_rows = jnp.zeros((rows, width), jnp.float32)
    zero_pair = jnp.zeros((2, rows, width), jnp.float32)
    grad_query = zero_rows
    grad_pair = zero_pair

    def whole(keys_in):
        parts = scores_grads(query_rows, grad_out, normalizer, delta, keys_in[0], keys_in[1], scale)
        return (grad_of_query(parts, scale), grads_of_keys(parts, scale))

    def nothing(unused):
        return (zero_rows, zero_pair)

    for j in range(WIN):
        offset = j - RADIUS
        if offset == 0:
            keys_here = pairs
        else:
            keys_here = shifted(pairs, "tok", -offset)
        own_flag = task_flag(keep_tasks, place, j, count)
        term_q, term_k = lax.cond(own_flag > 0, whole, nothing, keys_here)
        grad_query = grad_query + term_q
        if offset == 0:
            grad_pair = grad_pair + term_k
        else:
            grad_pair = grad_pair + shifted(term_k, "tok", offset)
    return (
        grad_query.astype(jnp.bfloat16),
        grad_pair[0].astype(jnp.bfloat16),
        grad_pair[1].astype(jnp.bfloat16),
    )


def solution(mesh):
    return jax.shard_map(
        per_device,
        mesh=mesh,
        in_specs=(
            P(("groups", "tok"), None),
            P(("groups", "tok"), None),
            P(("groups", "tok"), None),
            P(("groups", "tok"), None),
            P(("groups", "tok"), None),
            P(None, ("groups", "tok")),
            P("groups", None),
        ),
        out_specs=(
            P(("groups", "tok"), None),
            P(("groups", "tok"), None),
            P(("groups", "tok"), None),
        ),
        check_vma=False,
    )
```

profile of v0, /device:TPU:17, one launch (start us, length us, event | category | flops | bytes accessed | tf_op | source)
XLA Modules:
  0.0 204.6 jit_solution(5160384420963412973)
XLA Ops:
  4.0 3.1 %collective-permute-start.3 = (bf16[2,256,768]{1,2,0:T(8,128)(2,1)}, bf16[2,256,768]{1,2,0:T(8,128)(2,1)S(1)}, u32[]{:S(2)}, u32[]{:S(2)}) collective-permute-start(bf16[2,256,768]{1,2,0:T(8,128)(2,1)} %pad_maximum_fusion.5), channel_id=1, source_target_pairs={{2,0},{3,1},{4,2},{5,3},{6,4},{7,5},{8,6},{9,7},{10,8},{11,9},{12,... | collective-permute-start | bytes 2359304 | tf_op jit(solution)/shard_map/ppermute | solution.py:14
  7.2 2.9 %collective-permute-start.2 = (bf16[2,256,768]{1,2,0:T(8,128)(2,1)}, bf16[2,256,768]{1,2,0:T(8,128)(2,1)}, u32[]{:S(2)}, u32[]{:S(2)}) collective-permute-start(bf16[2,256,768]{1,2,0:T(8,128)(2,1)} %pad_maximum_fusion.5), channel_id=1, source_target_pairs={{1,0},{2,1},{3,2},{4,3},{5,4},{6,5},{7,6},{8,7},{9,8},{10,9},{11,1... | collective-permute-start | bytes 2359304 | tf_op jit(solution)/shard_map/ppermute | solution.py:14
  10.0 2.7 %collective-permute-start.1 = (bf16[2,256,768]{1,2,0:T(8,128)(2,1)}, bf16[2,256,768]{1,2,0:T(8,128)(2,1)}, u32[]{:S(2)}, u32[]{:S(2)}) collective-permute-start(bf16[2,256,768]{1,2,0:T(8,128)(2,1)} %pad_maximum_fusion.5), channel_id=1, source_target_pairs={{0,1},{1,2},{2,3},{3,4},{4,5},{5,6},{6,7},{7,8},{8,9},{9,10},{10,1... | collective-permute-start | bytes 2359304 | tf_op jit(solution)/shard_map/ppermute | solution.py:14
  12.8 3.5 %collective-permute-start = (bf16[2,256,768]{1,2,0:T(8,128)(2,1)}, bf16[2,256,768]{1,2,0:T(8,128)(2,1)}, u32[]{:S(2)}, u32[]{:S(2)}) collective-permute-start(bf16[2,256,768]{1,2,0:T(8,128)(2,1)} %pad_maximum_fusion.5), channel_id=1, source_target_pairs={{0,2},{1,3},{2,4},{3,5},{4,6},{5,7},{6,8},{7,9},{8,10},{9,11},{10,... | collective-permute-start | bytes 2359304 | tf_op jit(solution)/shard_map/ppermute | solution.py:14
  20.0 29.9 %collective-permute-done.3 = bf16[2,256,768]{1,2,0:T(8,128)(2,1)S(1)} collective-permute-done((bf16[2,256,768]{1,2,0:T(8,128)(2,1)}, bf16[2,256,768]{1,2,0:T(8,128)(2,1)S(1)}, u32[]{:S(2)}, u32[]{:S(2)}) %collective-permute-start.3) | collective-permute-done | bytes 786464 | tf_op jit(solution)/shard_map/ppermute | solution.py:14
  50.0 8.7 %conditional.9 = (f32[2,256,768]{1,2,0:T(8,128)S(1)}, f32[256,768]{1,0:T(8,128)}) conditional(s32[]{:T(128)} %convert_element_type.70, () %tuple.56, (bf16[256,768]{1,0:T(8,128)(2,1)S(1)}, bf16[2,256,768]{1,2,0:T(8,128)(2,1)S(1)}, f32[16,256]{1,0:T(8,128)S(1)}, bf16[256,768]{1,0:T(8,128)(2,1)S(1)}, f32[16,256]{1,0:T(8,128)S(1)}) %tuple.116), branch_computations={%region_9.10_spmd, %region_10.11_spmd} | conditional | flops 512491520 | bytes 31899664 | solution.py:91
  53.0 2.0 multiply_convert_fusion.4
  60.3 9.8 %conditional.8 = (f32[2,256,768]{1,2,0:T(8,128)S(1)}, f32[256,768]{1,0:T(8,128)}) conditional(s32[]{:T(128)} %convert_element_type.69, () %tuple.54, (bf16[256,768]{1,0:T(8,128)(2,1)S(1)}, bf16[2,256,768]{1,2,0:T(8,128)(2,1)}, f32[16,256]{1,0:T(8,128)S(1)}, bf16[256,768]{1,0:T(8,128)(2,1)S(1)}, f32[16,256]{1,0:T(8,128)S(1)}) %tuple.117), branch_computations={%region_7.8_spmd, %region_8.9_spmd} | conditional | flops 512491520 | bytes 31899664 | solution.py:91
  64.5 2.0 multiply_convert_fusion.3
  71.7 9.8 %conditional.6 = (f32[2,256,768]{1,2,0:T(8,128)S(1)}, f32[256,768]{1,0:T(8,128)}) conditional(s32[]{:T(128)} %convert_element_type.67, () %tuple.50, (bf16[256,768]{1,0:T(8,128)(2,1)S(1)}, bf16[2,256,768]{1,2,0:T(8,128)(2,1)}, f32[16,256]{1,0:T(8,128)S(1)}, bf16[256,768]{1,0:T(8,128)(2,1)S(1)}, f32[16,256]{1,0:T(8,128)S(1)}) %tuple.118), branch_computations={%region_3.4_spmd, %region_4.5_spmd} | conditional | flops 512491520 | bytes 31899664 | solution.py:91
  74.0 1.9 fusion.7
  75.9 2.0 multiply_convert_fusion.1
  83.2 9.8 %conditional.5 = (f32[2,256,768]{1,2,0:T(8,128)S(1)}, f32[256,768]{1,0:T(8,128)}) conditional(s32[]{:T(128)} %convert_element_type.64, () %tuple.48, (bf16[256,768]{1,0:T(8,128)(2,1)S(1)}, bf16[2,256,768]{1,2,0:T(8,128)(2,1)}, f32[16,256]{1,0:T(8,128)S(1)}, bf16[256,768]{1,0:T(8,128)(2,1)S(1)}, f32[16,256]{1,0:T(8,128)S(1)}) %tuple.119), branch_computations={%region_1.2_spmd, %region_2.3_spmd} | conditional | flops 512491520 | bytes 31899664 | solution.py:91
  87.4 2.0 multiply_convert_fusion
  94.7 1.9 collective-permute-start.4
  96.6 3.5 %collective-permute-start.5 = (f32[2,256,768]{2,1,0:T(8,128)}, f32[2,256,768]{2,1,0:T(8,128)}, u32[]{:S(2)}, u32[]{:S(2)}) collective-permute-start(f32[2,256,768]{2,1,0:T(8,128)} %copy.56), channel_id=1, source_target_pairs={{1,0},{2,1},{3,2},{4,3},{5,4},{6,5},{7,6},{8,7},{9,8},{10,9},{11,1... | collective-permute-start | bytes 4718600 | tf_op jit(solution)/shard_map/ppermute | solution.py:14
  100.1 3.5 %collective-permute-start.6 = (f32[2,256,768]{2,1,0:T(8,128)}, f32[2,256,768]{2,1,0:T(8,128)}, u32[]{:S(2)}, u32[]{:S(2)}) collective-permute-start(f32[2,256,768]{2,1,0:T(8,128)} %copy.58), channel_id=1, source_target_pairs={{0,1},{1,2},{2,3},{3,4},{4,5},{5,6},{6,7},{7,8},{8,9},{9,10},{10,1... | collective-permute-start | bytes 4718600 | tf_op jit(solution)/shard_map/ppermute | solution.py:14
  103.6 2.8 %collective-permute-start.7 = (f32[2,256,768]{2,1,0:T(8,128)}, f32[2,256,768]{2,1,0:T(8,128)}, u32[]{:S(2)}, u32[]{:S(2)}) collective-permute-start(f32[2,256,768]{2,1,0:T(8,128)} %copy.59), channel_id=1, source_target_pairs={{0,2},{1,3},{2,4},{3,5},{4,6},{5,7},{6,8},{7,9},{8,10},{9,11},{10,... | collective-permute-start | bytes 4718600 | tf_op jit(solution)/shard_map/ppermute | solution.py:14
  107.1 9.1 %conditional.7 = (f32[256,768]{1,0:T(8,128)}, f32[2,256,768]{2,1,0:T(8,128)S(1)}) conditional(s32[]{:T(128)} %convert_element_type.68, () %tuple.52, (bf16[256,768]{1,0:T(8,128)(2,1)S(1)}, bf16[256,768]{1,0:T(8,128)(2,1)}, f32[16,256]{1,0:T(8,128)S(1)}, bf16[256,768]{1,0:T(8,128)(2,1)S(1)}, bf16[256,768]{1,0:T(8,128)(2,1)S(1)}, ...), branch_computations={%region_5.6_spmd, %region_6.7_spmd} | conditional | flops 512491520 | bytes 35110956 | solution.py:91
  111.2 2.0 multiply_convert_fusion.2
  116.2 3.0 %add_convert_fusion.1 = bf16[256,768]{1,0:T(8,128)(2,1)} fusion(f32[256,768]{1,0:T(8,128)} %get-tuple-element.158, f32[256,768]{1,0:T(8,128)} %get-tuple-element.157, f32[256,768]{1,0:T(8,128)} %get-tuple-element.155, f32[256,768]{1,0:T(8,128)} %get-tuple-element.153, f32[256,768]{1,0:T(8,128)} %get-tuple-element.154), kind=kLoop, calls=%fused_computation.52 | loop fusion | flops 983040 | bytes 4325376 | tf_op jit(solution)/shard_map/convert_element_type | solution.py:98
  119.2 62.6 %collective-permute-done.4 = f32[2,256,768]{2,1,0:T(8,128)} collective-permute-done((f32[2,256,768]{2,1,0:T(8,128)}, f32[2,256,768]{2,1,0:T(8,128)}, u32[]{:S(2)}, u32[]{:S(2)}) %collective-permute-start.4) | collective-permute-done | bytes 1572896 | tf_op jit(solution)/shard_map/ppermute | solution.py:14
  181.8 18.6 %collective-permute-done.5 = f32[2,256,768]{2,1,0:T(8,128)} collective-permute-done((f32[2,256,768]{2,1,0:T(8,128)}, f32[2,256,768]{2,1,0:T(8,128)}, u32[]{:S(2)}, u32[]{:S(2)}) %collective-permute-start.5) | collective-permute-done | bytes 1572896 | tf_op jit(solution)/shard_map/ppermute | solution.py:14
  200.4 3.2 %add_convert_fusion = bf16[2,256,768]{2,1,0:T(8,128)(2,1)S(1)} fusion(f32[2,256,768]{2,1,0:T(8,128)} %collective-permute-done.7, f32[2,256,768]{2,1,0:T(8,128)} %collective-permute-done.6, f32[2,256,768]{2,1,0:T(8,128)S(1)} %get-tuple-element.156, f32[2,256,768]{2,1,0:T(8,128)} %collective-permute-done.4, f32[2,256,768]{2,1,0:T(8,128)} %collective-permute-done.5), kind=kLoop, calls=%fused_computation.50 | loop fusion | flops 1966080 | bytes 8650752 | tf_op jit(solution)/shard_map/convert.1
  (80 shorter events, 47.1 us)
Async XLA Ops:
  0.6 15.6 %copy-start.7 = (s32[16,5]{0,1:T(8,128)S(1)}, s32[16,5]{0,1:T(8,128)}, u32[]{:S(2)}) copy-start(s32[16,5]{0,1:T(8,128)} %param.23) | copy-start | bytes 964
  0.6 18.8 %copy-start.6 = (bf16[256,768]{1,0:T(8,128)(2,1)S(1)}, bf16[256,768]{1,0:T(8,128)(2,1)}, u32[]{:S(2)}) copy-start(bf16[256,768]{1,0:T(8,128)(2,1)} %param.20) | copy-start | bytes 1179652
  0.7 19.0 %copy-start = (bf16[256,768]{1,0:T(8,128)(2,1)S(1)}, bf16[256,768]{1,0:T(8,128)(2,1)}, u32[]{:S(2)}) copy-start(bf16[256,768]{1,0:T(8,128)(2,1)} %param.21) | copy-start | bytes 1179652
  4.0 45.9 %copy-start.1 = (bf16[256,768]{1,0:T(8,128)(2,1)S(1)}, bf16[256,768]{1,0:T(8,128)(2,1)}, u32[]{:S(2)}) copy-start(bf16[256,768]{1,0:T(8,128)(2,1)} %param.17) | copy-start | bytes 1179652
  4.0 45.9 %copy-start.2 = (f32[16,256]{1,0:T(8,128)S(1)}, f32[16,256]{1,0:T(8,128)}, u32[]{:S(2)}) copy-start(f32[16,256]{1,0:T(8,128)} %param.22) | copy-start | bytes 49156
  4.0 45.9 %collective-permute-start.3 = (bf16[2,256,768]{1,2,0:T(8,128)(2,1)}, bf16[2,256,768]{1,2,0:T(8,128)(2,1)S(1)}, u32[]{:S(2)}, u32[]{:S(2)}) collective-permute-start(bf16[2,256,768]{1,2,0:T(8,128)(2,1)} %pad_maximum_fusion.5), channel_id=1, source_target_pairs={{2,0},{3,1},{4,2},{5,3},{6,4},{7,5},{8,6},{9,7},{10,8},{11,9},{12,... | collective-permute-start | bytes 2359304 | tf_op jit(solution)/shard_map/ppermute | solution.py:14
  7.2 53.1 %collective-permute-start.2 = (bf16[2,256,768]{1,2,0:T(8,128)(2,1)}, bf16[2,256,768]{1,2,0:T(8,128)(2,1)}, u32[]{:S(2)}, u32[]{:S(2)}) collective-permute-start(bf16[2,256,768]{1,2,0:T(8,128)(2,1)} %pad_maximum_fusion.5), channel_id=1, source_target_pairs={{1,0},{2,1},{3,2},{4,3},{5,4},{6,5},{7,6},{8,7},{9,8},{10,9},{11,1... | collective-permute-start | bytes 2359304 | tf_op jit(solution)/shard_map/ppermute | solution.py:14
  10.0 61.7 %collective-permute-start.1 = (bf16[2,256,768]{1,2,0:T(8,128)(2,1)}, bf16[2,256,768]{1,2,0:T(8,128)(2,1)}, u32[]{:S(2)}, u32[]{:S(2)}) collective-permute-start(bf16[2,256,768]{1,2,0:T(8,128)(2,1)} %pad_maximum_fusion.5), channel_id=1, source_target_pairs={{0,1},{1,2},{2,3},{3,4},{4,5},{5,6},{6,7},{7,8},{8,9},{9,10},{10,1... | collective-permute-start | bytes 2359304 | tf_op jit(solution)/shard_map/ppermute | solution.py:14
  12.8 70.4 %collective-permute-start = (bf16[2,256,768]{1,2,0:T(8,128)(2,1)}, bf16[2,256,768]{1,2,0:T(8,128)(2,1)}, u32[]{:S(2)}, u32[]{:S(2)}) collective-permute-start(bf16[2,256,768]{1,2,0:T(8,128)(2,1)} %pad_maximum_fusion.5), channel_id=1, source_target_pairs={{0,2},{1,3},{2,4},{3,5},{4,6},{5,7},{6,8},{7,9},{8,10},{9,11},{10,... | collective-permute-start | bytes 2359304 | tf_op jit(solution)/shard_map/ppermute | solution.py:14
  20.0 63.2 %copy-start.4 = (f32[256,16]{0,1:T(8,128)}, f32[256,16]{0,1:T(8,128)S(1)}, u32[]{:S(2)}) copy-start(f32[256,16]{0,1:T(8,128)S(1)} %reduce_sum.9) | copy-start | bytes 49156
  93.1 14.1 %copy-start.3 = (bf16[256,768]{1,0:T(8,128)(2,1)S(1)}, bf16[256,768]{1,0:T(8,128)(2,1)}, u32[]{:S(2)}) copy-start(bf16[256,768]{1,0:T(8,128)(2,1)} %param.19) | copy-start | bytes 1179652
  94.7 87.1 %collective-permute-start.4 = (f32[2,256,768]{2,1,0:T(8,128)}, f32[2,256,768]{2,1,0:T(8,128)}, u32[]{:S(2)}, u32[]{:S(2)}) collective-permute-start(f32[2,256,768]{2,1,0:T(8,128)} %copy.55), channel_id=1, source_target_pairs={{2,0},{3,1},{4,2},{5,3},{6,4},{7,5},{8,6},{9,7},{10,8},{11,9},{12,... | collective-permute-start | bytes 4718600 | tf_op jit(solution)/shard_map/ppermute | solution.py:14
  96.6 103.8 %collective-permute-start.5 = (f32[2,256,768]{2,1,0:T(8,128)}, f32[2,256,768]{2,1,0:T(8,128)}, u32[]{:S(2)}, u32[]{:S(2)}) collective-permute-start(f32[2,256,768]{2,1,0:T(8,128)} %copy.56), channel_id=1, source_target_pairs={{1,0},{2,1},{3,2},{4,3},{5,4},{6,5},{7,6},{8,7},{9,8},{10,9},{11,1... | collective-permute-start | bytes 4718600 | tf_op jit(solution)/shard_map/ppermute | solution.py:14
  100.1 100.4 %collective-permute-start.6 = (f32[2,256,768]{2,1,0:T(8,128)}, f32[2,256,768]{2,1,0:T(8,128)}, u32[]{:S(2)}, u32[]{:S(2)}) collective-permute-start(f32[2,256,768]{2,1,0:T(8,128)} %copy.58), channel_id=1, source_target_pairs={{0,1},{1,2},{2,3},{3,4},{4,5},{5,6},{6,7},{7,8},{8,9},{9,10},{10,1... | collective-permute-start | bytes 4718600 | tf_op jit(solution)/shard_map/ppermute | solution.py:14
  103.6 96.8 %collective-permute-start.7 = (f32[2,256,768]{2,1,0:T(8,128)}, f32[2,256,768]{2,1,0:T(8,128)}, u32[]{:S(2)}, u32[]{:S(2)}) collective-permute-start(f32[2,256,768]{2,1,0:T(8,128)} %copy.59), channel_id=1, source_target_pairs={{0,2},{1,3},{2,4},{3,5},{4,6},{5,7},{6,8},{7,9},{8,10},{9,11},{10,... | collective-permute-start | bytes 4718600 | tf_op jit(solution)/shard_map/ppermute | solution.py:14
  109.6 1.6 copy-start.5
where the time goes:
time: 205 us
  waiting for transfers between devices  111 us (54%)
  matrix products  29 us (14%)
  starting transfers between devices  23.9 us (12%)
  local copies, waits for them, and re-layouts  23.8 us (12%)
  other arithmetic  12.4 us (6%)
  between operations  4.06 us (2%)
    ppermute x8, waiting for transfers between devices, shifted(): lax.ppermute(value, axis, [(source, source + steps) for source in range(f...  111 us
    ppermute x8, starting transfers between devices, shifted(): lax.ppermute(value, axis, [(source, source + steps) for source in range(f...  23.9 us
    cond x10, local copies, waits for them, and re-layouts, per_device(): term_q, term_k = lax.cond(own_flag > 0, whole, nothing, keys_here)  12.9 us
    dot_general x5, matrix products, scores_grads(): jnp.einsum('qhe,khe->hqk', dout_heads, v_heads, preferred_element_type=jn...  9.98 us
    dot_general x5, matrix products, grads_of_keys(): jnp.einsum('hqk,qhe->khe', probs_low, dout_heads, preferred_element_type=...  9.19 us
    another operation x5, other arithmetic, grads_of_keys(): stacked = jnp.stack([term_k, term_v])  5.04 us
  transfers between devices with their start and end apart: 8, of which 3 were waited for; matrix products, arithmetic and copies ran while one was open for 23% of the time, Pallas kernels for 0%

commit v1 on v0

v1 whole, which is shorter than its diff:
```python
import functools
import math

import jax
import jax.numpy as jnp
from jax import lax
from jax.experimental import pallas as pl
from jax.experimental.pallas import tpu as pltpu
from jax.sharding import PartitionSpec as P

HEADS = 16
RADIUS = 2
WIN = 5
PARTS = 3
CHUNK_HEADS = (8, 8)
NN = (((1,), (0,)), ((), ()))
NT = (((1,), (1,)), ((), ()))
TN = (((0,), (0,)), ((), ()))
LOG2E = math.log2(math.e)
F32 = jnp.float32
BF16 = jnp.bfloat16
VMEM = pl.BlockSpec(memory_space=pltpu.VMEM)
SMEM = pl.BlockSpec(memory_space=pltpu.SMEM)


def dot(left, right, dims):
    return lax.dot_general(left, right, dims, preferred_element_type=F32)


def params():
    return pltpu.CompilerParams(vmem_limit_bytes=40 * 1024 * 1024)


def cost(flops, size):
    return pl.CostEstimate(flops=flops, bytes_accessed=size, transcendentals=0)


def split_parts(value):
    out = []
    for _ in range(PARTS):
        piece = value.astype(BF16)
        out.append(piece)
        value = value - piece.astype(F32)
    return out


def extra_rows(heads):
    return -(-2 * PARTS * heads // 16) * 16


def pack_queries(chunks, head_dim, q_ref, do_ref, o_ref, lse_ref, *out_refs):
    q_t = q_ref[...].T
    do_t = do_ref[...].T
    o_t = o_ref[...].T
    lse = lse_ref[...] * LOG2E
    first = 0
    for heads, out_ref in zip(chunks, out_refs):
        rows = heads * head_dim
        span = slice(first * head_dim, first * head_dim + rows)
        out_ref[:rows] = q_t[span]
        out_ref[rows : 2 * rows] = do_t[span]
        product = do_t[span].astype(F32) * o_t[span].astype(F32)
        delta = jnp.concatenate(
            [
                jnp.sum(product[h * head_dim : (h + 1) * head_dim], axis=0, keepdims=True)
                for h in range(heads)
            ],
            axis=0,
        )
        pieces = split_parts(jnp.concatenate([lse[first : first + heads], delta], axis=0))
        pad = extra_rows(heads) - 2 * PARTS * heads
        if pad:
            pieces.append(jnp.zeros((pad, lse.shape[1]), BF16))
        joined = jnp.concatenate([piece.astype(F32) for piece in pieces], axis=0)
        out_ref[2 * rows :] = joined.astype(BF16)
        first += heads


def pack_keys(chunks, head_dim, k_ref, v_ref, *out_refs):
    k_t = k_ref[...].T
    v_t = v_ref[...].T
    first = 0
    for heads, out_ref in zip(chunks, out_refs):
        rows = heads * head_dim
        span = slice(first * head_dim, first * head_dim + rows)
        out_ref[:rows] = k_t[span]
        out_ref[rows:] = v_t[span]
        first += heads


def read_queries(x_ref, heads, head_dim):
    rows = heads * head_dim
    q = [x_ref[h * head_dim : (h + 1) * head_dim] for h in range(heads)]
    do = [x_ref[rows + h * head_dim : rows + (h + 1) * head_dim] for h in range(heads)]
    extra = x_ref[2 * rows :].astype(F32)
    step = 2 * heads
    total = extra[:step]
    for i in range(1, PARTS):
        total = total + extra[i * step : (i + 1) * step]
    lse = [total[h : h + 1] for h in range(heads)]
    delta = [total[heads + h : heads + h + 1] for h in range(heads)]
    return q, do, lse, delta


def read_keys(ref, heads, head_dim):
    rows = heads * head_dim
    k = [ref[h * head_dim : (h + 1) * head_dim] for h in range(heads)]
    v = [ref[rows + h * head_dim : rows + (h + 1) * head_dim] for h in range(heads)]
    return k, v


def task(queries, keys, factor):
    q, do, lse, delta = queries
    k, v = keys
    span = range(len(q))
    scores = [dot(k[i], q[i], TN) for i in span]
    prob_grad = [dot(v[i], do[i], TN) for i in span]
    probs = [jnp.exp2(scores[i] * factor - lse[i]) for i in span]
    score_grad = [(probs[i] * (prob_grad[i] - delta[i])).astype(BF16) for i in span]
    probs = [x.astype(BF16) for x in probs]
    dv = [dot(do[i], probs[i], NT) for i in span]
    dk = [dot(q[i], score_grad[i], NT) for i in span]
    dq = [dot(k[i], score_grad[i], NN) for i in span]
    return dq, dk, dv


def join(parts):
    return jnp.concatenate(parts, axis=0)


def flag_of(keep_ref, count, query, key):
    offset = key - query + RADIUS
    inside = (key >= 0) & (key < count) & (offset >= 0) & (offset < WIN)
    value = keep_ref[query, jnp.clip(offset, 0, WIN - 1)]
    return inside & (value > 0)


def own_kernel(heads, head_dim, factor, count, keep_ref, place_ref, x_ref, kv_ref, pkv_ref,
               dq_ref, dkv_ref, pdkv_ref):
    place = place_ref[0]
    partner = place + 1 - 2 * lax.rem(place, 2)
    queries = read_queries(x_ref, heads, head_dim)
    dq, dk, dv = task(queries, read_keys(kv_ref, heads, head_dim), factor)
    dq_ref[...] = join(dq)
    dkv_ref[...] = join(dk + dv)
    flag = flag_of(keep_ref, count, place, partner)

    @pl.when(flag)
    def _():
        dq, dk, dv = task(queries, read_keys(pkv_ref, heads, head_dim), factor)
        dq_ref[...] += join(dq)
        pdkv_ref[...] = join(dk + dv).astype(BF16)

    @pl.when(jnp.logical_not(flag))
    def _():
        pdkv_ref[...] = jnp.zeros_like(pdkv_ref)


def far_kernel(heads, head_dim, factor, count, keep_ref, place_ref, x_ref, kv_ref, pkv_ref,
               fkv_ref, zkv_ref, dq_ref, dkv_ref, sdkv_ref, zdkv_ref, acc_ref):
    place = place_ref[0]
    spot = lax.rem(place, 4)
    low = spot < 2
    outer = (spot == 0) | (spot == 3)
    partner = place + 1 - 2 * lax.rem(place, 2)
    query = jnp.where(low, place + 2, place - 2)
    jump = jnp.where(low, 4, -4)
    queries = read_queries(x_ref, heads, head_dim)
    acc_ref[...] = jnp.zeros_like(acc_ref)

    def run(flag, load, out_ref):
        @pl.when(flag)
        def _():
            dq, dk, dv = task(queries, load(), factor)
            acc_ref[...] += join(dq)
            out_ref[...] = join(dk + dv).astype(out_ref.dtype)

        @pl.when(jnp.logical_not(flag))
        def _():
            out_ref[...] = jnp.zeros_like(out_ref)

    def side():
        k_p, v_p = read_keys(pkv_ref, heads, head_dim)
        k_f, v_f = read_keys(fkv_ref, heads, head_dim)
        pick = lambda a, b: jnp.where(outer, a, b)
        return [pick(a, b) for a, b in zip(k_p, k_f)], [pick(a, b) for a, b in zip(v_p, v_f)]

    side_key = jnp.where(outer, partner, partner + jump)
    run(flag_of(keep_ref, count, query, place), lambda: read_keys(kv_ref, heads, head_dim), dkv_ref)
    run(flag_of(keep_ref, count, query, side_key), side, sdkv_ref)
    run(
        flag_of(keep_ref, count, query, place + jump),
        lambda: read_keys(zkv_ref, heads, head_dim),
        zdkv_ref,
    )
    dq_ref[...] = acc_ref[...].astype(BF16)


def finish_kernel(chunks, head_dim, scale, *refs):
    ins, outs = refs[:-3], refs[-3:]
    groups = [ins[i * 7 : (i + 1) * 7] for i in range(len(chunks))]
    dq_all, dk_all, dv_all = [], [], []
    for heads, group in zip(chunks, groups):
        dq_own, dq_far, dkv_own, dkv_far, pdkv, sdkv, zdkv = group
        rows = heads * head_dim
        total = dkv_own[...] + dkv_far[...]
        for ref in (pdkv, sdkv, zdkv):
            total = total + ref[...].astype(F32)
        dq_all.append(((dq_own[...] + dq_far[...].astype(F32)) * scale).astype(BF16))
        dk_all.append((total[:rows] * scale).astype(BF16))
        dv_all.append(total[rows:].astype(BF16))
    for parts, ref in zip((dq_all, dk_all, dv_all), outs):
        ref[...] = join(parts).T


def per_device(query_rows, key_rows, value_rows, out_rows, grad_out, normalizer, keep_tasks):
    tokens, width = query_rows.shape
    head_dim = width // HEADS
    scale = head_dim ** (-0.5)
    factor = scale * LOG2E
    count = lax.axis_size("tok")
    chunks = CHUNK_HEADS
    place = jnp.reshape(lax.axis_index("tok"), (1,)).astype(jnp.int32)

    def send(value, pairs):
        pairs = [(a, b) for a, b in pairs if 0 <= b < count]
        return lax.ppermute(value, "tok", pairs)

    everyone = range(count)
    across = [(i, i ^ 2) for i in everyone]
    core = [(i, i ^ 1) for i in everyone]
    level_in = [(i, i - 4 if i % 4 < 2 else i + 4) for i in everyone]
    level_out = [(i, i + 4 if i % 4 < 2 else i - 4) for i in everyone]
    forward = [(i, i ^ 1) for i in everyone if i % 4 in (0, 3)]
    side_out = [(i, {0: i + 1, 1: i + 3, 2: i - 3, 3: i - 1}[i % 4]) for i in everyone]

    def shape(rows, dtype):
        return jax.ShapeDtypeStruct((rows, tokens), dtype)

    x_own = pl.pallas_call(
        functools.partial(pack_queries, chunks, head_dim),
        out_shape=[shape(2 * h * head_dim + extra_rows(h), BF16) for h in chunks],
        in_specs=[VMEM] * 4,
        out_specs=[VMEM] * len(chunks),
        compiler_params=params(),
        name="pack_queries",
    )(query_rows, grad_out, out_rows, normalizer)
    kv_own = pl.pallas_call(
        functools.partial(pack_keys, chunks, head_dim),
        out_shape=[shape(2 * h * head_dim, BF16) for h in chunks],
        in_specs=[VMEM] * 2,
        out_specs=[VMEM] * len(chunks),
        compiler_params=params(),
        name="pack_keys",
    )(key_rows, value_rows)
    x_far = [send(x, across) for x in x_own]
    kv_level = [send(kv, level_in) for kv in kv_own]
    kv_core = [send(kv, core) for kv in kv_own]
    kv_forward = [send(kv, forward) for kv in kv_level]

    finish_args = []
    for c, heads in enumerate(chunks):
        rows = heads * head_dim
        work = 10 * tokens * tokens * 256 * heads
        dq_own, dkv_own, pdkv = pl.pallas_call(
            functools.partial(own_kernel, heads, head_dim, factor, count),
            out_shape=[shape(rows, F32), shape(2 * rows, F32), shape(2 * rows, BF16)],
            in_specs=[SMEM] * 2 + [VMEM] * 3,
            out_specs=[VMEM] * 3,
            compiler_params=params(),
            cost_estimate=cost(2 * work, 8 * rows * tokens * 2),
            name="own_tasks",
        )(keep_tasks, place, x_own[c], kv_own[c], kv_core[c])
        dq_far, dkv_far, sdkv, zdkv = pl.pallas_call(
            functools.partial(far_kernel, heads, head_dim, factor, count),
            out_shape=[shape(rows, BF16), shape(2 * rows, F32), shape(2 * rows, BF16), shape(2 * rows, BF16)],
            in_specs=[SMEM] * 2 + [VMEM] * 5,
            out_specs=[VMEM] * 4,
            scratch_shapes=[pltpu.VMEM((rows, tokens), F32)],
            compiler_params=params(),
            cost_estimate=cost(3 * work, 16 * rows * tokens * 2),
            name="far_tasks",
        )(keep_tasks, place, x_far[c], kv_own[c], kv_core[c], kv_forward[c], kv_level[c])
        finish_args += [
            dq_own,
            send(dq_far, across),
            dkv_own,
            dkv_far,
            send(pdkv, core),
            send(sdkv, side_out),
            send(zdkv, level_out),
        ]
    grad_query, grad_key, grad_value = pl.pallas_call(
        functools.partial(finish_kernel, chunks, head_dim, scale),
        out_shape=[jax.ShapeDtypeStruct((tokens, width), BF16)] * 3,
        in_specs=[VMEM] * len(finish_args),
        out_specs=[VMEM] * 3,
        compiler_params=params(),
        name="finish",
    )(*finish_args)
    return grad_query, grad_key, grad_value


def solution(mesh):
    rows = P(("groups", "tok"), None)
    return jax.shard_map(
        per_device,
        mesh=mesh,
        in_specs=(rows, rows, rows, rows, rows, P(None, ("groups", "tok")), P("groups", None)),
        out_specs=(rows, rows, rows),
        check_vma=False,
    )
```

time: 205 us -> 72.3 us (0.35)
  the two profiles are of different devices: /device:TPU:17 before, /device:TPU:1 now
where the time goes in v1:
time: 72.3 us; the launch traced here: 72.2 us
  starting transfers between devices  33.2 us (46%)
  waiting for transfers between devices  25.3 us (35%)
  Pallas kernels  9.14 us (13%)
  local copies, waits for them, and re-layouts  3.79 us (5%)
  between operations  0.81 us (1%)
    ppermute x16, starting transfers between devices, send(): return lax.ppermute(value, 'tok', pairs)  33.2 us
    ppermute x16, waiting for transfers between devices, send(): return lax.ppermute(value, 'tok', pairs)  25.3 us
    pallas_call x2, Pallas kernels, per_device(): pl.pallas_call(functools.partial(own_kernel, heads, head_dim, factor, cou...  4.77 us
    unnamed x15, local copies, waits for them, and re-layouts  3.79 us
    pallas_call x2, Pallas kernels, per_device(): pl.pallas_call(functools.partial(far_kernel, heads, head_dim, factor, cou...  2.27 us
    pallas_call x1, Pallas kernels, per_device(): pl.pallas_call(functools.partial(finish_kernel, chunks, head_dim, scale),...  1.46 us
  transfers between devices with their start and end apart: 16, of which 6 were waited for; matrix products, arithmetic and copies ran while one was open for 0% of the time, Pallas kernels for 10%

profile of v1, /device:TPU:1, one launch (start us, length us, event | category | flops | bytes accessed | tf_op | source)
XLA Modules:
  0.0 72.2 jit_solution(10563179680353186193)
XLA Ops:
  0.6 1.0 %copy-done = bf16[256,768]{1,0:T(8,128)(2,1)S(1)} copy-done((bf16[256,768]{1,0:T(8,128)(2,1)S(1)}, bf16[256,768]{1,0:T(8,128)(2,1)}, u32[]{:S(2)}) %copy-start) | copy-done | bytes 393240
  1.6 1.0 %copy-done.1 = bf16[256,768]{1,0:T(8,128)(2,1)S(1)} copy-done((bf16[256,768]{1,0:T(8,128)(2,1)S(1)}, bf16[256,768]{1,0:T(8,128)(2,1)}, u32[]{:S(2)}) %copy-start.1) | copy-done | bytes 393240
  2.9 1.3 %collective-permute-start.10 = (bf16[768,256]{1,0:T(8,128)(2,1)S(1)}, bf16[768,256]{1,0:T(8,128)(2,1)S(1)}, u32[]{:S(2)}, u32[]{:S(2)}) collective-permute-start(bf16[768,256]{1,0:T(8,128)(2,1)S(1)} %get-tuple-element.31.kv_ref), channel_id=1, source_target_pairs={{2,6},{3,7},{4,0},{5,1},{6,10},{7,11},{8,4},{9,5},{10,14},{11,15},... | collective-permute-start | bytes 1179656 | tf_op jit(solution)/shard_map/ppermute | solution.py:227
  4.3 1.3 %collective-permute-start.2 = (bf16[768,256]{1,0:T(8,128)(2,1)S(1)}, bf16[768,256]{1,0:T(8,128)(2,1)S(1)}, u32[]{:S(2)}, u32[]{:S(2)}) collective-permute-start(bf16[768,256]{1,0:T(8,128)(2,1)S(1)} %get-tuple-element.22.kv_ref), channel_id=1, source_target_pairs={{2,6},{3,7},{4,0},{5,1},{6,10},{7,11},{8,4},{9,5},{10,14},{11,15},... | collective-permute-start | bytes 1179656 | tf_op jit(solution)/shard_map/ppermute | solution.py:227
  6.1 1.0 %copy-done.4 = bf16[256,768]{1,0:T(8,128)(2,1)S(1)} copy-done((bf16[256,768]{1,0:T(8,128)(2,1)S(1)}, bf16[256,768]{1,0:T(8,128)(2,1)}, u32[]{:S(2)}) %copy-start.4) | copy-done | bytes 393240
  8.3 6.7 %collective-permute-start.1 = (bf16[816,256]{1,0:T(8,128)(2,1)S(1)}, bf16[816,256]{1,0:T(8,128)(2,1)S(1)}, u32[]{:S(2)}, u32[]{:S(2)}) collective-permute-start(bf16[816,256]{1,0:T(8,128)(2,1)S(1)} %get-tuple-element.21.x_ref), channel_id=1, source_target_pairs={{0,2},{1,3},{2,0},{3,1},{4,6},{5,7},{6,4},{7,5},{8,10},{9,11},{10,... | collective-permute-start | bytes 1253384 | tf_op jit(solution)/shard_map/ppermute | solution.py:227
  15.9 1.3 %collective-permute-start.11 = (bf16[768,256]{1,0:T(8,128)(2,1)S(1)}, bf16[768,256]{1,0:T(8,128)(2,1)S(1)}, u32[]{:S(2)}, u32[]{:S(2)}) collective-permute-start(bf16[768,256]{1,0:T(8,128)(2,1)S(1)} %collective-permute-done.10.zkv_ref), channel_id=1, source_target_pairs={{0,1},{3,2},{4,5},{7,6},{8,9},{11,10},{12,13},{15,14},{16,17},{19,... | collective-permute-start | bytes 1179656 | tf_op jit(solution)/shard_map/ppermute | solution.py:227
  17.2 2.6 %own_tasks.3 = (f32[384,256]{1,0:T(8,128)S(1)}, f32[768,256]{1,0:T(8,128)S(1)}, bf16[768,256]{1,0:T(8,128)(2,1)S(1)}) custom-call(s32[16,5]{1,0:T(8,128)S(1)} %copy.10.keep_ref, s32[1]{0:T(128)} %bitcast.place_ref, bf16[816,256]{1,0:T(8,128)(2,1)S(1)} %get-tuple-element.30.x_ref, bf16[768,256]{1,0:T(8,128)(2,1)S(1)} %get-tuple-element.31.kv_ref, ...), custom_call_target="tpu_custom_call" | custom-call | flops 2684354560 | bytes 1572864 | tf_op jit(solution)/shard_map/own_tasks/pallas_call | solution.py:265
  19.8 4.4 %collective-permute-done.2.zkv_ref = bf16[768,256]{1,0:T(8,128)(2,1)S(1)} collective-permute-done((bf16[768,256]{1,0:T(8,128)(2,1)S(1)}, bf16[768,256]{1,0:T(8,128)(2,1)S(1)}, u32[]{:S(2)}, u32[]{:S(2)}) %collective-permute-start.2) | collective-permute-done | bytes 393248 | tf_op jit(solution)/shard_map/ppermute | solution.py:227
  24.2 1.2 %collective-permute-start.13 = (bf16[768,256]{1,0:T(8,128)(2,1)S(1)}, bf16[768,256]{1,0:T(8,128)(2,1)S(1)}, u32[]{:S(2)}, u32[]{:S(2)}) collective-permute-start(bf16[768,256]{1,0:T(8,128)(2,1)S(1)} %get-tuple-element.36), channel_id=1, source_target_pairs={{0,1},{1,0},{2,3},{3,2},{4,5},{5,4},{6,7},{7,6},{8,9},{9,8},{10,11... | collective-permute-start | bytes 1179656 | tf_op jit(solution)/shard_map/ppermute | solution.py:227
  25.4 1.3 %collective-permute-start.3 = (bf16[768,256]{1,0:T(8,128)(2,1)S(1)}, bf16[768,256]{1,0:T(8,128)(2,1)S(1)}, u32[]{:S(2)}, u32[]{:S(2)}) collective-permute-start(bf16[768,256]{1,0:T(8,128)(2,1)S(1)} %collective-permute-done.2.zkv_ref), channel_id=1, source_target_pairs={{0,1},{3,2},{4,5},{7,6},{8,9},{11,10},{12,13},{15,14},{16,17},{19,... | collective-permute-start | bytes 1179656 | tf_op jit(solution)/shard_map/ppermute | solution.py:227
  26.7 2.2 %own_tasks.2 = (f32[384,256]{1,0:T(8,128)S(1)}, f32[768,256]{1,0:T(8,128)S(1)}, bf16[768,256]{1,0:T(8,128)(2,1)S(1)}) custom-call(s32[16,5]{1,0:T(8,128)S(1)} %copy.10.keep_ref, s32[1]{0:T(128)} %bitcast.place_ref, bf16[816,256]{1,0:T(8,128)(2,1)S(1)} %get-tuple-element.21.x_ref, bf16[768,256]{1,0:T(8,128)(2,1)S(1)} %get-tuple-element.22.kv_ref, ...), custom_call_target="tpu_custom_call" | custom-call | flops 2684354560 | bytes 1572864 | tf_op jit(solution)/shard_map/own_tasks/pallas_call | solution.py:265
  28.9 4.9 %collective-permute-done.9.x_ref = bf16[816,256]{1,0:T(8,128)(2,1)S(1)} collective-permute-done((bf16[816,256]{1,0:T(8,128)(2,1)S(1)}, bf16[816,256]{1,0:T(8,128)(2,1)S(1)}, u32[]{:S(2)}, u32[]{:S(2)}) %collective-permute-start.9) | collective-permute-done | bytes 417824 | tf_op jit(solution)/shard_map/ppermute | solution.py:227
  34.5 1.2 %far_tasks.3 = (bf16[384,256]{1,0:T(8,128)(2,1)S(1)}, f32[768,256]{1,0:T(8,128)S(1)}, bf16[768,256]{1,0:T(8,128)(2,1)S(1)}, bf16[768,256]{1,0:T(8,128)(2,1)S(1)}) custom-call(s32[16,5]{1,0:T(8,128)S(1)} %copy.10.keep_ref, s32[1]{0:T(128)} %bitcast.place_ref, bf16[816,256]{1,0:T(8,128)(2,1)S(1)} %collective-permute-done.9.x_ref, ...), custom_call_target="tpu_custom_call" | custom-call | flops 4026531840 | bytes 3145728 | tf_op jit(solution)/shard_map/far_tasks/pallas_call | solution.py:274
  35.7 1.5 %collective-permute-start.12 = (bf16[384,256]{1,0:T(8,128)(2,1)S(1)}, bf16[384,256]{1,0:T(8,128)(2,1)S(1)}, u32[]{:S(2)}, u32[]{:S(2)}) collective-permute-start(bf16[384,256]{1,0:T(8,128)(2,1)S(1)} %get-tuple-element.33), channel_id=1, source_target_pairs={{0,2},{1,3},{2,0},{3,1},{4,6},{5,7},{6,4},{7,5},{8,10},{9,11},{10,... | collective-permute-start | bytes 589832 | tf_op jit(solution)/shard_map/ppermute | solution.py:227
  37.3 7.8 %collective-permute-start.14 = (bf16[768,256]{1,0:T(8,128)(2,1)S(1)}, bf16[768,256]{1,0:T(8,128)(2,1)S(1)}, u32[]{:S(2)}, u32[]{:S(2)}) collective-permute-start(bf16[768,256]{1,0:T(8,128)(2,1)S(1)} %get-tuple-element.37), channel_id=1, source_target_pairs={{0,1},{1,4},{3,2},{4,5},{5,8},{6,3},{7,6},{8,9},{9,12},{10,7},{11,... | collective-permute-start | bytes 1179656 | tf_op jit(solution)/shard_map/ppermute | solution.py:227
  45.0 1.3 %collective-permute-start.15 = (bf16[768,256]{1,0:T(8,128)(2,1)S(1)}, bf16[768,256]{1,0:T(8,128)(2,1)S(1)}, u32[]{:S(2)}, u32[]{:S(2)}) collective-permute-start(bf16[768,256]{1,0:T(8,128)(2,1)S(1)} %get-tuple-element.38), channel_id=1, source_target_pairs={{0,4},{1,5},{4,8},{5,9},{6,2},{7,3},{8,12},{9,13},{10,6},{11,7},{1... | collective-permute-start | bytes 1179656 | tf_op jit(solution)/shard_map/ppermute | solution.py:227
  46.4 1.1 %far_tasks.2 = (bf16[384,256]{1,0:T(8,128)(2,1)S(1)}, f32[768,256]{1,0:T(8,128)S(1)}, bf16[768,256]{1,0:T(8,128)(2,1)S(1)}, bf16[768,256]{1,0:T(8,128)(2,1)S(1)}) custom-call(s32[16,5]{1,0:T(8,128)S(1)} %copy.10.keep_ref, s32[1]{0:T(128)} %bitcast.place_ref, bf16[816,256]{1,0:T(8,128)(2,1)S(1)} %collective-permute-done.1.x_ref, ...), custom_call_target="tpu_custom_call" | custom-call | flops 4026531840 | bytes 3145728 | tf_op jit(solution)/shard_map/far_tasks/pallas_call | solution.py:274
  47.4 5.5 %collective-permute-start.6 = (bf16[768,256]{1,0:T(8,128)(2,1)S(1)}, bf16[768,256]{1,0:T(8,128)(2,1)S(1)}, u32[]{:S(2)}, u32[]{:S(2)}) collective-permute-start(bf16[768,256]{1,0:T(8,128)(2,1)S(1)} %get-tuple-element.28), channel_id=1, source_target_pairs={{0,1},{1,4},{3,2},{4,5},{5,8},{6,3},{7,6},{8,9},{9,12},{10,7},{11,... | collective-permute-start | bytes 1179656 | tf_op jit(solution)/shard_map/ppermute | solution.py:227
  52.9 2.5 %collective-permute-start.7 = (bf16[768,256]{1,0:T(8,128)(2,1)S(1)}, bf16[768,256]{1,0:T(8,128)(2,1)S(1)}, u32[]{:S(2)}, u32[]{:S(2)}) collective-permute-start(bf16[768,256]{1,0:T(8,128)(2,1)S(1)} %get-tuple-element.29), channel_id=1, source_target_pairs={{0,4},{1,5},{4,8},{5,9},{6,2},{7,3},{8,12},{9,13},{10,6},{11,7},{1... | collective-permute-start | bytes 1179656 | tf_op jit(solution)/shard_map/ppermute | solution.py:227
  55.6 5.6 %collective-permute-done.4.refs_1_ = bf16[384,256]{1,0:T(8,128)(2,1)S(1)} collective-permute-done((bf16[384,256]{1,0:T(8,128)(2,1)S(1)}, bf16[384,256]{1,0:T(8,128)(2,1)S(1)}, u32[]{:S(2)}, u32[]{:S(2)}) %collective-permute-start.4) | collective-permute-done | bytes 196640 | tf_op jit(solution)/shard_map/ppermute | solution.py:227
  61.2 5.4 %collective-permute-done.6.refs_5_ = bf16[768,256]{1,0:T(8,128)(2,1)S(1)} collective-permute-done((bf16[768,256]{1,0:T(8,128)(2,1)S(1)}, bf16[768,256]{1,0:T(8,128)(2,1)S(1)}, u32[]{:S(2)}, u32[]{:S(2)}) %collective-permute-start.6) | collective-permute-done | bytes 393248 | tf_op jit(solution)/shard_map/ppermute | solution.py:227
  66.6 4.2 %collective-permute-done.7.refs_6_ = bf16[768,256]{1,0:T(8,128)(2,1)S(1)} collective-permute-done((bf16[768,256]{1,0:T(8,128)(2,1)S(1)}, bf16[768,256]{1,0:T(8,128)(2,1)S(1)}, u32[]{:S(2)}, u32[]{:S(2)}) %collective-permute-start.7) | collective-permute-done | bytes 393248 | tf_op jit(solution)/shard_map/ppermute | solution.py:227
  70.8 1.5 %finish.1 = (bf16[256,768]{1,0:T(8,128)(2,1)}, bf16[256,768]{1,0:T(8,128)(2,1)}, bf16[256,768]{1,0:T(8,128)(2,1)}) custom-call(f32[384,256]{1,0:T(8,128)S(1)} %get-tuple-element.23.refs_0_, bf16[384,256]{1,0:T(8,128)(2,1)S(1)} %collective-permute-done.4.refs_1_, f32[768,256]{1,0:T(8,128)S(1)} %get-tuple-element.25.refs_2_, ...), custom_call_target="tpu_custom_call" | custom-call | tf_op jit(solution)/shard_map/finish/pallas_call | solution.py:293
  (30 shorter events, 3.8 us)
Async XLA Ops:
  0.6 1.0 %copy-start = (bf16[256,768]{1,0:T(8,128)(2,1)S(1)}, bf16[256,768]{1,0:T(8,128)(2,1)}, u32[]{:S(2)}) copy-start(bf16[256,768]{1,0:T(8,128)(2,1)} %k_ref.1) | copy-start | bytes 1179652
  1.6 1.0 %copy-start.1 = (bf16[256,768]{1,0:T(8,128)(2,1)S(1)}, bf16[256,768]{1,0:T(8,128)(2,1)}, u32[]{:S(2)}) copy-start(bf16[256,768]{1,0:T(8,128)(2,1)} %v_ref.1) | copy-start | bytes 1179652
  2.6 3.5 %copy-start.2 = (bf16[256,768]{1,0:T(8,128)(2,1)S(1)}, bf16[256,768]{1,0:T(8,128)(2,1)}, u32[]{:S(2)}) copy-start(bf16[256,768]{1,0:T(8,128)(2,1)} %q_ref.1) | copy-start | bytes 1179652
  2.6 3.5 %copy-start.3 = (bf16[256,768]{1,0:T(8,128)(2,1)S(1)}, bf16[256,768]{1,0:T(8,128)(2,1)}, u32[]{:S(2)}) copy-start(bf16[256,768]{1,0:T(8,128)(2,1)} %do_ref.1) | copy-start | bytes 1179652
  2.9 12.9 %collective-permute-start.10 = (bf16[768,256]{1,0:T(8,128)(2,1)S(1)}, bf16[768,256]{1,0:T(8,128)(2,1)S(1)}, u32[]{:S(2)}, u32[]{:S(2)}) collective-permute-start(bf16[768,256]{1,0:T(8,128)(2,1)S(1)} %get-tuple-element.31.kv_ref), channel_id=1, source_target_pairs={{2,6},{3,7},{4,0},{5,1},{6,10},{7,11},{8,4},{9,5},{10,14},{11,15},... | collective-permute-start | bytes 1179656 | tf_op jit(solution)/shard_map/ppermute | solution.py:227
  4.2 11.7 %collective-permute-start.8 = (bf16[768,256]{1,0:T(8,128)(2,1)S(1)}, bf16[768,256]{1,0:T(8,128)(2,1)}, u32[]{:S(2)}, u32[]{:S(2)}) collective-permute-start(bf16[768,256]{1,0:T(8,128)(2,1)S(1)} %get-tuple-element.31.kv_ref), channel_id=1, source_target_pairs={{0,1},{1,0},{2,3},{3,2},{4,5},{5,4},{6,7},{7,6},{8,9},{9,8},{10,11... | collective-permute-start | bytes 1179656 | tf_op jit(solution)/shard_map/ppermute | solution.py:227
  4.3 19.9 %collective-permute-start.2 = (bf16[768,256]{1,0:T(8,128)(2,1)S(1)}, bf16[768,256]{1,0:T(8,128)(2,1)S(1)}, u32[]{:S(2)}, u32[]{:S(2)}) collective-permute-start(bf16[768,256]{1,0:T(8,128)(2,1)S(1)} %get-tuple-element.22.kv_ref), channel_id=1, source_target_pairs={{2,6},{3,7},{4,0},{5,1},{6,10},{7,11},{8,4},{9,5},{10,14},{11,15},... | collective-permute-start | bytes 1179656 | tf_op jit(solution)/shard_map/ppermute | solution.py:227
  5.6 19.8 %collective-permute-start = (bf16[768,256]{1,0:T(8,128)(2,1)S(1)}, bf16[768,256]{1,0:T(8,128)(2,1)S(1)}, u32[]{:S(2)}, u32[]{:S(2)}) collective-permute-start(bf16[768,256]{1,0:T(8,128)(2,1)S(1)} %get-tuple-element.22.kv_ref), channel_id=1, source_target_pairs={{0,1},{1,0},{2,3},{3,2},{4,5},{5,4},{6,7},{7,6},{8,9},{9,8},{10,11... | collective-permute-start | bytes 1179656 | tf_op jit(solution)/shard_map/ppermute | solution.py:227
  6.1 1.0 %copy-start.4 = (bf16[256,768]{1,0:T(8,128)(2,1)S(1)}, bf16[256,768]{1,0:T(8,128)(2,1)}, u32[]{:S(2)}) copy-start(bf16[256,768]{1,0:T(8,128)(2,1)} %o_ref.1) | copy-start | bytes 1179652
  7.1 0.7 copy-start.5
  8.2 6.7 %copy-start.6 = (s32[16,5]{0,1:T(8,128)S(1)}, s32[16,5]{0,1:T(8,128)}, u32[]{:S(2)}) copy-start(s32[16,5]{0,1:T(8,128)} %param.13) | copy-start | bytes 964
  8.3 29.0 %collective-permute-start.1 = (bf16[816,256]{1,0:T(8,128)(2,1)S(1)}, bf16[816,256]{1,0:T(8,128)(2,1)S(1)}, u32[]{:S(2)}, u32[]{:S(2)}) collective-permute-start(bf16[816,256]{1,0:T(8,128)(2,1)S(1)} %get-tuple-element.21.x_ref), channel_id=1, source_target_pairs={{0,2},{1,3},{2,0},{3,1},{4,6},{5,7},{6,4},{7,5},{8,10},{9,11},{10,... | collective-permute-start | bytes 1253384 | tf_op jit(solution)/shard_map/ppermute | solution.py:227
  15.8 18.1 %collective-permute-start.9 = (bf16[816,256]{1,0:T(8,128)(2,1)S(1)}, bf16[816,256]{1,0:T(8,128)(2,1)S(1)}, u32[]{:S(2)}, u32[]{:S(2)}) collective-permute-start(bf16[816,256]{1,0:T(8,128)(2,1)S(1)} %get-tuple-element.30.x_ref), channel_id=1, source_target_pairs={{0,2},{1,3},{2,0},{3,1},{4,6},{5,7},{6,4},{7,5},{8,10},{9,11},{10,... | collective-permute-start | bytes 1253384 | tf_op jit(solution)/shard_map/ppermute | solution.py:227
  15.9 18.6 %collective-permute-start.11 = (bf16[768,256]{1,0:T(8,128)(2,1)S(1)}, bf16[768,256]{1,0:T(8,128)(2,1)S(1)}, u32[]{:S(2)}, u32[]{:S(2)}) collective-permute-start(bf16[768,256]{1,0:T(8,128)(2,1)S(1)} %collective-permute-done.10.zkv_ref), channel_id=1, source_target_pairs={{0,1},{3,2},{4,5},{7,6},{8,9},{11,10},{12,13},{15,14},{16,17},{19,... | collective-permute-start | bytes 1179656 | tf_op jit(solution)/shard_map/ppermute | solution.py:227
  24.2 23.2 %collective-permute-start.13 = (bf16[768,256]{1,0:T(8,128)(2,1)S(1)}, bf16[768,256]{1,0:T(8,128)(2,1)S(1)}, u32[]{:S(2)}, u32[]{:S(2)}) collective-permute-start(bf16[768,256]{1,0:T(8,128)(2,1)S(1)} %get-tuple-element.36), channel_id=1, source_target_pairs={{0,1},{1,0},{2,3},{3,2},{4,5},{5,4},{6,7},{7,6},{8,9},{9,8},{10,11... | collective-permute-start | bytes 1179656 | tf_op jit(solution)/shard_map/ppermute | solution.py:227
  25.4 19.6 %collective-permute-start.3 = (bf16[768,256]{1,0:T(8,128)(2,1)S(1)}, bf16[768,256]{1,0:T(8,128)(2,1)S(1)}, u32[]{:S(2)}, u32[]{:S(2)}) collective-permute-start(bf16[768,256]{1,0:T(8,128)(2,1)S(1)} %collective-permute-done.2.zkv_ref), channel_id=1, source_target_pairs={{0,1},{3,2},{4,5},{7,6},{8,9},{11,10},{12,13},{15,14},{16,17},{19,... | collective-permute-start | bytes 1179656 | tf_op jit(solution)/shard_map/ppermute | solution.py:227
  33.8 19.1 %collective-permute-start.5 = (bf16[768,256]{1,0:T(8,128)(2,1)S(1)}, bf16[768,256]{1,0:T(8,128)(2,1)S(1)}, u32[]{:S(2)}, u32[]{:S(2)}) collective-permute-start(bf16[768,256]{1,0:T(8,128)(2,1)S(1)} %get-tuple-element.27), channel_id=1, source_target_pairs={{0,1},{1,0},{2,3},{3,2},{4,5},{5,4},{6,7},{7,6},{8,9},{9,8},{10,11... | collective-permute-start | bytes 1179656 | tf_op jit(solution)/shard_map/ppermute | solution.py:227
  35.7 19.7 %collective-permute-start.12 = (bf16[384,256]{1,0:T(8,128)(2,1)S(1)}, bf16[384,256]{1,0:T(8,128)(2,1)S(1)}, u32[]{:S(2)}, u32[]{:S(2)}) collective-permute-start(bf16[384,256]{1,0:T(8,128)(2,1)S(1)} %get-tuple-element.33), channel_id=1, source_target_pairs={{0,2},{1,3},{2,0},{3,1},{4,6},{5,7},{6,4},{7,5},{8,10},{9,11},{10,... | collective-permute-start | bytes 589832 | tf_op jit(solution)/shard_map/ppermute | solution.py:227
  37.3 23.9 %collective-permute-start.14 = (bf16[768,256]{1,0:T(8,128)(2,1)S(1)}, bf16[768,256]{1,0:T(8,128)(2,1)S(1)}, u32[]{:S(2)}, u32[]{:S(2)}) collective-permute-start(bf16[768,256]{1,0:T(8,128)(2,1)S(1)} %get-tuple-element.37), channel_id=1, source_target_pairs={{0,1},{1,4},{3,2},{4,5},{5,8},{6,3},{7,6},{8,9},{9,12},{10,7},{11,... | collective-permute-start | bytes 1179656 | tf_op jit(solution)/shard_map/ppermute | solution.py:227
  45.0 16.2 %collective-permute-start.15 = (bf16[768,256]{1,0:T(8,128)(2,1)S(1)}, bf16[768,256]{1,0:T(8,128)(2,1)S(1)}, u32[]{:S(2)}, u32[]{:S(2)}) collective-permute-start(bf16[768,256]{1,0:T(8,128)(2,1)S(1)} %get-tuple-element.38), channel_id=1, source_target_pairs={{0,4},{1,5},{4,8},{5,9},{6,2},{7,3},{8,12},{9,13},{10,6},{11,7},{1... | collective-permute-start | bytes 1179656 | tf_op jit(solution)/shard_map/ppermute | solution.py:227
  47.4 19.1 %collective-permute-start.6 = (bf16[768,256]{1,0:T(8,128)(2,1)S(1)}, bf16[768,256]{1,0:T(8,128)(2,1)S(1)}, u32[]{:S(2)}, u32[]{:S(2)}) collective-permute-start(bf16[768,256]{1,0:T(8,128)(2,1)S(1)} %get-tuple-element.28), channel_id=1, source_target_pairs={{0,1},{1,4},{3,2},{4,5},{5,8},{6,3},{7,6},{8,9},{9,12},{10,7},{11,... | collective-permute-start | bytes 1179656 | tf_op jit(solution)/shard_map/ppermute | solution.py:227
  52.9 17.9 %collective-permute-start.7 = (bf16[768,256]{1,0:T(8,128)(2,1)S(1)}, bf16[768,256]{1,0:T(8,128)(2,1)S(1)}, u32[]{:S(2)}, u32[]{:S(2)}) collective-permute-start(bf16[768,256]{1,0:T(8,128)(2,1)S(1)} %get-tuple-element.29), channel_id=1, source_target_pairs={{0,4},{1,5},{4,8},{5,9},{6,2},{7,3},{8,12},{9,13},{10,6},{11,7},{1... | collective-permute-start | bytes 1179656 | tf_op jit(solution)/shard_map/ppermute | solution.py:227
  55.5 5.7 %collective-permute-start.4 = (bf16[384,256]{1,0:T(8,128)(2,1)S(1)}, bf16[384,256]{1,0:T(8,128)(2,1)S(1)}, u32[]{:S(2)}, u32[]{:S(2)}) collective-permute-start(bf16[384,256]{1,0:T(8,128)(2,1)S(1)} %get-tuple-element.24), channel_id=1, source_target_pairs={{0,2},{1,3},{2,0},{3,1},{4,6},{5,7},{6,4},{7,5},{8,10},{9,11},{10,... | collective-permute-start | bytes 589832 | tf_op jit(solution)/shard_map/ppermute | solution.py:227

commit v2 on v1

v2 whole, which is shorter than its diff:
```python
import functools
import math

import jax
import jax.numpy as jnp
from jax import lax
from jax.experimental import pallas as pl
from jax.experimental.pallas import tpu as pltpu
from jax.sharding import PartitionSpec as P

HEADS = 16
RADIUS = 2
WIN = 5
PARTS = 3
CHUNK_HEADS = (8, 8)
NN = (((1,), (0,)), ((), ()))
NT = (((1,), (1,)), ((), ()))
TN = (((0,), (0,)), ((), ()))
LOG2E = math.log2(math.e)
F32 = jnp.float32
BF16 = jnp.bfloat16
VMEM = pl.BlockSpec(memory_space=pltpu.VMEM)
SMEM = pl.BlockSpec(memory_space=pltpu.SMEM)


def dot(left, right, dims):
    return lax.dot_general(left, right, dims, preferred_element_type=F32)


def join(parts):
    return jnp.concatenate(parts, axis=0)


def params():
    return pltpu.CompilerParams(vmem_limit_bytes=40 * 1024 * 1024)


def cost(flops, size):
    return pl.CostEstimate(flops=flops, bytes_accessed=size, transcendentals=0)


def split_parts(value):
    out = []
    for _ in range(PARTS):
        piece = value.astype(BF16)
        out.append(piece)
        value = value - piece.astype(F32)
    return out


def extra_rows(heads):
    return -(-2 * PARTS * heads // 16) * 16


def pack_kernel(chunks, head_dim, q_hbm, do_hbm, o_hbm, lse_hbm, k_hbm, v_hbm, *rest):
    count = len(chunks)
    x_refs, kv_refs = rest[:count], rest[count : 2 * count]
    q_ref, do_ref, o_ref, lse_ref, k_ref, v_ref, sems = rest[2 * count :]
    sources = (q_hbm, do_hbm, o_hbm, lse_hbm, k_hbm, v_hbm)
    targets = (q_ref, do_ref, o_ref, lse_ref, k_ref, v_ref)
    copies = [
        pltpu.make_async_copy(source, target, sems.at[i])
        for i, (source, target) in enumerate(zip(sources, targets))
    ]
    for copy in copies:
        copy.start()
    for copy in copies[:4]:
        copy.wait()
    lse = lse_ref[...] * LOG2E
    first = 0
    for heads, out_ref in zip(chunks, x_refs):
        rows = heads * head_dim
        span = slice(first * head_dim, first * head_dim + rows)
        do_t = do_ref[:, span].T
        out_ref[:rows] = q_ref[:, span].T
        out_ref[rows : 2 * rows] = do_t
        product = do_t.astype(F32) * o_ref[:, span].T.astype(F32)
        delta = [
            jnp.sum(product[h * head_dim : (h + 1) * head_dim], axis=0, keepdims=True)
            for h in range(heads)
        ]
        pieces = split_parts(join([lse[first : first + heads]] + delta))
        pad = extra_rows(heads) - 2 * PARTS * heads
        if pad:
            pieces.append(jnp.zeros((pad, lse.shape[1]), BF16))
        out_ref[2 * rows :] = join([piece.astype(F32) for piece in pieces]).astype(BF16)
        first += heads
    for copy in copies[4:]:
        copy.wait()
    first = 0
    for heads, out_ref in zip(chunks, kv_refs):
        rows = heads * head_dim
        span = slice(first * head_dim, first * head_dim + rows)
        out_ref[:rows] = k_ref[:, span].T
        out_ref[rows:] = v_ref[:, span].T
        first += heads


def read_queries(x_ref, heads, head_dim):
    rows = heads * head_dim
    q = [x_ref[h * head_dim : (h + 1) * head_dim] for h in range(heads)]
    do = [x_ref[rows + h * head_dim : rows + (h + 1) * head_dim] for h in range(heads)]
    extra = x_ref[2 * rows :].astype(F32)
    step = 2 * heads
    total = extra[:step]
    for i in range(1, PARTS):
        total = total + extra[i * step : (i + 1) * step]
    lse = [total[h : h + 1] for h in range(heads)]
    delta = [total[heads + h : heads + h + 1] for h in range(heads)]
    return q, do, lse, delta


def read_keys(ref, heads, head_dim):
    rows = heads * head_dim
    k = [ref[h * head_dim : (h + 1) * head_dim] for h in range(heads)]
    v = [ref[rows + h * head_dim : rows + (h + 1) * head_dim] for h in range(heads)]
    return k, v


def task(queries, keys, factor):
    q, do, lse, delta = queries
    k, v = keys
    span = range(len(q))
    scores = [dot(k[i], q[i], TN) for i in span]
    prob_grad = [dot(v[i], do[i], TN) for i in span]
    probs = [jnp.exp2(scores[i] * factor - lse[i]) for i in span]
    score_grad = [(probs[i] * (prob_grad[i] - delta[i])).astype(BF16) for i in span]
    probs = [x.astype(BF16) for x in probs]
    dv = [dot(do[i], probs[i], NT) for i in span]
    dk = [dot(q[i], score_grad[i], NT) for i in span]
    dq = [dot(k[i], score_grad[i], NN) for i in span]
    return dq, dk, dv


def flag_of(keep_ref, count, query, key):
    offset = key - query + RADIUS
    inside = (key >= 0) & (key < count) & (offset >= 0) & (offset < WIN)
    value = keep_ref[query, jnp.clip(offset, 0, WIN - 1)]
    return inside & (value > 0)


def partner_of(place):
    return place + 1 - 2 * lax.rem(place, 2)


def own_kernel(heads, head_dim, factor, count, keep_ref, place_ref, x_ref, cx_ref, kv_ref,
               dq_ref, cdq_ref, dkv_ref):
    place = place_ref[0]
    keys = read_keys(kv_ref, heads, head_dim)
    dq, dk, dv = task(read_queries(x_ref, heads, head_dim), keys, factor)
    dq_ref[...] = join(dq)
    dkv_ref[...] = join(dk + dv)
    flag = flag_of(keep_ref, count, partner_of(place), place)

    @pl.when(flag)
    def _():
        dq, dk, dv = task(
            read_queries(cx_ref, heads, head_dim), read_keys(kv_ref, heads, head_dim), factor
        )
        cdq_ref[...] = join(dq).astype(BF16)
        dkv_ref[...] += join(dk + dv)

    @pl.when(jnp.logical_not(flag))
    def _():
        cdq_ref[...] = jnp.zeros_like(cdq_ref)


def far_kernel(heads, head_dim, factor, count, swapped, first, keep_ref, place_ref, x_ref, kv_ref,
               zkv_ref, *refs):
    if first:
        dq_ref, dkv_ref, zdkv_ref, acc_ref = refs
    else:
        dkv_in, zdkv_in, dq_ref, dkv_ref, zdkv_ref, acc_ref = refs
    place = place_ref[0]
    low = lax.rem(place, 4) < 2
    source = partner_of(place) if swapped else place
    query = jnp.where(low, source + 2, source - 2)
    target = jnp.where(low, place + 4, place - 4)
    flags = [flag_of(keep_ref, count, query, place), flag_of(keep_ref, count, query, target)]
    acc_ref[...] = jnp.zeros_like(acc_ref)
    sides = ((kv_ref, dkv_ref), (zkv_ref, zdkv_ref))
    if not first:
        earlier = (dkv_in, zdkv_in)
    for i, (keys_ref, out_ref) in enumerate(sides):

        @pl.when(flags[i])
        def _(i=i, keys_ref=keys_ref, out_ref=out_ref):
            dq, dk, dv = task(
                read_queries(x_ref, heads, head_dim), read_keys(keys_ref, heads, head_dim), factor
            )
            acc_ref[...] += join(dq)
            total = join(dk + dv)
            if not first:
                total = total + earlier[i][...].astype(F32)
            out_ref[...] = total.astype(out_ref.dtype)

        @pl.when(jnp.logical_not(flags[i]))
        def _(i=i, out_ref=out_ref):
            if first:
                out_ref[...] = jnp.zeros_like(out_ref)
            else:
                out_ref[...] = earlier[i][...].astype(out_ref.dtype)

    dq_ref[...] = acc_ref[...].astype(BF16)


def finish_kernel(chunks, head_dim, scale, *refs):
    ins, outs = refs[:-3], refs[-3:]
    groups = [ins[i * 6 : (i + 1) * 6] for i in range(len(chunks))]
    dq_all, dk_all, dv_all = [], [], []
    for heads, group in zip(chunks, groups):
        dq_own, dq_core, dq_far, dkv_own, dkv_far, zdkv = group
        rows = heads * head_dim
        dq = dq_own[...] + dq_core[...].astype(F32) + dq_far[...].astype(F32)
        total = dkv_own[...] + dkv_far[...] + zdkv[...].astype(F32)
        dq_all.append((dq * scale).astype(BF16))
        dk_all.append((total[:rows] * scale).astype(BF16))
        dv_all.append(total[rows:].astype(BF16))
    for parts, ref in zip((dq_all, dk_all, dv_all), outs):
        ref[...] = join(parts).T


def per_device(query_rows, key_rows, value_rows, out_rows, grad_out, normalizer, keep_tasks):
    tokens, width = query_rows.shape
    head_dim = width // HEADS
    scale = head_dim ** (-0.5)
    factor = scale * LOG2E
    count = lax.axis_size("tok")
    chunks = CHUNK_HEADS
    place = jnp.reshape(lax.axis_index("tok"), (1,)).astype(jnp.int32)

    def send(value, pairs):
        pairs = [(a, b) for a, b in pairs if 0 <= b < count]
        return lax.ppermute(value, "tok", pairs)

    everyone = range(count)
    across = [(i, i ^ 2) for i in everyone]
    core = [(i, i ^ 1) for i in everyone]
    level_in = [(i, i - 4 if i % 4 < 2 else i + 4) for i in everyone]
    level_out = [(i, i + 4 if i % 4 < 2 else i - 4) for i in everyone]

    def shape(rows, dtype):
        return jax.ShapeDtypeStruct((rows, tokens), dtype)

    x_rows = [2 * h * head_dim + extra_rows(h) for h in chunks]
    packed = pl.pallas_call(
        functools.partial(pack_kernel, chunks, head_dim),
        out_shape=[shape(n, BF16) for n in x_rows] + [shape(2 * h * head_dim, BF16) for h in chunks],
        in_specs=[pl.BlockSpec(memory_space=pltpu.HBM)] * 6,
        out_specs=[VMEM] * (2 * len(chunks)),
        scratch_shapes=[pltpu.VMEM((tokens, width), BF16)] * 3
        + [pltpu.VMEM((HEADS, tokens), F32)]
        + [pltpu.VMEM((tokens, width), BF16)] * 2
        + [pltpu.SemaphoreType.DMA((6,))],
        compiler_params=params(),
        name="pack",
    )(query_rows, grad_out, out_rows, normalizer, key_rows, value_rows)
    x_own, kv_own = packed[: len(chunks)], packed[len(chunks) :]
    x_far = [send(x, across) for x in x_own]
    kv_level = [send(kv, level_in) for kv in kv_own]
    x_core = [send(x, core) for x in x_own]
    x_far_core = [send(x, core) for x in x_far]

    finish_args = []
    for c, heads in enumerate(chunks):
        rows = heads * head_dim
        work = 10 * tokens * tokens * 256 * heads

        def far(swapped, first, x, *earlier):
            return pl.pallas_call(
                functools.partial(far_kernel, heads, head_dim, factor, count, swapped, first),
                out_shape=[shape(rows, BF16), shape(2 * rows, F32), shape(2 * rows, F32 if first else BF16)],
                in_specs=[SMEM] * 2 + [VMEM] * (3 + len(earlier)),
                out_specs=[VMEM] * 3,
                scratch_shapes=[pltpu.VMEM((rows, tokens), F32)],
                compiler_params=params(),
                cost_estimate=cost(2 * work, 16 * rows * tokens * 2),
                name="far_tasks",
            )(keep_tasks, place, x, kv_own[c], kv_level[c], *earlier)

        dq_own, dq_core, dkv_own = pl.pallas_call(
            functools.partial(own_kernel, heads, head_dim, factor, count),
            out_shape=[shape(rows, F32), shape(rows, BF16), shape(2 * rows, F32)],
            in_specs=[SMEM] * 2 + [VMEM] * 3,
            out_specs=[VMEM] * 3,
            compiler_params=params(),
            cost_estimate=cost(2 * work, 8 * rows * tokens * 2),
            name="own_tasks",
        )(keep_tasks, place, x_own[c], x_core[c], kv_own[c])
        dq_a, dkv_a, zdkv_a = far(False, True, x_far[c])
        dq_b, dkv_far, zdkv = far(True, False, x_far_core[c], dkv_a, zdkv_a)
        dq_far = (dq_a.astype(F32) + send(dq_b, core).astype(F32)).astype(BF16)
        finish_args += [
            dq_own,
            send(dq_core, core),
            send(dq_far, across),
            dkv_own,
            dkv_far,
            send(zdkv, level_out),
        ]
    grad_query, grad_key, grad_value = pl.pallas_call(
        functools.partial(finish_kernel, chunks, head_dim, scale),
        out_shape=[jax.ShapeDtypeStruct((tokens, width), BF16)] * 3,
        in_specs=[VMEM] * len(finish_args),
        out_specs=[VMEM] * 3,
        compiler_params=params(),
        name="finish",
    )(*finish_args)
    return grad_query, grad_key, grad_value


def solution(mesh):
    rows = P(("groups", "tok"), None)
    return jax.shard_map(
        per_device,
        mesh=mesh,
        in_specs=(rows, rows, rows, rows, rows, P(None, ("groups", "tok")), P("groups", None)),
        out_specs=(rows, rows, rows),
        check_vma=False,
    )
```

time: 72.3 us -> 63.9 us (0.88)
  the two profiles are of different devices: /device:TPU:1 before, /device:TPU:0 now
where the time goes in v2:
time: 63.9 us; the launch traced here: 63.6 us
  Pallas kernels  20.4 us (32%)
  waiting for transfers between devices  18.3 us (29%)
  starting transfers between devices  18.2 us (28%)
  local copies, waits for them, and re-layouts  5.78 us (9%)
  between operations  0.86 us (1%)
    ppermute x16, waiting for transfers between devices, send(): return lax.ppermute(value, 'tok', pairs)  18.3 us
    ppermute x16, starting transfers between devices, send(): return lax.ppermute(value, 'tok', pairs)  18.2 us
    pallas_call x4, Pallas kernels, far(): pl.pallas_call(functools.partial(far_kernel, heads, head_dim, factor, cou...  10 us
    pallas_call x2, Pallas kernels, per_device(): pl.pallas_call(functools.partial(own_kernel, heads, head_dim, factor, cou...  7.45 us
    unnamed x15, local copies, waits for them, and re-layouts  5.78 us
    pallas_call x1, Pallas kernels, per_device(): pl.pallas_call(functools.partial(pack_kernel, chunks, head_dim), out_shap...  1.66 us
  transfers between devices with their start and end apart: 16, of which 5 were waited for; matrix products, arithmetic and copies ran while one was open for 0% of the time, Pallas kernels for 27%

profile of v2, /device:TPU:0, one launch (start us, length us, event | category | flops | bytes accessed | tf_op | source)
XLA Modules:
  0.0 63.6 jit_solution(8008759216954961847)
XLA Ops:
  0.6 1.0 %copy-done = bf16[256,768]{1,0:T(8,128)(2,1)S(1)} copy-done((bf16[256,768]{1,0:T(8,128)(2,1)S(1)}, bf16[256,768]{1,0:T(8,128)(2,1)}, u32[]{:S(2)}) %copy-start) | copy-done | bytes 393240
  1.6 1.0 %copy-done.1 = bf16[256,768]{1,0:T(8,128)(2,1)S(1)} copy-done((bf16[256,768]{1,0:T(8,128)(2,1)S(1)}, bf16[256,768]{1,0:T(8,128)(2,1)}, u32[]{:S(2)}) %copy-start.1) | copy-done | bytes 393240
  2.6 1.0 %copy-done.2 = bf16[256,768]{1,0:T(8,128)(2,1)S(1)} copy-done((bf16[256,768]{1,0:T(8,128)(2,1)S(1)}, bf16[256,768]{1,0:T(8,128)(2,1)}, u32[]{:S(2)}) %copy-start.2) | copy-done | bytes 393240
  3.6 1.0 %copy-done.3 = bf16[256,768]{1,0:T(8,128)(2,1)S(1)} copy-done((bf16[256,768]{1,0:T(8,128)(2,1)S(1)}, bf16[256,768]{1,0:T(8,128)(2,1)}, u32[]{:S(2)}) %copy-start.3) | copy-done | bytes 393240
  4.6 1.0 %copy-done.4 = bf16[256,768]{1,0:T(8,128)(2,1)S(1)} copy-done((bf16[256,768]{1,0:T(8,128)(2,1)S(1)}, bf16[256,768]{1,0:T(8,128)(2,1)}, u32[]{:S(2)}) %copy-start.4) | copy-done | bytes 393240
  6.3 1.7 %pack.1 = (bf16[816,256]{1,0:T(8,128)(2,1)S(1)}, bf16[816,256]{1,0:T(8,128)(2,1)S(1)}, bf16[768,256]{1,0:T(8,128)(2,1)S(1)}, bf16[768,256]{1,0:T(8,128)(2,1)S(1)}) custom-call(bf16[256,768]{1,0:T(8,128)(2,1)S(1)} %copy-done, bf16[256,768]{1,0:T(8,128)(2,1)S(1)} %copy-done.1, bf16[256,768]{1,0:T(8,128)(2,1)S(1)} %copy-done.2, f32[16,256]{1,0:T(8,128)S(1)} %copy-done.5, ...), custom_call_target="tpu_custom_call" | custom-call | tf_op jit(solution)/shard_map/pack/pallas_call | solution.py:246
  8.6 2.9 %collective-permute-start.10 = (bf16[816,256]{1,0:T(8,128)(2,1)S(1)}, bf16[816,256]{1,0:T(8,128)(2,1)S(1)}, u32[]{:S(2)}, u32[]{:S(2)}) collective-permute-start(bf16[816,256]{1,0:T(8,128)(2,1)S(1)} %get-tuple-element.36.x_ref), channel_id=1, source_target_pairs={{0,2},{1,3},{2,0},{3,1},{4,6},{5,7},{6,4},{7,5},{8,10},{9,11},{10,... | collective-permute-start | bytes 1253384 | tf_op jit(solution)/shard_map/ppermute | solution.py:234
  11.6 1.3 %collective-permute-start.11 = (bf16[768,256]{1,0:T(8,128)(2,1)S(1)}, bf16[768,256]{1,0:T(8,128)(2,1)}, u32[]{:S(2)}, u32[]{:S(2)}) collective-permute-start(bf16[768,256]{1,0:T(8,128)(2,1)S(1)} %get-tuple-element.37.kv_ref), channel_id=1, source_target_pairs={{2,6},{3,7},{4,0},{5,1},{6,10},{7,11},{8,4},{9,5},{10,14},{11,15},... | collective-permute-start | bytes 1179656 | tf_op jit(solution)/shard_map/ppermute | solution.py:234
  12.9 1.3 %collective-permute-start.3 = (bf16[768,256]{1,0:T(8,128)(2,1)S(1)}, bf16[768,256]{1,0:T(8,128)(2,1)S(1)}, u32[]{:S(2)}, u32[]{:S(2)}) collective-permute-start(bf16[768,256]{1,0:T(8,128)(2,1)S(1)} %get-tuple-element.26.kv_ref), channel_id=1, source_target_pairs={{2,6},{3,7},{4,0},{5,1},{6,10},{7,11},{8,4},{9,5},{10,14},{11,15},... | collective-permute-start | bytes 1179656 | tf_op jit(solution)/shard_map/ppermute | solution.py:234
  14.2 3.7 %own_tasks.3 = (f32[384,256]{1,0:T(8,128)S(1)}, bf16[384,256]{1,0:T(8,128)(2,1)S(1)}, f32[768,256]{1,0:T(8,128)S(1)}) custom-call(s32[16,5]{1,0:T(8,128)S(1)} %copy.10.keep_ref, s32[1]{0:T(128)} %bitcast.place_ref, bf16[816,256]{1,0:T(8,128)(2,1)S(1)} %get-tuple-element.36.x_ref, bf16[816,256]{1,0:T(8,128)(2,1)S(1)} %collective-permute-done.8.cx_ref, ...), custom_call_target="tpu_custom_call" | custom-call | flops 2684354560 | bytes 1572864 | tf_op jit(solution)/shard_map/own_tasks/pallas_call | solution.py:281
  18.0 3.7 %own_tasks.2 = (f32[384,256]{1,0:T(8,128)S(1)}, bf16[384,256]{1,0:T(8,128)(2,1)S(1)}, f32[768,256]{1,0:T(8,128)S(1)}) custom-call(s32[16,5]{1,0:T(8,128)S(1)} %copy.10.keep_ref, s32[1]{0:T(128)} %bitcast.place_ref, bf16[816,256]{1,0:T(8,128)(2,1)S(1)} %get-tuple-element.25.x_ref, bf16[816,256]{1,0:T(8,128)(2,1)S(1)} %collective-permute-done.cx_ref, ...), custom_call_target="tpu_custom_call" | custom-call | flops 2684354560 | bytes 1572864 | tf_op jit(solution)/shard_map/own_tasks/pallas_call | solution.py:281
  21.8 3.8 %collective-permute-done.11.zkv_ref = bf16[768,256]{1,0:T(8,128)(2,1)} collective-permute-done((bf16[768,256]{1,0:T(8,128)(2,1)S(1)}, bf16[768,256]{1,0:T(8,128)(2,1)}, u32[]{:S(2)}, u32[]{:S(2)}) %collective-permute-start.11) | collective-permute-done | bytes 393248 | tf_op jit(solution)/shard_map/ppermute | solution.py:234
  26.1 4.2 %collective-permute-done.2.x_ref = bf16[816,256]{1,0:T(8,128)(2,1)S(1)} collective-permute-done((bf16[816,256]{1,0:T(8,128)(2,1)S(1)}, bf16[816,256]{1,0:T(8,128)(2,1)S(1)}, u32[]{:S(2)}, u32[]{:S(2)}) %collective-permute-start.2) | collective-permute-done | bytes 417824 | tf_op jit(solution)/shard_map/ppermute | solution.py:234
  30.4 4.1 %far_tasks.6 = (bf16[384,256]{1,0:T(8,128)(2,1)S(1)}, f32[768,256]{1,0:T(8,128)S(1)}, f32[768,256]{1,0:T(8,128)S(1)}) custom-call(s32[16,5]{1,0:T(8,128)S(1)} %copy.10.keep_ref, s32[1]{0:T(128)} %bitcast.place_ref, bf16[816,256]{1,0:T(8,128)(2,1)S(1)} %collective-permute-done.10.x_ref, bf16[768,256]{1,0:T(8,128)(2,1)S(1)} %get-tuple-element.37.kv_ref, ...), custom_call_target="tpu_custom_call" | custom-call | flops 2684354560 | bytes 3145728 | tf_op jit(solution)/shard_map/far_tasks/pallas_call | solution.py:270
  34.5 3.8 %far_tasks.4 = (bf16[384,256]{1,0:T(8,128)(2,1)S(1)}, f32[768,256]{1,0:T(8,128)S(1)}, f32[768,256]{1,0:T(8,128)S(1)}) custom-call(s32[16,5]{1,0:T(8,128)S(1)} %copy.10.keep_ref, s32[1]{0:T(128)} %bitcast.place_ref, bf16[816,256]{1,0:T(8,128)(2,1)S(1)} %collective-permute-done.2.x_ref, bf16[768,256]{1,0:T(8,128)(2,1)S(1)} %get-tuple-element.26.kv_ref, ...), custom_call_target="tpu_custom_call" | custom-call | flops 2684354560 | bytes 3145728 | tf_op jit(solution)/shard_map/far_tasks/pallas_call | solution.py:270
  38.3 1.3 %far_tasks.7 = (bf16[384,256]{1,0:T(8,128)(2,1)S(1)}, f32[768,256]{1,0:T(8,128)S(1)}, bf16[768,256]{1,0:T(8,128)(2,1)S(1)}) custom-call(s32[16,5]{1,0:T(8,128)S(1)} %copy.10.keep_ref, s32[1]{0:T(128)} %bitcast.place_ref, bf16[816,256]{1,0:T(8,128)(2,1)S(1)} %collective-permute-done.12.x_ref, bf16[768,256]{1,0:T(8,128)(2,1)S(1)} %get-tuple-element.37.kv_ref, ...), custom_call_target="tpu_custom_call" | custom-call | flops 2684354560 | bytes 3145728 | tf_op jit(solution)/shard_map/far_tasks/pallas_call | solution.py:270
  39.7 5.7 %collective-permute-start.15 = (bf16[768,256]{1,0:T(8,128)(2,1)S(1)}, bf16[768,256]{1,0:T(8,128)(2,1)S(1)}, u32[]{:S(2)}, u32[]{:S(2)}) collective-permute-start(bf16[768,256]{1,0:T(8,128)(2,1)S(1)} %get-tuple-element.46), channel_id=1, source_target_pairs={{0,4},{1,5},{4,8},{5,9},{6,2},{7,3},{8,12},{9,13},{10,6},{11,7},{1... | collective-permute-start | bytes 1179656 | tf_op jit(solution)/shard_map/ppermute | solution.py:234
  45.4 0.8 %far_tasks.5 = (bf16[384,256]{1,0:T(8,128)(2,1)S(1)}, f32[768,256]{1,0:T(8,128)S(1)}, bf16[768,256]{1,0:T(8,128)(2,1)S(1)}) custom-call(s32[16,5]{1,0:T(8,128)S(1)} %copy.10.keep_ref, s32[1]{0:T(128)} %bitcast.place_ref, bf16[816,256]{1,0:T(8,128)(2,1)S(1)} %collective-permute-done.4.x_ref, bf16[768,256]{1,0:T(8,128)(2,1)S(1)} %get-tuple-element.26.kv_ref, ...), custom_call_target="tpu_custom_call" | custom-call | flops 2684354560 | bytes 3145728 | tf_op jit(solution)/shard_map/far_tasks/pallas_call | solution.py:270
  46.3 3.5 %collective-permute-start.7 = (bf16[768,256]{1,0:T(8,128)(2,1)S(1)}, bf16[768,256]{1,0:T(8,128)(2,1)S(1)}, u32[]{:S(2)}, u32[]{:S(2)}) collective-permute-start(bf16[768,256]{1,0:T(8,128)(2,1)S(1)} %get-tuple-element.35), channel_id=1, source_target_pairs={{0,4},{1,5},{4,8},{5,9},{6,2},{7,3},{8,12},{9,13},{10,6},{11,7},{1... | collective-permute-start | bytes 1179656 | tf_op jit(solution)/shard_map/ppermute | solution.py:234
  50.0 2.1 %collective-permute-start.6 = (bf16[384,256]{1,0:T(8,128)(2,1)S(1)}, bf16[384,256]{1,0:T(8,128)(2,1)S(1)}, u32[]{:S(2)}, u32[]{:S(2)}) collective-permute-start(bf16[384,256]{1,0:T(8,128)(2,1)S(1)} %add_convert_fusion.1), channel_id=1, source_target_pairs={{0,2},{1,3},{2,0},{3,1},{4,6},{5,7},{6,4},{7,5},{8,10},{9,11},{10,... | collective-permute-start | bytes 589832 | tf_op jit(solution)/shard_map/ppermute | solution.py:234
  52.1 5.6 %collective-permute-done.14.refs_8_ = bf16[384,256]{1,0:T(8,128)(2,1)S(1)} collective-permute-done((bf16[384,256]{1,0:T(8,128)(2,1)S(1)}, bf16[384,256]{1,0:T(8,128)(2,1)S(1)}, u32[]{:S(2)}, u32[]{:S(2)}) %collective-permute-start.14) | collective-permute-done | bytes 196640 | tf_op jit(solution)/shard_map/ppermute | solution.py:234
  57.7 3.5 %collective-permute-done.6.refs_2_ = bf16[384,256]{1,0:T(8,128)(2,1)S(1)} collective-permute-done((bf16[384,256]{1,0:T(8,128)(2,1)S(1)}, bf16[384,256]{1,0:T(8,128)(2,1)S(1)}, u32[]{:S(2)}, u32[]{:S(2)}) %collective-permute-start.6) | collective-permute-done | bytes 196640 | tf_op jit(solution)/shard_map/ppermute | solution.py:234
  61.2 1.2 %collective-permute-done.7.refs_5_ = bf16[768,256]{1,0:T(8,128)(2,1)S(1)} collective-permute-done((bf16[768,256]{1,0:T(8,128)(2,1)S(1)}, bf16[768,256]{1,0:T(8,128)(2,1)S(1)}, u32[]{:S(2)}, u32[]{:S(2)}) %collective-permute-start.7) | collective-permute-done | bytes 393248 | tf_op jit(solution)/shard_map/ppermute | solution.py:234
  62.4 1.3 %finish.1 = (bf16[256,768]{1,0:T(8,128)(2,1)}, bf16[256,768]{1,0:T(8,128)(2,1)}, bf16[256,768]{1,0:T(8,128)(2,1)}) custom-call(f32[384,256]{1,0:T(8,128)S(1)} %get-tuple-element.27.refs_0_, bf16[384,256]{1,0:T(8,128)(2,1)S(1)} %collective-permute-done.1.refs_1_, bf16[384,256]{1,0:T(8,128)(2,1)S(1)} %collective-permute-done.6.refs_2_, ...), custom_call_target="tpu_custom_call" | custom-call | tf_op jit(solution)/shard_map/finish/pallas_call | solution.py:301
  (33 shorter events, 2.4 us)
Async XLA Ops:
  0.6 1.0 %copy-start = (bf16[256,768]{1,0:T(8,128)(2,1)S(1)}, bf16[256,768]{1,0:T(8,128)(2,1)}, u32[]{:S(2)}) copy-start(bf16[256,768]{1,0:T(8,128)(2,1)} %q_hbm.1) | copy-start | bytes 1179652
  1.6 1.0 %copy-start.1 = (bf16[256,768]{1,0:T(8,128)(2,1)S(1)}, bf16[256,768]{1,0:T(8,128)(2,1)}, u32[]{:S(2)}) copy-start(bf16[256,768]{1,0:T(8,128)(2,1)} %do_hbm.1) | copy-start | bytes 1179652
  2.6 1.0 %copy-start.2 = (bf16[256,768]{1,0:T(8,128)(2,1)S(1)}, bf16[256,768]{1,0:T(8,128)(2,1)}, u32[]{:S(2)}) copy-start(bf16[256,768]{1,0:T(8,128)(2,1)} %o_hbm.1) | copy-start | bytes 1179652
  3.6 1.0 %copy-start.3 = (bf16[256,768]{1,0:T(8,128)(2,1)S(1)}, bf16[256,768]{1,0:T(8,128)(2,1)}, u32[]{:S(2)}) copy-start(bf16[256,768]{1,0:T(8,128)(2,1)} %k_hbm.1) | copy-start | bytes 1179652
  4.6 1.0 %copy-start.4 = (bf16[256,768]{1,0:T(8,128)(2,1)S(1)}, bf16[256,768]{1,0:T(8,128)(2,1)}, u32[]{:S(2)}) copy-start(bf16[256,768]{1,0:T(8,128)(2,1)} %v_hbm.1) | copy-start | bytes 1179652
  5.6 0.7 %copy-start.5 = (f32[16,256]{1,0:T(8,128)S(1)}, f32[16,256]{1,0:T(8,128)}, u32[]{:S(2)}) copy-start(f32[16,256]{1,0:T(8,128)} %lse_hbm.1) | copy-start | bytes 49156
  8.0 4.9 %copy-start.6 = (s32[16,5]{0,1:T(8,128)S(1)}, s32[16,5]{0,1:T(8,128)}, u32[]{:S(2)}) copy-start(s32[16,5]{0,1:T(8,128)} %param.13) | copy-start | bytes 964
  8.0 4.9 %collective-permute-start.8 = (bf16[816,256]{1,0:T(8,128)(2,1)S(1)}, bf16[816,256]{1,0:T(8,128)(2,1)S(1)}, u32[]{:S(2)}, u32[]{:S(2)}) collective-permute-start(bf16[816,256]{1,0:T(8,128)(2,1)S(1)} %get-tuple-element.36.x_ref), channel_id=1, source_target_pairs={{0,1},{1,0},{2,3},{3,2},{4,5},{5,4},{6,7},{7,6},{8,9},{9,8},{10,11... | collective-permute-start | bytes 1253384 | tf_op jit(solution)/shard_map/ppermute | solution.py:234
  8.5 9.4 %collective-permute-start = (bf16[816,256]{1,0:T(8,128)(2,1)S(1)}, bf16[816,256]{1,0:T(8,128)(2,1)S(1)}, u32[]{:S(2)}, u32[]{:S(2)}) collective-permute-start(bf16[816,256]{1,0:T(8,128)(2,1)S(1)} %get-tuple-element.25.x_ref), channel_id=1, source_target_pairs={{0,1},{1,0},{2,3},{3,2},{4,5},{5,4},{6,7},{7,6},{8,9},{9,8},{10,11... | collective-permute-start | bytes 1253384 | tf_op jit(solution)/shard_map/ppermute | solution.py:234
  8.6 17.0 %collective-permute-start.10 = (bf16[816,256]{1,0:T(8,128)(2,1)S(1)}, bf16[816,256]{1,0:T(8,128)(2,1)S(1)}, u32[]{:S(2)}, u32[]{:S(2)}) collective-permute-start(bf16[816,256]{1,0:T(8,128)(2,1)S(1)} %get-tuple-element.36.x_ref), channel_id=1, source_target_pairs={{0,2},{1,3},{2,0},{3,1},{4,6},{5,7},{6,4},{7,5},{8,10},{9,11},{10,... | collective-permute-start | bytes 1253384 | tf_op jit(solution)/shard_map/ppermute | solution.py:234
  11.5 18.8 %collective-permute-start.2 = (bf16[816,256]{1,0:T(8,128)(2,1)S(1)}, bf16[816,256]{1,0:T(8,128)(2,1)S(1)}, u32[]{:S(2)}, u32[]{:S(2)}) collective-permute-start(bf16[816,256]{1,0:T(8,128)(2,1)S(1)} %get-tuple-element.25.x_ref), channel_id=1, source_target_pairs={{0,2},{1,3},{2,0},{3,1},{4,6},{5,7},{6,4},{7,5},{8,10},{9,11},{10,... | collective-permute-start | bytes 1253384 | tf_op jit(solution)/shard_map/ppermute | solution.py:234
  11.6 14.1 %collective-permute-start.11 = (bf16[768,256]{1,0:T(8,128)(2,1)S(1)}, bf16[768,256]{1,0:T(8,128)(2,1)}, u32[]{:S(2)}, u32[]{:S(2)}) collective-permute-start(bf16[768,256]{1,0:T(8,128)(2,1)S(1)} %get-tuple-element.37.kv_ref), channel_id=1, source_target_pairs={{2,6},{3,7},{4,0},{5,1},{6,10},{7,11},{8,4},{9,5},{10,14},{11,15},... | collective-permute-start | bytes 1179656 | tf_op jit(solution)/shard_map/ppermute | solution.py:234
  12.9 21.5 %collective-permute-start.3 = (bf16[768,256]{1,0:T(8,128)(2,1)S(1)}, bf16[768,256]{1,0:T(8,128)(2,1)S(1)}, u32[]{:S(2)}, u32[]{:S(2)}) collective-permute-start(bf16[768,256]{1,0:T(8,128)(2,1)S(1)} %get-tuple-element.26.kv_ref), channel_id=1, source_target_pairs={{2,6},{3,7},{4,0},{5,1},{6,10},{7,11},{8,4},{9,5},{10,14},{11,15},... | collective-permute-start | bytes 1179656 | tf_op jit(solution)/shard_map/ppermute | solution.py:234
  18.0 32.1 %collective-permute-start.9 = (bf16[384,256]{1,0:T(8,128)(2,1)S(1)}, bf16[384,256]{1,0:T(8,128)(2,1)S(1)}, u32[]{:S(2)}, u32[]{:S(2)}) collective-permute-start(bf16[384,256]{1,0:T(8,128)(2,1)S(1)} %get-tuple-element.39), channel_id=1, source_target_pairs={{0,1},{1,0},{2,3},{3,2},{4,5},{5,4},{6,7},{7,6},{8,9},{9,8},{10,11... | collective-permute-start | bytes 589832 | tf_op jit(solution)/shard_map/ppermute | solution.py:234
  25.6 26.5 %collective-permute-start.1 = (bf16[384,256]{1,0:T(8,128)(2,1)S(1)}, bf16[384,256]{1,0:T(8,128)(2,1)S(1)}, u32[]{:S(2)}, u32[]{:S(2)}) collective-permute-start(bf16[384,256]{1,0:T(8,128)(2,1)S(1)} %get-tuple-element.28), channel_id=1, source_target_pairs={{0,1},{1,0},{2,3},{3,2},{4,5},{5,4},{6,7},{7,6},{8,9},{9,8},{10,11... | collective-permute-start | bytes 589832 | tf_op jit(solution)/shard_map/ppermute | solution.py:234
  25.6 12.6 %collective-permute-start.12 = (bf16[816,256]{1,0:T(8,128)(2,1)S(1)}, bf16[816,256]{1,0:T(8,128)(2,1)S(1)}, u32[]{:S(2)}, u32[]{:S(2)}) collective-permute-start(bf16[816,256]{1,0:T(8,128)(2,1)S(1)} %collective-permute-done.10.x_ref), channel_id=1, source_target_pairs={{0,1},{1,0},{2,3},{3,2},{4,5},{5,4},{6,7},{7,6},{8,9},{9,8},{10,11... | collective-permute-start | bytes 1253384 | tf_op jit(solution)/shard_map/ppermute | solution.py:234
  30.4 15.1 %collective-permute-start.4 = (bf16[816,256]{1,0:T(8,128)(2,1)S(1)}, bf16[816,256]{1,0:T(8,128)(2,1)S(1)}, u32[]{:S(2)}, u32[]{:S(2)}) collective-permute-start(bf16[816,256]{1,0:T(8,128)(2,1)S(1)} %collective-permute-done.2.x_ref), channel_id=1, source_target_pairs={{0,1},{1,0},{2,3},{3,2},{4,5},{5,4},{6,7},{7,6},{8,9},{9,8},{10,11... | collective-permute-start | bytes 1253384 | tf_op jit(solution)/shard_map/ppermute | solution.py:234
  39.6 6.7 %collective-permute-start.13 = (bf16[384,256]{1,0:T(8,128)(2,1)S(1)}, bf16[384,256]{1,0:T(8,128)(2,1)S(1)}, u32[]{:S(2)}, u32[]{:S(2)}) collective-permute-start(bf16[384,256]{1,0:T(8,128)(2,1)S(1)} %get-tuple-element.43), channel_id=1, source_target_pairs={{0,1},{1,0},{2,3},{3,2},{4,5},{5,4},{6,7},{7,6},{8,9},{9,8},{10,11... | collective-permute-start | bytes 589832 | tf_op jit(solution)/shard_map/ppermute | solution.py:234
  39.7 18.0 %collective-permute-start.15 = (bf16[768,256]{1,0:T(8,128)(2,1)S(1)}, bf16[768,256]{1,0:T(8,128)(2,1)S(1)}, u32[]{:S(2)}, u32[]{:S(2)}) collective-permute-start(bf16[768,256]{1,0:T(8,128)(2,1)S(1)} %get-tuple-element.46), channel_id=1, source_target_pairs={{0,4},{1,5},{4,8},{5,9},{6,2},{7,3},{8,12},{9,13},{10,6},{11,7},{1... | collective-permute-start | bytes 1179656 | tf_op jit(solution)/shard_map/ppermute | solution.py:234
  46.2 3.6 %collective-permute-start.5 = (bf16[384,256]{1,0:T(8,128)(2,1)S(1)}, bf16[384,256]{1,0:T(8,128)(2,1)S(1)}, u32[]{:S(2)}, u32[]{:S(2)}) collective-permute-start(bf16[384,256]{1,0:T(8,128)(2,1)S(1)} %get-tuple-element.32), channel_id=1, source_target_pairs={{0,1},{1,0},{2,3},{3,2},{4,5},{5,4},{6,7},{7,6},{8,9},{9,8},{10,11... | collective-permute-start | bytes 589832 | tf_op jit(solution)/shard_map/ppermute | solution.py:234
  46.3 16.0 %collective-permute-start.7 = (bf16[768,256]{1,0:T(8,128)(2,1)S(1)}, bf16[768,256]{1,0:T(8,128)(2,1)S(1)}, u32[]{:S(2)}, u32[]{:S(2)}) collective-permute-start(bf16[768,256]{1,0:T(8,128)(2,1)S(1)} %get-tuple-element.35), channel_id=1, source_target_pairs={{0,4},{1,5},{4,8},{5,9},{6,2},{7,3},{8,12},{9,13},{10,6},{11,7},{1... | collective-permute-start | bytes 1179656 | tf_op jit(solution)/shard_map/ppermute | solution.py:234
  49.9 7.8 %collective-permute-start.14 = (bf16[384,256]{1,0:T(8,128)(2,1)S(1)}, bf16[384,256]{1,0:T(8,128)(2,1)S(1)}, u32[]{:S(2)}, u32[]{:S(2)}) collective-permute-start(bf16[384,256]{1,0:T(8,128)(2,1)S(1)} %add_convert_fusion), channel_id=1, source_target_pairs={{0,2},{1,3},{2,0},{3,1},{4,6},{5,7},{6,4},{7,5},{8,10},{9,11},{10,... | collective-permute-start | bytes 589832 | tf_op jit(solution)/shard_map/ppermute | solution.py:234
  50.0 11.1 %collective-permute-start.6 = (bf16[384,256]{1,0:T(8,128)(2,1)S(1)}, bf16[384,256]{1,0:T(8,128)(2,1)S(1)}, u32[]{:S(2)}, u32[]{:S(2)}) collective-permute-start(bf16[384,256]{1,0:T(8,128)(2,1)S(1)} %add_convert_fusion.1), channel_id=1, source_target_pairs={{0,2},{1,3},{2,0},{3,1},{4,6},{5,7},{6,4},{7,5},{8,10},{9,11},{10,... | collective-permute-start | bytes 589832 | tf_op jit(solution)/shard_map/ppermute | solution.py:234

commit v3 on v2

--- a/solution.py
+++ b/solution.py
@@ -13,6 +13,8 @@
 WIN = 5
 PARTS = 3
 CHUNK_HEADS = (8, 8)
+HOPS = 2
+CORE_COST, FAR_COST, SELF_COST = (0.01, 0.01, 0.01)
 NN = (((1,), (0,)), ((), ()))
 NT = (((1,), (1,)), ((), ()))
 TN = (((0,), (0,)), ((), ()))
@@ -31,8 +33,12 @@
     return jnp.concatenate(parts, axis=0)
 
 
-def params():
-    return pltpu.CompilerParams(vmem_limit_bytes=40 * 1024 * 1024)
+def params(mib=40):
+    return pltpu.CompilerParams(vmem_limit_bytes=mib * 1024 * 1024)
+
+
+def after(value, *tokens):
+    return lax.optimization_barrier((value,) + tokens)[0]
 
 
 def cost(flops, size):
@@ -96,11 +102,12 @@
         first += heads
 
 
-def read_queries(x_ref, heads, head_dim):
-    rows = heads * head_dim
-    q = [x_ref[h * head_dim : (h + 1) * head_dim] for h in range(heads)]
-    do = [x_ref[rows + h * head_dim : rows + (h + 1) * head_dim] for h in range(heads)]
-    extra = x_ref[2 * rows :].astype(F32)
+def read_queries(x_refs, heads, head_dim):
+    blocks = []
+    for ref in x_refs:
+        blocks += [ref[i : i + head_dim] for i in range(0, 2 * heads * head_dim, head_dim) if i < ref.shape[0]]
+    q, do = blocks[:heads], blocks[heads : 2 * heads]
+    extra = x_refs[-1][-extra_rows(heads) :].astype(F32)
     step = 2 * heads
     total = extra[:step]
     for i in range(1, PARTS):
@@ -143,76 +150,71 @@
     return place + 1 - 2 * lax.rem(place, 2)
 
 
-def own_kernel(heads, head_dim, factor, count, keep_ref, place_ref, x_ref, cx_ref, kv_ref,
-               dq_ref, cdq_ref, dkv_ref):
+def near_kernel(chunks, head_dim, factor, count, swapped, keep_ref, place_ref, *refs):
+    size = len(chunks)
+    x_refs, kv_refs = refs[:size], refs[size : 2 * size]
+    outs = refs[2 * size :]
     place = place_ref[0]
-    keys = read_keys(kv_ref, heads, head_dim)
-    dq, dk, dv = task(read_queries(x_ref, heads, head_dim), keys, factor)
-    dq_ref[...] = join(dq)
-    dkv_ref[...] = join(dk + dv)
-    flag = flag_of(keep_ref, count, partner_of(place), place)
-
-    @pl.when(flag)
-    def _():
-        dq, dk, dv = task(
-            read_queries(cx_ref, heads, head_dim), read_keys(kv_ref, heads, head_dim), factor
-        )
-        cdq_ref[...] = join(dq).astype(BF16)
-        dkv_ref[...] += join(dk + dv)
-
-    @pl.when(jnp.logical_not(flag))
-    def _():
-        cdq_ref[...] = jnp.zeros_like(cdq_ref)
-
-
-def far_kernel(heads, head_dim, factor, count, swapped, first, keep_ref, place_ref, x_ref, kv_ref,
-               zkv_ref, *refs):
+    flag = flag_of(keep_ref, count, partner_of(place) if swapped else place, place)
+    for c, heads in enumerate(chunks):
+        dq_ref, dkv_ref = outs[2 * c : 2 * c + 2]
+
+        @pl.when(flag)
+        def _(c=c, heads=heads, dq_ref=dq_ref, dkv_ref=dkv_ref):
+            dq, dk, dv = task(
+                read_queries(x_refs[c : c + 1], heads, head_dim), read_keys(kv_refs[c], heads, head_dim), factor
+            )
+            dq_ref[...] = join(dq).astype(dq_ref.dtype)
+            dkv_ref[...] = join(dk + dv)
+
+        @pl.when(jnp.logical_not(flag))
+        def _(dq_ref=dq_ref, dkv_ref=dkv_ref):
+            dq_ref[...] = jnp.zeros_like(dq_ref)
+            dkv_ref[...] = jnp.zeros_like(dkv_ref)
+
+
+def far_kernel(heads, head_dim, factor, count, level, first, keep_ref, place_ref, x_ref, *refs):
+    c_refs, kv_ref, refs = refs[:HOPS], refs[HOPS], refs[HOPS + 1 :]
     if first:
-        dq_ref, dkv_ref, zdkv_ref, acc_ref = refs
+        earlier, (dq_ref, cdq_ref, dkv_ref, acc_ref) = None, refs
     else:
-        dkv_in, zdkv_in, dq_ref, dkv_ref, zdkv_ref, acc_ref = refs
+        earlier, (dq_ref, cdq_ref, dkv_ref, acc_ref) = refs[:2], refs[2:]
     place = place_ref[0]
-    low = lax.rem(place, 4) < 2
-    source = partner_of(place) if swapped else place
-    query = jnp.where(low, source + 2, source - 2)
-    target = jnp.where(low, place + 4, place - 4)
-    flags = [flag_of(keep_ref, count, query, place), flag_of(keep_ref, count, query, target)]
+    jump = jnp.where(lax.rem(place, 4) < 2, 2, -2)
+    target = place + 2 * jump if level else place
     acc_ref[...] = jnp.zeros_like(acc_ref)
-    sides = ((kv_ref, dkv_ref), (zkv_ref, zdkv_ref))
-    if not first:
-        earlier = (dkv_in, zdkv_in)
-    for i, (keys_ref, out_ref) in enumerate(sides):
-
-        @pl.when(flags[i])
-        def _(i=i, keys_ref=keys_ref, out_ref=out_ref):
+    slots = ((place + jump, (x_ref,), dq_ref), (partner_of(place) + jump, c_refs, cdq_ref))
+    for i, (query, queries_ref, out_ref) in enumerate(slots):
+        flag = flag_of(keep_ref, count, query, target)
+
+        @pl.when(flag)
+        def _(i=i, queries_ref=queries_ref, out_ref=out_ref):
             dq, dk, dv = task(
-                read_queries(x_ref, heads, head_dim), read_keys(keys_ref, heads, head_dim), factor
+                read_queries(queries_ref, heads, head_dim), read_keys(kv_ref, heads, head_dim), factor
             )
-            acc_ref[...] += join(dq)
-            total = join(dk + dv)
-            if not first:
-                total = total + earlier[i][...].astype(F32)
+            total = join(dq) if first else earlier[i][...] + join(dq)
             out_ref[...] = total.astype(out_ref.dtype)
-
-        @pl.when(jnp.logical_not(flags[i]))
+            acc_ref[...] += join(dk + dv)
+
+        @pl.when(jnp.logical_not(flag))
         def _(i=i, out_ref=out_ref):
             if first:
                 out_ref[...] = jnp.zeros_like(out_ref)
             else:
                 out_ref[...] = earlier[i][...].astype(out_ref.dtype)
 
-    dq_ref[...] = acc_ref[...].astype(BF16)
+    dkv_ref[...] = acc_ref[...].astype(dkv_ref.dtype)
 
 
 def finish_kernel(chunks, head_dim, scale, *refs):
     ins, outs = refs[:-3], refs[-3:]
-    groups = [ins[i * 6 : (i + 1) * 6] for i in range(len(chunks))]
+    groups = [ins[i * 7 : (i + 1) * 7] for i in range(len(chunks))]
     dq_all, dk_all, dv_all = [], [], []
     for heads, group in zip(chunks, groups):
-        dq_own, dq_core, dq_far, dkv_own, dkv_far, zdkv = group
+        dq_own, dq_core, dq_far, dkv_own, dkv_core, dkv_far, zdkv = group
         rows = heads * head_dim
         dq = dq_own[...] + dq_core[...].astype(F32) + dq_far[...].astype(F32)
-        total = dkv_own[...] + dkv_far[...] + zdkv[...].astype(F32)
+        total = dkv_own[...] + dkv_core[...] + dkv_far[...] + zdkv[...].astype(F32)
         dq_all.append((dq * scale).astype(BF16))
         dk_all.append((total[:rows] * scale).astype(BF16))
         dv_all.append(total[rows:].astype(BF16))
@@ -230,8 +232,7 @@
     place = jnp.reshape(lax.axis_index("tok"), (1,)).astype(jnp.int32)
 
     def send(value, pairs):
-        pairs = [(a, b) for a, b in pairs if 0 <= b < count]
-        return lax.ppermute(value, "tok", pairs)
+        return lax.ppermute(value, "tok", [(a, b % count) for a, b in pairs])
 
     everyone = range(count)
     across = [(i, i ^ 2) for i in everyone]
@@ -254,49 +255,77 @@
         + [pltpu.SemaphoreType.DMA((6,))],
         compiler_params=params(),
         name="pack",
-    )(query_rows, grad_out, out_rows, normalizer, key_rows, value_rows)
+    )(
+        *[
+            pltpu.with_memory_space_constraint(value, pltpu.HBM)
+            for value in (query_rows, grad_out, out_rows, normalizer, key_rows, value_rows)
+        ]
+    )
     x_own, kv_own = packed[: len(chunks)], packed[len(chunks) :]
     x_far = [send(x, across) for x in x_own]
     kv_level = [send(kv, level_in) for kv in kv_own]
     x_core = [send(x, core) for x in x_own]
-    x_far_core = [send(x, core) for x in x_far]
-
+
+    def work_of(heads):
+        return 10 * tokens * tokens * 256 * heads
+
+    def near(swapped, xs, dq_type, share):
+        out = []
+        for heads in chunks:
+            rows = heads * head_dim
+            out += [shape(rows, dq_type), shape(2 * rows, F32)]
+        got = pl.pallas_call(
+            functools.partial(near_kernel, chunks, head_dim, factor, count, swapped),
+            out_shape=out,
+            in_specs=[SMEM] * 2 + [VMEM] * (2 * len(chunks)),
+            out_specs=[VMEM] * len(out),
+            compiler_params=params(),
+            cost_estimate=cost(int(work_of(HEADS) * share), 1024),
+            name="near_tasks",
+        )(keep_tasks, place, *xs, *kv_own)
+        return got[::2], got[1::2]
+
+    def far(c, level, x, hop, keys, earlier):
+        rows = chunks[c] * head_dim
+        dq_type = BF16 if earlier else F32
+        return pl.pallas_call(
+            functools.partial(far_kernel, chunks[c], head_dim, factor, count, level, not earlier),
+            out_shape=[shape(rows, dq_type)] * 2 + [shape(2 * rows, BF16 if level else F32)],
+            in_specs=[SMEM] * 2 + [VMEM] * (2 + HOPS + len(earlier)),
+            out_specs=[VMEM] * 3,
+            scratch_shapes=[pltpu.VMEM((2 * rows, tokens), F32)],
+            compiler_params=params(),
+            cost_estimate=cost(int(work_of(chunks[c]) * FAR_COST), 1024),
+            name="far_tasks",
+        )(keep_tasks, place, x, *hop, keys, *earlier)
+
+    done = x_core[0]
+    far_out = []
+    for c in range(len(chunks)):
+        x = after(x_far[c], done)
+        cuts = [2 * chunks[c] * i // HOPS * head_dim for i in range(HOPS)] + [x.shape[0]]
+        cuts = [-(-cut // head_dim) * head_dim for cut in cuts]
+        hop = [send(x[i:j], core) for i, j in zip(cuts, cuts[1:])]
+        dq_x, dq_c, dkv_far = far(c, False, x, hop, kv_own[c], ())
+        z = after(kv_level[c], dq_x)
+        dq_x, dq_c, zdkv = far(c, True, x, hop, z, (dq_x, dq_c))
+        done = dq_x
+        dq_far = (dq_x.astype(F32) + send(dq_c, core).astype(F32)).astype(BF16)
+        far_out.append((send(dq_far, across), dkv_far, send(zdkv, level_out)))
+    dq_core, dkv_core = near(True, [after(value, done) for value in x_core], BF16, CORE_COST)
+    done = dq_core[0]
+    dq_own, dkv_own = near(False, [after(x, done, far_out[0][2]) for x in x_own], F32, SELF_COST)
     finish_args = []
-    for c, heads in enumerate(chunks):
-        rows = heads * head_dim
-        work = 10 * tokens * tokens * 256 * heads
-
-        def far(swapped, first, x, *earlier):
-            return pl.pallas_call(
-                functools.partial(far_kernel, heads, head_dim, factor, count, swapped, first),
-                out_shape=[shape(rows, BF16), shape(2 * rows, F32), shape(2 * rows, F32 if first else BF16)],
-                in_specs=[SMEM] * 2 + [VMEM] * (3 + len(earlier)),
-                out_specs=[VMEM] * 3,
-                scratch_shapes=[pltpu.VMEM((rows, tokens), F32)],
-                compiler_params=params(),
-                cost_estimate=cost(2 * work, 16 * rows * tokens * 2),
-                name="far_tasks",
-            )(keep_tasks, place, x, kv_own[c], kv_level[c], *earlier)
-
-        dq_own, dq_core, dkv_own = pl.pallas_call(
-            functools.partial(own_kernel, heads, head_dim, factor, count),
-            out_shape=[shape(rows, F32), shape(rows, BF16), shape(2 * rows, F32)],
-            in_specs=[SMEM] * 2 + [VMEM] * 3,
-            out_specs=[VMEM] * 3,
-            compiler_params=params(),
-            cost_estimate=cost(2 * work, 8 * rows * tokens * 2),
-            name="own_tasks",
-        )(keep_tasks, place, x_own[c], x_core[c], kv_own[c])
-        dq_a, dkv_a, zdkv_a = far(False, True, x_far[c])
-        dq_b, dkv_far, zdkv = far(True, False, x_far_core[c], dkv_a, zdkv_a)
-        dq_far = (dq_a.astype(F32) + send(dq_b, core).astype(F32)).astype(BF16)
+    for c in range(len(chunks)):
+        dq_far, dkv_far, zdkv = far_out[c]
         finish_args += [
-            dq_own,
-            send(dq_core, core),
-            send(dq_far, across),
-            dkv_own,
+            dq_own[c],
+            send(dq_core[c], core),
+            dq_far,
+            dkv_own[c],
+            dkv_core[c],
             dkv_far,
-            send(zdkv, level_out),
+            zdkv,
         ]
     grad_query, grad_key, grad_value = pl.pallas_call(
         functools.partial(finish_kernel, chunks, head_dim, scale),

time: 63.9 us -> 52.5 us (0.82); the launches traced: 63.6 us -> 53 us
  local copies, waits for them, and re-layouts: 5.78 us -> 0.82 us
  waiting for transfers between devices: 18.3 us -> 13.5 us
  starting transfers between devices: 18.2 us -> 14 us
  Pallas kernels: 20.4 us -> 23.6 us
    unnamed x15 -> x3, local copies, waits for them, and re-layouts: 5.78 us -> 0.09 us
    ppermute x16 -> x18, waiting for transfers between devices: 18.3 us -> 13.5 us  [send(): return lax.ppermute(value, 'tok', [(a, b % count) for a, b in pairs])]
    ppermute x16 -> x18, starting transfers between devices: 18.2 us -> 14 us  [send(): return lax.ppermute(value, 'tok', [(a, b % count) for a, b in pairs])]
    pallas_call x6, Pallas kernels: 17.5 us -> 20.2 us  [the longest x4 12.9 us: far(): pl.pallas_call(functools.partial(far_kernel, chunks[c], head_dim, factor,...]
    slice x0 -> x4, local copies, waits for them, and re-layouts: none -> 0.74 us  [per_device(): hop = [send(x[i:j], core) for i, j in zip(cuts, cuts[1:])]]
  transfers between devices with their start and end apart: 16 -> 18, of which waited for: 5 -> 5; matrix products, arithmetic and copies ran while one was open for 0% -> 2% of each run, Pallas kernels for 27% -> 38%
where the time goes in v3:
time: 52.5 us; the launch traced here: 53 us
  Pallas kernels  23.6 us (45%)
  starting transfers between devices  14 us (27%)
  waiting for transfers between devices  13.5 us (26%)
  between operations  0.83 us (2%)
  local copies, waits for them, and re-layouts  0.82 us (2%)
    ppermute x18, starting transfers between devices, send(): return lax.ppermute(value, 'tok', [(a, b % count) for a, b in pairs])  14 us
    ppermute x18, waiting for transfers between devices, send(): return lax.ppermute(value, 'tok', [(a, b % count) for a, b in pairs])  13.5 us
    pallas_call x4, Pallas kernels, far(): pl.pallas_call(functools.partial(far_kernel, chunks[c], head_dim, factor,...  12.9 us
    pallas_call x2, Pallas kernels, near(): pl.pallas_call(functools.partial(near_kernel, chunks, head_dim, factor, c...  7.29 us
    pallas_call x1, Pallas kernels, per_device(): pl.pallas_call(functools.partial(pack_kernel, chunks, head_dim), out_shap...  1.94 us
    pallas_call x1, Pallas kernels, per_device(): pl.pallas_call(functools.partial(finish_kernel, chunks, head_dim, scale),...  1.47 us
  transfers between devices with their start and end apart: 18, of which 5 were waited for; matrix products, arithmetic and copies ran while one was open for 2% of the time, Pallas kernels for 38%

profile of v3, /device:TPU:0, one launch (start us, length us, event | category | flops | bytes accessed | tf_op | source)
XLA Modules:
  0.0 53.0 jit_solution(4843688046089613196)
XLA Ops:
  0.6 1.9 %pack.1 = (bf16[816,256]{1,0:T(8,128)(2,1)S(1)}, bf16[816,256]{1,0:T(8,128)(2,1)S(1)}, bf16[768,256]{1,0:T(8,128)(2,1)S(1)}, bf16[768,256]{1,0:T(8,128)(2,1)S(1)}) custom-call(bf16[256,768]{1,0:T(8,128)(2,1)} %q_hbm.1, bf16[256,768]{1,0:T(8,128)(2,1)} %do_hbm.1, bf16[256,768]{1,0:T(8,128)(2,1)} %o_hbm.1, f32[16,256]{1,0:T(8,128)} %lse_hbm.1, ...), custom_call_target="tpu_custom_call" | custom-call | tf_op jit(solution)/shard_map/pack/pallas_call | solution.py:247
  2.6 3.0 %collective-permute-start.2 = (bf16[816,256]{1,0:T(8,128)(2,1)S(1)}, bf16[816,256]{1,0:T(8,128)(2,1)S(1)}, u32[]{:S(2)}, u32[]{:S(2)}) collective-permute-start(bf16[816,256]{1,0:T(8,128)(2,1)S(1)} %get-tuple-element.53.refs_0_), channel_id=1, source_target_pairs={{0,2},{1,3},{2,0},{3,1},{4,6},{5,7},{6,4},{7,5},{8,10},{9,11},{10,... | collective-permute-start | bytes 1253384 | tf_op jit(solution)/shard_map/ppermute | solution.py:235
  5.6 0.2 collective-permute-start.1
  5.7 4.0 %collective-permute-start.5 = (bf16[768,256]{1,0:T(8,128)(2,1)S(1)}, bf16[768,256]{1,0:T(8,128)(2,1)}, u32[]{:S(2)}, u32[]{:S(2)}) collective-permute-start(bf16[768,256]{1,0:T(8,128)(2,1)S(1)} %get-tuple-element.38.refs_2_), channel_id=1, source_target_pairs={{0,12},{1,13},{2,6},{3,7},{4,0},{5,1},{6,10},{7,11},{8,4},{9,5},{1... | collective-permute-start | bytes 1179656 | tf_op jit(solution)/shard_map/ppermute | solution.py:235
  9.7 6.3 %collective-permute-done.2.x_ref = bf16[816,256]{1,0:T(8,128)(2,1)S(1)} collective-permute-done((bf16[816,256]{1,0:T(8,128)(2,1)S(1)}, bf16[816,256]{1,0:T(8,128)(2,1)S(1)}, u32[]{:S(2)}, u32[]{:S(2)}) %collective-permute-start.2) | collective-permute-done | bytes 417824 | tf_op jit(solution)/shard_map/ppermute | solution.py:235
  16.2 0.7 %slice.12 = bf16[384,256]{1,0:T(8,128)(2,1)} slice(bf16[816,256]{1,0:T(8,128)(2,1)S(1)} %collective-permute-done.2.x_ref), slice={[0:384], [0:256]} | slice | bytes 393216 | tf_op jit(solution)/shard_map/slice | solution.py:308
  16.8 0.5 collective-permute-start.3
  17.3 4.2 %collective-permute-start.8 = (bf16[768,256]{1,0:T(8,128)(2,1)S(1)}, bf16[768,256]{1,0:T(8,128)(2,1)}, u32[]{:S(2)}, u32[]{:S(2)}) collective-permute-start(bf16[768,256]{1,0:T(8,128)(2,1)S(1)} %get-tuple-element.44.refs_2_.refs_3_), channel_id=1, source_target_pairs={{0,12},{1,13},{2,6},{3,7},{4,0},{5,1},{6,10},{7,11},{8,4},{9,5},{1... | collective-permute-start | bytes 1179656 | tf_op jit(solution)/shard_map/ppermute | solution.py:235
  21.5 0.1 copy.15.keep_ref
  21.6 2.3 %far_tasks.4 = (f32[384,256]{1,0:T(8,128)S(1)}, f32[384,256]{1,0:T(8,128)S(1)}, f32[768,256]{1,0:T(8,128)S(1)}) custom-call(s32[16,5]{1,0:T(8,128)S(1)} %copy.15.keep_ref, s32[1]{0:T(128)} %bitcast.place_ref, bf16[816,256]{1,0:T(8,128)(2,1)S(1)} %collective-permute-done.2.x_ref, bf16[384,256]{1,0:T(8,128)(2,1)S(1)} %collective-permute-done.3.refs_0_, ...), custom_call_target="tpu_custom_call" | custom-call | flops 13421772 | bytes 1024 | tf_op jit(solution)/shard_map/far_tasks/pallas_call | solution.py:291
  23.9 4.2 %far_tasks.5 = (bf16[384,256]{1,0:T(8,128)(2,1)S(1)}, bf16[384,256]{1,0:T(8,128)(2,1)S(1)}, bf16[768,256]{1,0:T(8,128)(2,1)S(1)}) custom-call(s32[16,5]{1,0:T(8,128)S(1)} %copy.15.keep_ref, s32[1]{0:T(128)} %bitcast.place_ref, bf16[816,256]{1,0:T(8,128)(2,1)S(1)} %collective-permute-done.2.x_ref, bf16[384,256]{1,0:T(8,128)(2,1)S(1)} %collective-permute-done.3.refs_0_, ...), custom_call_target="tpu_custom_call" | custom-call | flops 13421772 | bytes 1024 | tf_op jit(solution)/shard_map/far_tasks/pallas_call | solution.py:291
  28.2 0.6 %collective-permute-start.6 = (bf16[384,256]{1,0:T(8,128)(2,1)S(1)}, bf16[384,256]{1,0:T(8,128)(2,1)S(1)}, u32[]{:S(2)}, u32[]{:S(2)}) collective-permute-start(bf16[384,256]{1,0:T(8,128)(2,1)S(1)} %slice.14), channel_id=1, source_target_pairs={{0,1},{1,0},{2,3},{3,2},{4,5},{5,4},{6,7},{7,6},{8,9},{9,8},{10,11... | collective-permute-start | bytes 589832 | tf_op jit(solution)/shard_map/ppermute | solution.py:235
  28.9 0.4 collective-permute-start.9
  29.3 0.7 %collective-permute-done.6.refs_0_ = bf16[384,256]{1,0:T(8,128)(2,1)S(1)} collective-permute-done((bf16[384,256]{1,0:T(8,128)(2,1)S(1)}, bf16[384,256]{1,0:T(8,128)(2,1)S(1)}, u32[]{:S(2)}, u32[]{:S(2)}) %collective-permute-start.6) | collective-permute-done | bytes 196640 | tf_op jit(solution)/shard_map/ppermute | solution.py:235
  30.0 2.3 %far_tasks.6 = (f32[384,256]{1,0:T(8,128)S(1)}, f32[384,256]{1,0:T(8,128)S(1)}, f32[768,256]{1,0:T(8,128)S(1)}) custom-call(s32[16,5]{1,0:T(8,128)S(1)} %copy.15.keep_ref, s32[1]{0:T(128)} %bitcast.place_ref, bf16[816,256]{1,0:T(8,128)(2,1)S(1)} %collective-permute-done.1.x_ref, bf16[384,256]{1,0:T(8,128)(2,1)S(1)} %collective-permute-done.6.refs_0_, ...), custom_call_target="tpu_custom_call" | custom-call | flops 13421772 | bytes 1024 | tf_op jit(solution)/shard_map/far_tasks/pallas_call | solution.py:291
  32.3 4.2 %far_tasks.7 = (bf16[384,256]{1,0:T(8,128)(2,1)S(1)}, bf16[384,256]{1,0:T(8,128)(2,1)S(1)}, bf16[768,256]{1,0:T(8,128)(2,1)S(1)}) custom-call(s32[16,5]{1,0:T(8,128)S(1)} %copy.15.keep_ref, s32[1]{0:T(128)} %bitcast.place_ref, bf16[816,256]{1,0:T(8,128)(2,1)S(1)} %collective-permute-done.1.x_ref, bf16[384,256]{1,0:T(8,128)(2,1)S(1)} %collective-permute-done.6.refs_0_, ...), custom_call_target="tpu_custom_call" | custom-call | flops 13421772 | bytes 1024 | tf_op jit(solution)/shard_map/far_tasks/pallas_call | solution.py:291
  36.5 0.3 collective-permute-start.15
  37.0 3.8 %near_tasks.2 = (bf16[384,256]{1,0:T(8,128)(2,1)S(1)}, f32[768,256]{1,0:T(8,128)S(1)}, bf16[384,256]{1,0:T(8,128)(2,1)S(1)}, f32[768,256]{1,0:T(8,128)S(1)}) custom-call(s32[16,5]{1,0:T(8,128)S(1)} %copy.15.keep_ref, s32[1]{0:T(128)} %bitcast.place_ref, bf16[816,256]{1,0:T(8,128)(2,1)S(1)} %collective-permute-done.refs_0_, ...), custom_call_target="tpu_custom_call" | custom-call | flops 26843544 | bytes 1024 | tf_op jit(solution)/shard_map/near_tasks/pallas_call | solution.py:277
  40.8 0.5 collective-permute-start.11
  41.4 2.3 %collective-permute-done.10.refs_6_ = bf16[768,256]{1,0:T(8,128)(2,1)S(1)} collective-permute-done((bf16[768,256]{1,0:T(8,128)(2,1)S(1)}, bf16[768,256]{1,0:T(8,128)(2,1)S(1)}, u32[]{:S(2)}, u32[]{:S(2)}) %collective-permute-start.10) | collective-permute-done | bytes 393248 | tf_op jit(solution)/shard_map/ppermute | solution.py:235
  43.7 3.5 %near_tasks.3 = (f32[384,256]{1,0:T(8,128)S(1)}, f32[768,256]{1,0:T(8,128)S(1)}, f32[384,256]{1,0:T(8,128)S(1)}, f32[768,256]{1,0:T(8,128)S(1)}) custom-call(s32[16,5]{1,0:T(8,128)S(1)} %copy.15.keep_ref, s32[1]{0:T(128)} %bitcast.place_ref, bf16[816,256]{1,0:T(8,128)(2,1)S(1)} %get-tuple-element.53.refs_0_, bf16[816,256]{1,0:T(8,128)(2,1)S(1)} %get-tuple-element.54.refs_1_, ...), custom_call_target="tpu_custom_call" | custom-call | flops 26843544 | bytes 1024 | tf_op jit(solution)/shard_map/near_tasks/pallas_call | solution.py:277
  47.3 2.1 %collective-permute-done.16.refs_9_ = bf16[384,256]{1,0:T(8,128)(2,1)S(1)} collective-permute-done((bf16[384,256]{1,0:T(8,128)(2,1)S(1)}, bf16[384,256]{1,0:T(8,128)(2,1)S(1)}, u32[]{:S(2)}, u32[]{:S(2)}) %collective-permute-start.16) | collective-permute-done | bytes 196640 | tf_op jit(solution)/shard_map/ppermute | solution.py:235
  49.4 2.1 %collective-permute-done.17.refs_13_ = bf16[768,256]{1,0:T(8,128)(2,1)S(1)} collective-permute-done((bf16[768,256]{1,0:T(8,128)(2,1)S(1)}, bf16[768,256]{1,0:T(8,128)(2,1)S(1)}, u32[]{:S(2)}, u32[]{:S(2)}) %collective-permute-start.17) | collective-permute-done | bytes 393248 | tf_op jit(solution)/shard_map/ppermute | solution.py:235
  51.5 1.5 %finish.1 = (bf16[256,768]{1,0:T(8,128)(2,1)}, bf16[256,768]{1,0:T(8,128)(2,1)}, bf16[256,768]{1,0:T(8,128)(2,1)}) custom-call(f32[384,256]{1,0:T(8,128)S(1)} %get-tuple-element.55.refs_0_, bf16[384,256]{1,0:T(8,128)(2,1)S(1)} %collective-permute-done.11.refs_1_, bf16[384,256]{1,0:T(8,128)(2,1)S(1)} %collective-permute-done.13.refs_2_, ...), custom_call_target="tpu_custom_call" | custom-call | tf_op jit(solution)/shard_map/finish/pallas_call | solution.py:330
  (29 shorter events, 0.6 us)
Async XLA Ops:
  2.6 13.5 %collective-permute-start.2 = (bf16[816,256]{1,0:T(8,128)(2,1)S(1)}, bf16[816,256]{1,0:T(8,128)(2,1)S(1)}, u32[]{:S(2)}, u32[]{:S(2)}) collective-permute-start(bf16[816,256]{1,0:T(8,128)(2,1)S(1)} %get-tuple-element.53.refs_0_), channel_id=1, source_target_pairs={{0,2},{1,3},{2,0},{3,1},{4,6},{5,7},{6,4},{7,5},{8,10},{9,11},{10,... | collective-permute-start | bytes 1253384 | tf_op jit(solution)/shard_map/ppermute | solution.py:235
  5.6 10.5 %collective-permute-start = (bf16[816,256]{1,0:T(8,128)(2,1)S(1)}, bf16[816,256]{1,0:T(8,128)(2,1)S(1)}, u32[]{:S(2)}, u32[]{:S(2)}) collective-permute-start(bf16[816,256]{1,0:T(8,128)(2,1)S(1)} %get-tuple-element.53.refs_0_), channel_id=1, source_target_pairs={{0,1},{1,0},{2,3},{3,2},{4,5},{5,4},{6,7},{7,6},{8,9},{9,8},{10,11... | collective-permute-start | bytes 1253384 | tf_op jit(solution)/shard_map/ppermute | solution.py:235
  5.6 22.5 %collective-permute-start.1 = (bf16[816,256]{1,0:T(8,128)(2,1)S(1)}, bf16[816,256]{1,0:T(8,128)(2,1)S(1)}, u32[]{:S(2)}, u32[]{:S(2)}) collective-permute-start(bf16[816,256]{1,0:T(8,128)(2,1)S(1)} %get-tuple-element.54.refs_1_), channel_id=1, source_target_pairs={{0,2},{1,3},{2,0},{3,1},{4,6},{5,7},{6,4},{7,5},{8,10},{9,11},{10,... | collective-permute-start | bytes 1253384 | tf_op jit(solution)/shard_map/ppermute | solution.py:235
  5.7 18.2 %collective-permute-start.5 = (bf16[768,256]{1,0:T(8,128)(2,1)S(1)}, bf16[768,256]{1,0:T(8,128)(2,1)}, u32[]{:S(2)}, u32[]{:S(2)}) collective-permute-start(bf16[768,256]{1,0:T(8,128)(2,1)S(1)} %get-tuple-element.38.refs_2_), channel_id=1, source_target_pairs={{0,12},{1,13},{2,6},{3,7},{4,0},{5,1},{6,10},{7,11},{8,4},{9,5},{1... | collective-permute-start | bytes 1179656 | tf_op jit(solution)/shard_map/ppermute | solution.py:235
  16.1 5.5 %collective-permute-start.4 = (bf16[432,256]{1,0:T(8,128)(2,1)S(1)}, bf16[432,256]{1,0:T(8,128)(2,1)S(1)}, u32[]{:S(2)}, u32[]{:S(2)}) collective-permute-start(bf16[432,256]{1,0:T(8,128)(2,1)S(1)} %slice.13), channel_id=1, source_target_pairs={{0,1},{1,0},{2,3},{3,2},{4,5},{5,4},{6,7},{7,6},{8,9},{9,8},{10,11... | collective-permute-start | bytes 663560 | tf_op jit(solution)/shard_map/ppermute | solution.py:235
  16.8 4.7 %copy-start = (s32[16,5]{0,1:T(8,128)S(1)}, s32[16,5]{0,1:T(8,128)}, u32[]{:S(2)}) copy-start(s32[16,5]{0,1:T(8,128)} %param.13) | copy-start | bytes 964
  16.8 4.8 %collective-permute-start.3 = (bf16[384,256]{1,0:T(8,128)(2,1)}, bf16[384,256]{1,0:T(8,128)(2,1)S(1)}, u32[]{:S(2)}, u32[]{:S(2)}) collective-permute-start(bf16[384,256]{1,0:T(8,128)(2,1)} %slice.12), channel_id=1, source_target_pairs={{0,1},{1,0},{2,3},{3,2},{4,5},{5,4},{6,7},{7,6},{8,9},{9,8},{10,11... | collective-permute-start | bytes 589832 | tf_op jit(solution)/shard_map/ppermute | solution.py:235
  17.3 14.9 %collective-permute-start.8 = (bf16[768,256]{1,0:T(8,128)(2,1)S(1)}, bf16[768,256]{1,0:T(8,128)(2,1)}, u32[]{:S(2)}, u32[]{:S(2)}) collective-permute-start(bf16[768,256]{1,0:T(8,128)(2,1)S(1)} %get-tuple-element.44.refs_2_.refs_3_), channel_id=1, source_target_pairs={{0,12},{1,13},{2,6},{3,7},{4,0},{5,1},{6,10},{7,11},{8,4},{9,5},{1... | collective-permute-start | bytes 1179656 | tf_op jit(solution)/shard_map/ppermute | solution.py:235
  28.1 1.8 %collective-permute-start.7 = (bf16[432,256]{1,0:T(8,128)(2,1)S(1)}, bf16[432,256]{1,0:T(8,128)(2,1)S(1)}, u32[]{:S(2)}, u32[]{:S(2)}) collective-permute-start(bf16[432,256]{1,0:T(8,128)(2,1)S(1)} %slice.15), channel_id=1, source_target_pairs={{0,1},{1,0},{2,3},{3,2},{4,5},{5,4},{6,7},{7,6},{8,9},{9,8},{10,11... | collective-permute-start | bytes 663560 | tf_op jit(solution)/shard_map/ppermute | solution.py:235
  28.2 1.7 %collective-permute-start.6 = (bf16[384,256]{1,0:T(8,128)(2,1)S(1)}, bf16[384,256]{1,0:T(8,128)(2,1)S(1)}, u32[]{:S(2)}, u32[]{:S(2)}) collective-permute-start(bf16[384,256]{1,0:T(8,128)(2,1)S(1)} %slice.14), channel_id=1, source_target_pairs={{0,1},{1,0},{2,3},{3,2},{4,5},{5,4},{6,7},{7,6},{8,9},{9,8},{10,11... | collective-permute-start | bytes 589832 | tf_op jit(solution)/shard_map/ppermute | solution.py:235
  28.8 8.0 %collective-permute-start.12 = (bf16[384,256]{1,0:T(8,128)(2,1)S(1)}, bf16[384,256]{1,0:T(8,128)(2,1)S(1)}, u32[]{:S(2)}, u32[]{:S(2)}) collective-permute-start(bf16[384,256]{1,0:T(8,128)(2,1)S(1)} %get-tuple-element.56), channel_id=1, source_target_pairs={{0,1},{1,0},{2,3},{3,2},{4,5},{5,4},{6,7},{7,6},{8,9},{9,8},{10,11... | collective-permute-start | bytes 589832 | tf_op jit(solution)/shard_map/ppermute | solution.py:235
  28.9 8.0 %collective-permute-start.9 = (bf16[816,256]{1,0:T(8,128)(2,1)S(1)}, bf16[816,256]{1,0:T(8,128)(2,1)S(1)}, u32[]{:S(2)}, u32[]{:S(2)}) collective-permute-start(bf16[816,256]{1,0:T(8,128)(2,1)S(1)} %get-tuple-element.54.refs_1_), channel_id=1, source_target_pairs={{0,1},{1,0},{2,3},{3,2},{4,5},{5,4},{6,7},{7,6},{8,9},{9,8},{10,11... | collective-permute-start | bytes 1253384 | tf_op jit(solution)/shard_map/ppermute | solution.py:235
  30.0 13.7 %collective-permute-start.10 = (bf16[768,256]{1,0:T(8,128)(2,1)S(1)}, bf16[768,256]{1,0:T(8,128)(2,1)S(1)}, u32[]{:S(2)}, u32[]{:S(2)}) collective-permute-start(bf16[768,256]{1,0:T(8,128)(2,1)S(1)} %get-tuple-element.52), channel_id=1, source_target_pairs={{0,4},{1,5},{2,14},{3,15},{4,8},{5,9},{6,2},{7,3},{8,12},{9,13},{1... | collective-permute-start | bytes 1179656 | tf_op jit(solution)/shard_map/ppermute | solution.py:235
  36.5 4.4 %collective-permute-start.15 = (bf16[384,256]{1,0:T(8,128)(2,1)S(1)}, bf16[384,256]{1,0:T(8,128)(2,1)S(1)}, u32[]{:S(2)}, u32[]{:S(2)}) collective-permute-start(bf16[384,256]{1,0:T(8,128)(2,1)S(1)} %get-tuple-element.62), channel_id=1, source_target_pairs={{0,1},{1,0},{2,3},{3,2},{4,5},{5,4},{6,7},{7,6},{8,9},{9,8},{10,11... | collective-permute-start | bytes 589832 | tf_op jit(solution)/shard_map/ppermute | solution.py:235
  36.8 10.4 %collective-permute-start.13 = (bf16[384,256]{1,0:T(8,128)(2,1)S(1)}, bf16[384,256]{1,0:T(8,128)(2,1)S(1)}, u32[]{:S(2)}, u32[]{:S(2)}) collective-permute-start(bf16[384,256]{1,0:T(8,128)(2,1)S(1)} %add_convert_fusion.1), channel_id=1, source_target_pairs={{0,2},{1,3},{2,0},{3,1},{4,6},{5,7},{6,4},{7,5},{8,10},{9,11},{10,... | collective-permute-start | bytes 589832 | tf_op jit(solution)/shard_map/ppermute | solution.py:235
  36.9 14.6 %collective-permute-start.17 = (bf16[768,256]{1,0:T(8,128)(2,1)S(1)}, bf16[768,256]{1,0:T(8,128)(2,1)S(1)}, u32[]{:S(2)}, u32[]{:S(2)}) collective-permute-start(bf16[768,256]{1,0:T(8,128)(2,1)S(1)} %get-tuple-element.66), channel_id=1, source_target_pairs={{0,4},{1,5},{2,14},{3,15},{4,8},{5,9},{6,2},{7,3},{8,12},{9,13},{1... | collective-permute-start | bytes 1179656 | tf_op jit(solution)/shard_map/ppermute | solution.py:235
  40.8 6.5 %collective-permute-start.14 = (bf16[384,256]{1,0:T(8,128)(2,1)S(1)}, bf16[384,256]{1,0:T(8,128)(2,1)S(1)}, u32[]{:S(2)}, u32[]{:S(2)}) collective-permute-start(bf16[384,256]{1,0:T(8,128)(2,1)S(1)} %get-tuple-element.61), channel_id=1, source_target_pairs={{0,1},{1,0},{2,3},{3,2},{4,5},{5,4},{6,7},{7,6},{8,9},{9,8},{10,11... | collective-permute-start | bytes 589832 | tf_op jit(solution)/shard_map/ppermute | solution.py:235
  40.8 6.4 %collective-permute-start.11 = (bf16[384,256]{1,0:T(8,128)(2,1)S(1)}, bf16[384,256]{1,0:T(8,128)(2,1)S(1)}, u32[]{:S(2)}, u32[]{:S(2)}) collective-permute-start(bf16[384,256]{1,0:T(8,128)(2,1)S(1)} %get-tuple-element.51), channel_id=1, source_target_pairs={{0,1},{1,0},{2,3},{3,2},{4,5},{5,4},{6,7},{7,6},{8,9},{9,8},{10,11... | collective-permute-start | bytes 589832 | tf_op jit(solution)/shard_map/ppermute | solution.py:235
  43.7 5.7 %collective-permute-start.16 = (bf16[384,256]{1,0:T(8,128)(2,1)S(1)}, bf16[384,256]{1,0:T(8,128)(2,1)S(1)}, u32[]{:S(2)}, u32[]{:S(2)}) collective-permute-start(bf16[384,256]{1,0:T(8,128)(2,1)S(1)} %add_convert_fusion), channel_id=1, source_target_pairs={{0,2},{1,3},{2,0},{3,1},{4,6},{5,7},{6,4},{7,5},{8,10},{9,11},{10,... | collective-permute-start | bytes 589832 | tf_op jit(solution)/shard_map/ppermute | solution.py:235

commit v4 on v3

--- a/solution.py
+++ b/solution.py
@@ -33,7 +33,7 @@
     return jnp.concatenate(parts, axis=0)
 
 
-def params(mib=40):
+def params(mib=24):
     return pltpu.CompilerParams(vmem_limit_bytes=mib * 1024 * 1024)
 
 
@@ -58,20 +58,20 @@
     return -(-2 * PARTS * heads // 16) * 16
 
 
-def pack_kernel(chunks, head_dim, q_hbm, do_hbm, o_hbm, lse_hbm, k_hbm, v_hbm, *rest):
-    count = len(chunks)
-    x_refs, kv_refs = rest[:count], rest[count : 2 * count]
-    q_ref, do_ref, o_ref, lse_ref, k_ref, v_ref, sems = rest[2 * count :]
-    sources = (q_hbm, do_hbm, o_hbm, lse_hbm, k_hbm, v_hbm)
-    targets = (q_ref, do_ref, o_ref, lse_ref, k_ref, v_ref)
+def fetch(sources, targets, sems):
     copies = [
         pltpu.make_async_copy(source, target, sems.at[i])
         for i, (source, target) in enumerate(zip(sources, targets))
     ]
     for copy in copies:
         copy.start()
-    for copy in copies[:4]:
+    for copy in copies:
         copy.wait()
+
+
+def pack_queries(chunks, head_dim, q_hbm, do_hbm, o_hbm, lse_hbm, *rest):
+    x_refs, (q_ref, do_ref, o_ref, lse_ref, sems) = rest[: len(chunks)], rest[len(chunks) :]
+    fetch((q_hbm, do_hbm, o_hbm, lse_hbm), (q_ref, do_ref, o_ref, lse_ref), sems)
     lse = lse_ref[...] * LOG2E
     first = 0
     for heads, out_ref in zip(chunks, x_refs):
@@ -91,8 +91,11 @@
             pieces.append(jnp.zeros((pad, lse.shape[1]), BF16))
         out_ref[2 * rows :] = join([piece.astype(F32) for piece in pieces]).astype(BF16)
         first += heads
-    for copy in copies[4:]:
-        copy.wait()
+
+
+def pack_keys(chunks, head_dim, k_hbm, v_hbm, token_ref, *rest):
+    kv_refs, (k_ref, v_ref, sems) = rest[: len(chunks)], rest[len(chunks) :]
+    fetch((k_hbm, v_hbm), (k_ref, v_ref), sems)
     first = 0
     for heads, out_ref in zip(chunks, kv_refs):
         rows = heads * head_dim
@@ -244,24 +247,27 @@
         return jax.ShapeDtypeStruct((rows, tokens), dtype)
 
     x_rows = [2 * h * head_dim + extra_rows(h) for h in chunks]
-    packed = pl.pallas_call(
-        functools.partial(pack_kernel, chunks, head_dim),
-        out_shape=[shape(n, BF16) for n in x_rows] + [shape(2 * h * head_dim, BF16) for h in chunks],
-        in_specs=[pl.BlockSpec(memory_space=pltpu.HBM)] * 6,
-        out_specs=[VMEM] * (2 * len(chunks)),
+    hbm = pl.BlockSpec(memory_space=pltpu.HBM)
+    fixed = lambda *values: [pltpu.with_memory_space_constraint(v, pltpu.HBM) for v in values]
+    x_own = pl.pallas_call(
+        functools.partial(pack_queries, chunks, head_dim),
+        out_shape=[shape(n, BF16) for n in x_rows],
+        in_specs=[hbm] * 4,
+        out_specs=[VMEM] * len(chunks),
         scratch_shapes=[pltpu.VMEM((tokens, width), BF16)] * 3
-        + [pltpu.VMEM((HEADS, tokens), F32)]
-        + [pltpu.VMEM((tokens, width), BF16)] * 2
-        + [pltpu.SemaphoreType.DMA((6,))],
+        + [pltpu.VMEM((HEADS, tokens), F32), pltpu.SemaphoreType.DMA((4,))],
         compiler_params=params(),
-        name="pack",
-    )(
-        *[
-            pltpu.with_memory_space_constraint(value, pltpu.HBM)
-            for value in (query_rows, grad_out, out_rows, normalizer, key_rows, value_rows)
-        ]
-    )
-    x_own, kv_own = packed[: len(chunks)], packed[len(chunks) :]
+        name="pack_queries",
+    )(*fixed(query_rows, grad_out, out_rows, normalizer))
+    kv_own = pl.pallas_call(
+        functools.partial(pack_keys, chunks, head_dim),
+        out_shape=[shape(2 * h * head_dim, BF16) for h in chunks],
+        in_specs=[hbm] * 2 + [pl.BlockSpec(memory_space=pl.ANY)],
+        out_specs=[VMEM] * len(chunks),
+        scratch_shapes=[pltpu.VMEM((tokens, width), BF16)] * 2 + [pltpu.SemaphoreType.DMA((2,))],
+        compiler_params=params(),
+        name="pack_keys",
+    )(*fixed(key_rows, value_rows), x_own[0])
     x_far = [send(x, across) for x in x_own]
     kv_level = [send(kv, level_in) for kv in kv_own]
     x_core = [send(x, core) for x in x_own]

time: 52.5 us -> 51.5 us (0.981); the launches traced: 53 us -> 51.2 us
  Pallas kernels: 23.6 us -> 19 us
  waiting for transfers between devices: 13.5 us -> 15.4 us
  starting transfers between devices: 14 us -> 15.1 us
    pallas_call x4, Pallas kernels: 12.9 us -> 9.94 us  [far(): pl.pallas_call(functools.partial(far_kernel, chunks[c], head_dim, factor,...]
    pallas_call x2, Pallas kernels: 7.29 us -> 4.51 us  [near(): pl.pallas_call(functools.partial(near_kernel, chunks, head_dim, factor, c...]
    ppermute x18, waiting for transfers between devices: 13.5 us -> 15.4 us  [send(): return lax.ppermute(value, 'tok', [(a, b % count) for a, b in pairs])]
    pallas_call x1 -> x2, Pallas kernels: 1.94 us -> 3.05 us  [the longest x1 1.66 us: per_device(): pl.pallas_call(functools.partial(pack_queries, chunks, head_dim), out_sha...]
    ppermute x18, starting transfers between devices: 14 us -> 15.1 us  [send(): return lax.ppermute(value, 'tok', [(a, b % count) for a, b in pairs])]
  transfers between devices with their start and end apart: 18 -> 18, of which waited for: 5 -> 6; matrix products, arithmetic and copies ran while one was open for 2% -> 2% of each run, Pallas kernels for 38% -> 31%
where the time goes in v4:
time: 51.5 us; the launch traced here: 51.2 us
  Pallas kernels  19 us (37%)
  waiting for transfers between devices  15.4 us (30%)
  starting transfers between devices  15.1 us (29%)
  local copies, waits for them, and re-layouts  0.82 us (2%)
  between operations  0.81 us (2%)
    ppermute x18, waiting for transfers between devices, send(): return lax.ppermute(value, 'tok', [(a, b % count) for a, b in pairs])  15.4 us
    ppermute x18, starting transfers between devices, send(): return lax.ppermute(value, 'tok', [(a, b % count) for a, b in pairs])  15.1 us
    pallas_call x4, Pallas kernels, far(): pl.pallas_call(functools.partial(far_kernel, chunks[c], head_dim, factor,...  9.94 us
    pallas_call x2, Pallas kernels, near(): pl.pallas_call(functools.partial(near_kernel, chunks, head_dim, factor, c...  4.51 us
    pallas_call x1, Pallas kernels, per_device(): pl.pallas_call(functools.partial(pack_queries, chunks, head_dim), out_sha...  1.66 us
    pallas_call x1, Pallas kernels, per_device(): pl.pallas_call(functools.partial(finish_kernel, chunks, head_dim, scale),...  1.49 us
    pallas_call x1, Pallas kernels, per_device(): pl.pallas_call(functools.partial(pack_keys, chunks, head_dim), out_shape=...  1.39 us
  transfers between devices with their start and end apart: 18, of which 6 were waited for; matrix products, arithmetic and copies ran while one was open for 2% of the time, Pallas kernels for 31%

profile of v4, /device:TPU:0, one launch (start us, length us, event | category | flops | bytes accessed | tf_op | source)
XLA Modules:
  0.0 51.2 jit_solution(1219424681154733518)
XLA Ops:
  0.6 1.7 %pack_queries.1 = (bf16[816,256]{1,0:T(8,128)(2,1)S(1)}, bf16[816,256]{1,0:T(8,128)(2,1)S(1)}) custom-call(bf16[256,768]{1,0:T(8,128)(2,1)} %q_hbm.1, bf16[256,768]{1,0:T(8,128)(2,1)} %do_hbm.1, bf16[256,768]{1,0:T(8,128)(2,1)} %o_hbm.1, f32[16,256]{1,0:T(8,128)} %lse_hbm.1), custom_call_target="tpu_custom_call" | custom-call | tf_op jit(solution)/shard_map/pack_queries/pallas_call | solution.py:252
  2.3 3.0 %collective-permute-start.2 = (bf16[816,256]{1,0:T(8,128)(2,1)S(1)}, bf16[816,256]{1,0:T(8,128)(2,1)S(1)}, u32[]{:S(2)}, u32[]{:S(2)}) collective-permute-start(bf16[816,256]{1,0:T(8,128)(2,1)S(1)} %get-tuple-element.53.token_ref.refs_0_), channel_id=1, source_target_pairs={{0,2},{1,3},{2,0},{3,1},{4,6},{5,7},{6,4},{7,5},{8,10},{9,11},{10,... | collective-permute-start | bytes 1253384 | tf_op jit(solution)/shard_map/ppermute | solution.py:238
  5.5 1.4 %pack_keys.1 = (bf16[768,256]{1,0:T(8,128)(2,1)S(1)}, bf16[768,256]{1,0:T(8,128)(2,1)S(1)}) custom-call(bf16[256,768]{1,0:T(8,128)(2,1)} %k_hbm.1, bf16[256,768]{1,0:T(8,128)(2,1)} %v_hbm.1, bf16[816,256]{1,0:T(8,128)(2,1)S(1)} %get-tuple-element.53.token_ref.refs_0_), custom_call_target="tpu_custom_call" | custom-call | tf_op jit(solution)/shard_map/pack_keys/pallas_call | solution.py:262
  6.9 4.0 %collective-permute-start.5 = (bf16[768,256]{1,0:T(8,128)(2,1)S(1)}, bf16[768,256]{1,0:T(8,128)(2,1)}, u32[]{:S(2)}, u32[]{:S(2)}) collective-permute-start(bf16[768,256]{1,0:T(8,128)(2,1)S(1)} %get-tuple-element.38.refs_2_), channel_id=1, source_target_pairs={{0,12},{1,13},{2,6},{3,7},{4,0},{5,1},{6,10},{7,11},{8,4},{9,5},{1... | collective-permute-start | bytes 1179656 | tf_op jit(solution)/shard_map/ppermute | solution.py:238
  10.9 4.9 %collective-permute-done.2.x_ref = bf16[816,256]{1,0:T(8,128)(2,1)S(1)} collective-permute-done((bf16[816,256]{1,0:T(8,128)(2,1)S(1)}, bf16[816,256]{1,0:T(8,128)(2,1)S(1)}, u32[]{:S(2)}, u32[]{:S(2)}) %collective-permute-start.2) | collective-permute-done | bytes 417824 | tf_op jit(solution)/shard_map/ppermute | solution.py:238
  15.9 0.7 %slice.12 = bf16[384,256]{1,0:T(8,128)(2,1)} slice(bf16[816,256]{1,0:T(8,128)(2,1)S(1)} %collective-permute-done.2.x_ref), slice={[0:384], [0:256]} | slice | bytes 393216 | tf_op jit(solution)/shard_map/slice | solution.py:314
  16.6 0.5 collective-permute-start.3
  17.1 4.2 %collective-permute-start.8 = (bf16[768,256]{1,0:T(8,128)(2,1)S(1)}, bf16[768,256]{1,0:T(8,128)(2,1)}, u32[]{:S(2)}, u32[]{:S(2)}) collective-permute-start(bf16[768,256]{1,0:T(8,128)(2,1)S(1)} %get-tuple-element.44.refs_2_.refs_3_), channel_id=1, source_target_pairs={{0,12},{1,13},{2,6},{3,7},{4,0},{5,1},{6,10},{7,11},{8,4},{9,5},{1... | collective-permute-start | bytes 1179656 | tf_op jit(solution)/shard_map/ppermute | solution.py:238
  21.3 2.3 %far_tasks.4 = (f32[384,256]{1,0:T(8,128)S(1)}, f32[384,256]{1,0:T(8,128)S(1)}, f32[768,256]{1,0:T(8,128)S(1)}) custom-call(s32[16,5]{1,0:T(8,128)S(1)} %copy.15.keep_ref, s32[1]{0:T(128)} %bitcast.place_ref, bf16[816,256]{1,0:T(8,128)(2,1)S(1)} %collective-permute-done.2.x_ref, bf16[384,256]{1,0:T(8,128)(2,1)S(1)} %collective-permute-done.3.refs_0_, ...), custom_call_target="tpu_custom_call" | custom-call | flops 13421772 | bytes 1024 | tf_op jit(solution)/shard_map/far_tasks/pallas_call | solution.py:297
  23.7 2.7 %far_tasks.5 = (bf16[384,256]{1,0:T(8,128)(2,1)S(1)}, bf16[384,256]{1,0:T(8,128)(2,1)S(1)}, bf16[768,256]{1,0:T(8,128)(2,1)S(1)}) custom-call(s32[16,5]{1,0:T(8,128)S(1)} %copy.15.keep_ref, s32[1]{0:T(128)} %bitcast.place_ref, bf16[816,256]{1,0:T(8,128)(2,1)S(1)} %collective-permute-done.2.x_ref, bf16[384,256]{1,0:T(8,128)(2,1)S(1)} %collective-permute-done.3.refs_0_, ...), custom_call_target="tpu_custom_call" | custom-call | flops 13421772 | bytes 1024 | tf_op jit(solution)/shard_map/far_tasks/pallas_call | solution.py:297
  26.5 0.6 %collective-permute-start.6 = (bf16[384,256]{1,0:T(8,128)(2,1)S(1)}, bf16[384,256]{1,0:T(8,128)(2,1)S(1)}, u32[]{:S(2)}, u32[]{:S(2)}) collective-permute-start(bf16[384,256]{1,0:T(8,128)(2,1)S(1)} %slice.14), channel_id=1, source_target_pairs={{0,1},{1,0},{2,3},{3,2},{4,5},{5,4},{6,7},{7,6},{8,9},{9,8},{10,11... | collective-permute-start | bytes 589832 | tf_op jit(solution)/shard_map/ppermute | solution.py:238
  27.1 0.4 collective-permute-start.9
  27.5 0.7 %collective-permute-done.6.refs_0_ = bf16[384,256]{1,0:T(8,128)(2,1)S(1)} collective-permute-done((bf16[384,256]{1,0:T(8,128)(2,1)S(1)}, bf16[384,256]{1,0:T(8,128)(2,1)S(1)}, u32[]{:S(2)}, u32[]{:S(2)}) %collective-permute-start.6) | collective-permute-done | bytes 196640 | tf_op jit(solution)/shard_map/ppermute | solution.py:238
  28.2 2.3 %far_tasks.6 = (f32[384,256]{1,0:T(8,128)S(1)}, f32[384,256]{1,0:T(8,128)S(1)}, f32[768,256]{1,0:T(8,128)S(1)}) custom-call(s32[16,5]{1,0:T(8,128)S(1)} %copy.15.keep_ref, s32[1]{0:T(128)} %bitcast.place_ref, bf16[816,256]{1,0:T(8,128)(2,1)S(1)} %collective-permute-done.1.x_ref, bf16[384,256]{1,0:T(8,128)(2,1)S(1)} %collective-permute-done.6.refs_0_, ...), custom_call_target="tpu_custom_call" | custom-call | flops 13421772 | bytes 1024 | tf_op jit(solution)/shard_map/far_tasks/pallas_call | solution.py:297
  30.6 2.7 %far_tasks.7 = (bf16[384,256]{1,0:T(8,128)(2,1)S(1)}, bf16[384,256]{1,0:T(8,128)(2,1)S(1)}, bf16[768,256]{1,0:T(8,128)(2,1)S(1)}) custom-call(s32[16,5]{1,0:T(8,128)S(1)} %copy.15.keep_ref, s32[1]{0:T(128)} %bitcast.place_ref, bf16[816,256]{1,0:T(8,128)(2,1)S(1)} %collective-permute-done.1.x_ref, bf16[384,256]{1,0:T(8,128)(2,1)S(1)} %collective-permute-done.6.refs_0_, ...), custom_call_target="tpu_custom_call" | custom-call | flops 13421772 | bytes 1024 | tf_op jit(solution)/shard_map/far_tasks/pallas_call | solution.py:297
  33.9 1.0 %near_tasks.2 = (bf16[384,256]{1,0:T(8,128)(2,1)S(1)}, f32[768,256]{1,0:T(8,128)S(1)}, bf16[384,256]{1,0:T(8,128)(2,1)S(1)}, f32[768,256]{1,0:T(8,128)S(1)}) custom-call(s32[16,5]{1,0:T(8,128)S(1)} %copy.15.keep_ref, s32[1]{0:T(128)} %bitcast.place_ref, bf16[816,256]{1,0:T(8,128)(2,1)S(1)} %collective-permute-done.refs_0_, ...), custom_call_target="tpu_custom_call" | custom-call | flops 26843544 | bytes 1024 | tf_op jit(solution)/shard_map/near_tasks/pallas_call | solution.py:283
  34.9 0.3 collective-permute-start.14
  35.2 0.3 collective-permute-start.11
  35.5 6.4 %collective-permute-done.10.refs_6_ = bf16[768,256]{1,0:T(8,128)(2,1)S(1)} collective-permute-done((bf16[768,256]{1,0:T(8,128)(2,1)S(1)}, bf16[768,256]{1,0:T(8,128)(2,1)S(1)}, u32[]{:S(2)}, u32[]{:S(2)}) %collective-permute-start.10) | collective-permute-done | bytes 393248 | tf_op jit(solution)/shard_map/ppermute | solution.py:238
  41.9 1.0 %collective-permute-start.16 = (bf16[384,256]{1,0:T(8,128)(2,1)S(1)}, bf16[384,256]{1,0:T(8,128)(2,1)S(1)}, u32[]{:S(2)}, u32[]{:S(2)}) collective-permute-start(bf16[384,256]{1,0:T(8,128)(2,1)S(1)} %add_convert_fusion), channel_id=1, source_target_pairs={{0,2},{1,3},{2,0},{3,1},{4,6},{5,7},{6,4},{7,5},{8,10},{9,11},{10,... | collective-permute-start | bytes 589832 | tf_op jit(solution)/shard_map/ppermute | solution.py:238
  42.9 3.5 %near_tasks.3 = (f32[384,256]{1,0:T(8,128)S(1)}, f32[768,256]{1,0:T(8,128)S(1)}, f32[384,256]{1,0:T(8,128)S(1)}, f32[768,256]{1,0:T(8,128)S(1)}) custom-call(s32[16,5]{1,0:T(8,128)S(1)} %copy.15.keep_ref, s32[1]{0:T(128)} %bitcast.place_ref, bf16[816,256]{1,0:T(8,128)(2,1)S(1)} %get-tuple-element.53.token_ref.refs_0_, ...), custom_call_target="tpu_custom_call" | custom-call | flops 26843544 | bytes 1024 | tf_op jit(solution)/shard_map/near_tasks/pallas_call | solution.py:283
  46.4 1.6 %collective-permute-done.16.refs_9_ = bf16[384,256]{1,0:T(8,128)(2,1)S(1)} collective-permute-done((bf16[384,256]{1,0:T(8,128)(2,1)S(1)}, bf16[384,256]{1,0:T(8,128)(2,1)S(1)}, u32[]{:S(2)}, u32[]{:S(2)}) %collective-permute-start.16) | collective-permute-done | bytes 196640 | tf_op jit(solution)/shard_map/ppermute | solution.py:238
  48.0 1.7 %collective-permute-done.17.refs_13_ = bf16[768,256]{1,0:T(8,128)(2,1)S(1)} collective-permute-done((bf16[768,256]{1,0:T(8,128)(2,1)S(1)}, bf16[768,256]{1,0:T(8,128)(2,1)S(1)}, u32[]{:S(2)}, u32[]{:S(2)}) %collective-permute-start.17) | collective-permute-done | bytes 393248 | tf_op jit(solution)/shard_map/ppermute | solution.py:238
  49.7 1.5 %finish.1 = (bf16[256,768]{1,0:T(8,128)(2,1)}, bf16[256,768]{1,0:T(8,128)(2,1)}, bf16[256,768]{1,0:T(8,128)(2,1)}) custom-call(f32[384,256]{1,0:T(8,128)S(1)} %get-tuple-element.55.refs_0_, bf16[384,256]{1,0:T(8,128)(2,1)S(1)} %collective-permute-done.11.refs_1_, bf16[384,256]{1,0:T(8,128)(2,1)S(1)} %collective-permute-done.13.refs_2_, ...), custom_call_target="tpu_custom_call" | custom-call | tf_op jit(solution)/shard_map/finish/pallas_call | solution.py:336
  (30 shorter events, 1.3 us)
Async XLA Ops:
  2.3 13.5 %collective-permute-start.2 = (bf16[816,256]{1,0:T(8,128)(2,1)S(1)}, bf16[816,256]{1,0:T(8,128)(2,1)S(1)}, u32[]{:S(2)}, u32[]{:S(2)}) collective-permute-start(bf16[816,256]{1,0:T(8,128)(2,1)S(1)} %get-tuple-element.53.token_ref.refs_0_), channel_id=1, source_target_pairs={{0,2},{1,3},{2,0},{3,1},{4,6},{5,7},{6,4},{7,5},{8,10},{9,11},{10,... | collective-permute-start | bytes 1253384 | tf_op jit(solution)/shard_map/ppermute | solution.py:238
  5.3 10.5 %collective-permute-start = (bf16[816,256]{1,0:T(8,128)(2,1)S(1)}, bf16[816,256]{1,0:T(8,128)(2,1)S(1)}, u32[]{:S(2)}, u32[]{:S(2)}) collective-permute-start(bf16[816,256]{1,0:T(8,128)(2,1)S(1)} %get-tuple-element.53.token_ref.refs_0_), channel_id=1, source_target_pairs={{0,1},{1,0},{2,3},{3,2},{4,5},{5,4},{6,7},{7,6},{8,9},{9,8},{10,11... | collective-permute-start | bytes 1253384 | tf_op jit(solution)/shard_map/ppermute | solution.py:238
  5.3 21.0 %collective-permute-start.1 = (bf16[816,256]{1,0:T(8,128)(2,1)S(1)}, bf16[816,256]{1,0:T(8,128)(2,1)S(1)}, u32[]{:S(2)}, u32[]{:S(2)}) collective-permute-start(bf16[816,256]{1,0:T(8,128)(2,1)S(1)} %get-tuple-element.54.refs_1_), channel_id=1, source_target_pairs={{0,2},{1,3},{2,0},{3,1},{4,6},{5,7},{6,4},{7,5},{8,10},{9,11},{10,... | collective-permute-start | bytes 1253384 | tf_op jit(solution)/shard_map/ppermute | solution.py:238
  6.9 16.8 %collective-permute-start.5 = (bf16[768,256]{1,0:T(8,128)(2,1)S(1)}, bf16[768,256]{1,0:T(8,128)(2,1)}, u32[]{:S(2)}, u32[]{:S(2)}) collective-permute-start(bf16[768,256]{1,0:T(8,128)(2,1)S(1)} %get-tuple-element.38.refs_2_), channel_id=1, source_target_pairs={{0,12},{1,13},{2,6},{3,7},{4,0},{5,1},{6,10},{7,11},{8,4},{9,5},{1... | collective-permute-start | bytes 1179656 | tf_op jit(solution)/shard_map/ppermute | solution.py:238
  15.8 5.5 %collective-permute-start.4 = (bf16[432,256]{1,0:T(8,128)(2,1)S(1)}, bf16[432,256]{1,0:T(8,128)(2,1)S(1)}, u32[]{:S(2)}, u32[]{:S(2)}) collective-permute-start(bf16[432,256]{1,0:T(8,128)(2,1)S(1)} %slice.13), channel_id=1, source_target_pairs={{0,1},{1,0},{2,3},{3,2},{4,5},{5,4},{6,7},{7,6},{8,9},{9,8},{10,11... | collective-permute-start | bytes 663560 | tf_op jit(solution)/shard_map/ppermute | solution.py:238
  16.6 4.7 %copy-start = (s32[16,5]{0,1:T(8,128)S(1)}, s32[16,5]{0,1:T(8,128)}, u32[]{:S(2)}) copy-start(s32[16,5]{0,1:T(8,128)} %param.13) | copy-start | bytes 964
  16.6 4.8 %collective-permute-start.3 = (bf16[384,256]{1,0:T(8,128)(2,1)}, bf16[384,256]{1,0:T(8,128)(2,1)S(1)}, u32[]{:S(2)}, u32[]{:S(2)}) collective-permute-start(bf16[384,256]{1,0:T(8,128)(2,1)} %slice.12), channel_id=1, source_target_pairs={{0,1},{1,0},{2,3},{3,2},{4,5},{5,4},{6,7},{7,6},{8,9},{9,8},{10,11... | collective-permute-start | bytes 589832 | tf_op jit(solution)/shard_map/ppermute | solution.py:238
  17.1 13.6 %collective-permute-start.8 = (bf16[768,256]{1,0:T(8,128)(2,1)S(1)}, bf16[768,256]{1,0:T(8,128)(2,1)}, u32[]{:S(2)}, u32[]{:S(2)}) collective-permute-start(bf16[768,256]{1,0:T(8,128)(2,1)S(1)} %get-tuple-element.44.refs_2_.refs_3_), channel_id=1, source_target_pairs={{0,12},{1,13},{2,6},{3,7},{4,0},{5,1},{6,10},{7,11},{8,4},{9,5},{1... | collective-permute-start | bytes 1179656 | tf_op jit(solution)/shard_map/ppermute | solution.py:238
  26.4 1.8 %collective-permute-start.7 = (bf16[432,256]{1,0:T(8,128)(2,1)S(1)}, bf16[432,256]{1,0:T(8,128)(2,1)S(1)}, u32[]{:S(2)}, u32[]{:S(2)}) collective-permute-start(bf16[432,256]{1,0:T(8,128)(2,1)S(1)} %slice.15), channel_id=1, source_target_pairs={{0,1},{1,0},{2,3},{3,2},{4,5},{5,4},{6,7},{7,6},{8,9},{9,8},{10,11... | collective-permute-start | bytes 663560 | tf_op jit(solution)/shard_map/ppermute | solution.py:238
  26.5 1.7 %collective-permute-start.6 = (bf16[384,256]{1,0:T(8,128)(2,1)S(1)}, bf16[384,256]{1,0:T(8,128)(2,1)S(1)}, u32[]{:S(2)}, u32[]{:S(2)}) collective-permute-start(bf16[384,256]{1,0:T(8,128)(2,1)S(1)} %slice.14), channel_id=1, source_target_pairs={{0,1},{1,0},{2,3},{3,2},{4,5},{5,4},{6,7},{7,6},{8,9},{9,8},{10,11... | collective-permute-start | bytes 589832 | tf_op jit(solution)/shard_map/ppermute | solution.py:238
  27.0 6.5 %collective-permute-start.12 = (bf16[384,256]{1,0:T(8,128)(2,1)S(1)}, bf16[384,256]{1,0:T(8,128)(2,1)S(1)}, u32[]{:S(2)}, u32[]{:S(2)}) collective-permute-start(bf16[384,256]{1,0:T(8,128)(2,1)S(1)} %get-tuple-element.56), channel_id=1, source_target_pairs={{0,1},{1,0},{2,3},{3,2},{4,5},{5,4},{6,7},{7,6},{8,9},{9,8},{10,11... | collective-permute-start | bytes 589832 | tf_op jit(solution)/shard_map/ppermute | solution.py:238
  27.1 6.5 %collective-permute-start.9 = (bf16[816,256]{1,0:T(8,128)(2,1)S(1)}, bf16[816,256]{1,0:T(8,128)(2,1)S(1)}, u32[]{:S(2)}, u32[]{:S(2)}) collective-permute-start(bf16[816,256]{1,0:T(8,128)(2,1)S(1)} %get-tuple-element.54.refs_1_), channel_id=1, source_target_pairs={{0,1},{1,0},{2,3},{3,2},{4,5},{5,4},{6,7},{7,6},{8,9},{9,8},{10,11... | collective-permute-start | bytes 1253384 | tf_op jit(solution)/shard_map/ppermute | solution.py:238
  28.2 13.7 %collective-permute-start.10 = (bf16[768,256]{1,0:T(8,128)(2,1)S(1)}, bf16[768,256]{1,0:T(8,128)(2,1)S(1)}, u32[]{:S(2)}, u32[]{:S(2)}) collective-permute-start(bf16[768,256]{1,0:T(8,128)(2,1)S(1)} %get-tuple-element.52), channel_id=1, source_target_pairs={{0,4},{1,5},{2,14},{3,15},{4,8},{5,9},{6,2},{7,3},{8,12},{9,13},{1... | collective-permute-start | bytes 1179656 | tf_op jit(solution)/shard_map/ppermute | solution.py:238
  33.3 1.9 %collective-permute-start.15 = (bf16[384,256]{1,0:T(8,128)(2,1)S(1)}, bf16[384,256]{1,0:T(8,128)(2,1)S(1)}, u32[]{:S(2)}, u32[]{:S(2)}) collective-permute-start(bf16[384,256]{1,0:T(8,128)(2,1)S(1)} %get-tuple-element.62), channel_id=1, source_target_pairs={{0,1},{1,0},{2,3},{3,2},{4,5},{5,4},{6,7},{7,6},{8,9},{9,8},{10,11... | collective-permute-start | bytes 589832 | tf_op jit(solution)/shard_map/ppermute | solution.py:238
  33.6 12.8 %collective-permute-start.13 = (bf16[384,256]{1,0:T(8,128)(2,1)S(1)}, bf16[384,256]{1,0:T(8,128)(2,1)S(1)}, u32[]{:S(2)}, u32[]{:S(2)}) collective-permute-start(bf16[384,256]{1,0:T(8,128)(2,1)S(1)} %add_convert_fusion.1), channel_id=1, source_target_pairs={{0,2},{1,3},{2,0},{3,1},{4,6},{5,7},{6,4},{7,5},{8,10},{9,11},{10,... | collective-permute-start | bytes 589832 | tf_op jit(solution)/shard_map/ppermute | solution.py:238
  33.7 16.1 %collective-permute-start.17 = (bf16[768,256]{1,0:T(8,128)(2,1)S(1)}, bf16[768,256]{1,0:T(8,128)(2,1)S(1)}, u32[]{:S(2)}, u32[]{:S(2)}) collective-permute-start(bf16[768,256]{1,0:T(8,128)(2,1)S(1)} %get-tuple-element.66), channel_id=1, source_target_pairs={{0,4},{1,5},{2,14},{3,15},{4,8},{5,9},{6,2},{7,3},{8,12},{9,13},{1... | collective-permute-start | bytes 1179656 | tf_op jit(solution)/shard_map/ppermute | solution.py:238
  34.9 11.6 %collective-permute-start.14 = (bf16[384,256]{1,0:T(8,128)(2,1)S(1)}, bf16[384,256]{1,0:T(8,128)(2,1)S(1)}, u32[]{:S(2)}, u32[]{:S(2)}) collective-permute-start(bf16[384,256]{1,0:T(8,128)(2,1)S(1)} %get-tuple-element.61), channel_id=1, source_target_pairs={{0,1},{1,0},{2,3},{3,2},{4,5},{5,4},{6,7},{7,6},{8,9},{9,8},{10,11... | collective-permute-start | bytes 589832 | tf_op jit(solution)/shard_map/ppermute | solution.py:238
  35.2 11.3 %collective-permute-start.11 = (bf16[384,256]{1,0:T(8,128)(2,1)S(1)}, bf16[384,256]{1,0:T(8,128)(2,1)S(1)}, u32[]{:S(2)}, u32[]{:S(2)}) collective-permute-start(bf16[384,256]{1,0:T(8,128)(2,1)S(1)} %get-tuple-element.51), channel_id=1, source_target_pairs={{0,1},{1,0},{2,3},{3,2},{4,5},{5,4},{6,7},{7,6},{8,9},{9,8},{10,11... | collective-permute-start | bytes 589832 | tf_op jit(solution)/shard_map/ppermute | solution.py:238
  41.9 6.1 %collective-permute-start.16 = (bf16[384,256]{1,0:T(8,128)(2,1)S(1)}, bf16[384,256]{1,0:T(8,128)(2,1)S(1)}, u32[]{:S(2)}, u32[]{:S(2)}) collective-permute-start(bf16[384,256]{1,0:T(8,128)(2,1)S(1)} %add_convert_fusion), channel_id=1, source_target_pairs={{0,2},{1,3},{2,0},{3,1},{4,6},{5,7},{6,4},{7,5},{8,10},{9,11},{10,... | collective-permute-start | bytes 589832 | tf_op jit(solution)/shard_map/ppermute | solution.py:238

commit v5 on v3

--- a/solution.py
+++ b/solution.py
@@ -14,6 +14,7 @@
 PARTS = 3
 CHUNK_HEADS = (8, 8)
 HOPS = 2
+AHEAD = 2
 CORE_COST, FAR_COST, SELF_COST = (0.01, 0.01, 0.01)
 NN = (((1,), (0,)), ((), ()))
 NT = (((1,), (1,)), ((), ()))
@@ -33,7 +34,7 @@
     return jnp.concatenate(parts, axis=0)
 
 
-def params(mib=40):
+def params(mib=24):
     return pltpu.CompilerParams(vmem_limit_bytes=mib * 1024 * 1024)
 
 
@@ -127,15 +128,22 @@
 def task(queries, keys, factor):
     q, do, lse, delta = queries
     k, v = keys
-    span = range(len(q))
-    scores = [dot(k[i], q[i], TN) for i in span]
-    prob_grad = [dot(v[i], do[i], TN) for i in span]
-    probs = [jnp.exp2(scores[i] * factor - lse[i]) for i in span]
-    score_grad = [(probs[i] * (prob_grad[i] - delta[i])).astype(BF16) for i in span]
-    probs = [x.astype(BF16) for x in probs]
-    dv = [dot(do[i], probs[i], NT) for i in span]
-    dk = [dot(q[i], score_grad[i], NT) for i in span]
-    dq = [dot(k[i], score_grad[i], NN) for i in span]
+    size = len(q)
+    dq, dk, dv = [], [], []
+    ready = []
+    for i in range(size + AHEAD):
+        if i < size:
+            scores = dot(k[i], q[i], TN)
+            prob_grad = dot(v[i], do[i], TN)
+            probs = jnp.exp2(scores * factor - lse[i])
+            score_grad = (probs * (prob_grad - delta[i])).astype(BF16)
+            ready.append((probs.astype(BF16), score_grad))
+        if i >= AHEAD:
+            h = i - AHEAD
+            probs, score_grad = ready[h]
+            dv.append(dot(do[h], probs, NT))
+            dk.append(dot(q[h], score_grad, NT))
+            dq.append(dot(k[h], score_grad, NN))
     return dq, dk, dv
 
 

time: 52.5 us -> 50.3 us (0.958)
  Pallas kernels: 23.6 us -> 15.6 us
  starting transfers between devices: 14 us -> 18.1 us
  waiting for transfers between devices: 13.5 us -> 15.3 us
    pallas_call x4, Pallas kernels: 12.9 us -> 8.49 us  [far(): pl.pallas_call(functools.partial(far_kernel, chunks[c], head_dim, factor,...]
    ppermute x18, starting transfers between devices: 14 us -> 18.1 us  [send(): return lax.ppermute(value, 'tok', [(a, b % count) for a, b in pairs])]
    pallas_call x2, Pallas kernels: 7.29 us -> 3.75 us  [near(): pl.pallas_call(functools.partial(near_kernel, chunks, head_dim, factor, c...]
    ppermute x18, waiting for transfers between devices: 13.5 us -> 15.3 us  [send(): return lax.ppermute(value, 'tok', [(a, b % count) for a, b in pairs])]
  transfers between devices with their start and end apart: 18 -> 18, of which waited for: 5 -> 6; matrix products, arithmetic and copies ran while one was open for 2% -> 2% of each run, Pallas kernels for 38% -> 24%
where the time goes in v5:
time: 50.3 us; the launch traced here: 50.7 us
  starting transfers between devices  18.1 us (36%)
  Pallas kernels  15.6 us (31%)
  waiting for transfers between devices  15.3 us (30%)
  local copies, waits for them, and re-layouts  0.82 us (2%)
  between operations  0.8 us (2%)
    ppermute x18, starting transfers between devices, send(): return lax.ppermute(value, 'tok', [(a, b % count) for a, b in pairs])  18.1 us
    ppermute x18, waiting for transfers between devices, send(): return lax.ppermute(value, 'tok', [(a, b % count) for a, b in pairs])  15.3 us
    pallas_call x4, Pallas kernels, far(): pl.pallas_call(functools.partial(far_kernel, chunks[c], head_dim, factor,...  8.49 us
    pallas_call x2, Pallas kernels, near(): pl.pallas_call(functools.partial(near_kernel, chunks, head_dim, factor, c...  3.75 us
    pallas_call x1, Pallas kernels, per_device(): pl.pallas_call(functools.partial(pack_kernel, chunks, head_dim), out_shap...  1.94 us
    pallas_call x1, Pallas kernels, per_device(): pl.pallas_call(functools.partial(finish_kernel, chunks, head_dim, scale),...  1.47 us
  transfers between devices with their start and end apart: 18, of which 6 were waited for; matrix products, arithmetic and copies ran while one was open for 2% of the time, Pallas kernels for 24%

profile of v5, /device:TPU:0, one launch (start us, length us, event | category | flops | bytes accessed | tf_op | source)
XLA Modules:
  0.0 50.7 jit_solution(17908042321789439897)
XLA Ops:
  0.6 1.9 %pack.1 = (bf16[816,256]{1,0:T(8,128)(2,1)S(1)}, bf16[816,256]{1,0:T(8,128)(2,1)S(1)}, bf16[768,256]{1,0:T(8,128)(2,1)S(1)}, bf16[768,256]{1,0:T(8,128)(2,1)S(1)}) custom-call(bf16[256,768]{1,0:T(8,128)(2,1)} %q_hbm.1, bf16[256,768]{1,0:T(8,128)(2,1)} %do_hbm.1, bf16[256,768]{1,0:T(8,128)(2,1)} %o_hbm.1, f32[16,256]{1,0:T(8,128)} %lse_hbm.1, ...), custom_call_target="tpu_custom_call" | custom-call | tf_op jit(solution)/shard_map/pack/pallas_call | solution.py:255
  2.6 3.0 %collective-permute-start.2 = (bf16[816,256]{1,0:T(8,128)(2,1)S(1)}, bf16[816,256]{1,0:T(8,128)(2,1)S(1)}, u32[]{:S(2)}, u32[]{:S(2)}) collective-permute-start(bf16[816,256]{1,0:T(8,128)(2,1)S(1)} %get-tuple-element.53.refs_0_), channel_id=1, source_target_pairs={{0,2},{1,3},{2,0},{3,1},{4,6},{5,7},{6,4},{7,5},{8,10},{9,11},{10,... | collective-permute-start | bytes 1253384 | tf_op jit(solution)/shard_map/ppermute | solution.py:243
  5.7 4.0 %collective-permute-start.5 = (bf16[768,256]{1,0:T(8,128)(2,1)S(1)}, bf16[768,256]{1,0:T(8,128)(2,1)}, u32[]{:S(2)}, u32[]{:S(2)}) collective-permute-start(bf16[768,256]{1,0:T(8,128)(2,1)S(1)} %get-tuple-element.38.refs_2_), channel_id=1, source_target_pairs={{0,12},{1,13},{2,6},{3,7},{4,0},{5,1},{6,10},{7,11},{8,4},{9,5},{1... | collective-permute-start | bytes 1179656 | tf_op jit(solution)/shard_map/ppermute | solution.py:243
  9.7 6.3 %collective-permute-done.2.x_ref = bf16[816,256]{1,0:T(8,128)(2,1)S(1)} collective-permute-done((bf16[816,256]{1,0:T(8,128)(2,1)S(1)}, bf16[816,256]{1,0:T(8,128)(2,1)S(1)}, u32[]{:S(2)}, u32[]{:S(2)}) %collective-permute-start.2) | collective-permute-done | bytes 417824 | tf_op jit(solution)/shard_map/ppermute | solution.py:243
  16.2 0.7 %slice.12 = bf16[384,256]{1,0:T(8,128)(2,1)} slice(bf16[816,256]{1,0:T(8,128)(2,1)S(1)} %collective-permute-done.2.x_ref), slice={[0:384], [0:256]} | slice | bytes 393216 | tf_op jit(solution)/shard_map/slice | solution.py:316
  16.8 0.5 collective-permute-start.3
  17.3 4.2 %collective-permute-start.8 = (bf16[768,256]{1,0:T(8,128)(2,1)S(1)}, bf16[768,256]{1,0:T(8,128)(2,1)}, u32[]{:S(2)}, u32[]{:S(2)}) collective-permute-start(bf16[768,256]{1,0:T(8,128)(2,1)S(1)} %get-tuple-element.44.refs_2_.refs_3_), channel_id=1, source_target_pairs={{0,12},{1,13},{2,6},{3,7},{4,0},{5,1},{6,10},{7,11},{8,4},{9,5},{1... | collective-permute-start | bytes 1179656 | tf_op jit(solution)/shard_map/ppermute | solution.py:243
  21.6 2.0 %far_tasks.4 = (f32[384,256]{1,0:T(8,128)S(1)}, f32[384,256]{1,0:T(8,128)S(1)}, f32[768,256]{1,0:T(8,128)S(1)}) custom-call(s32[16,5]{1,0:T(8,128)S(1)} %copy.15.keep_ref, s32[1]{0:T(128)} %bitcast.place_ref, bf16[816,256]{1,0:T(8,128)(2,1)S(1)} %collective-permute-done.2.x_ref, bf16[384,256]{1,0:T(8,128)(2,1)S(1)} %collective-permute-done.3.refs_0_, ...), custom_call_target="tpu_custom_call" | custom-call | flops 13421772 | bytes 1024 | tf_op jit(solution)/shard_map/far_tasks/pallas_call | solution.py:299
  23.6 2.3 %far_tasks.5 = (bf16[384,256]{1,0:T(8,128)(2,1)S(1)}, bf16[384,256]{1,0:T(8,128)(2,1)S(1)}, bf16[768,256]{1,0:T(8,128)(2,1)S(1)}) custom-call(s32[16,5]{1,0:T(8,128)S(1)} %copy.15.keep_ref, s32[1]{0:T(128)} %bitcast.place_ref, bf16[816,256]{1,0:T(8,128)(2,1)S(1)} %collective-permute-done.2.x_ref, bf16[384,256]{1,0:T(8,128)(2,1)S(1)} %collective-permute-done.3.refs_0_, ...), custom_call_target="tpu_custom_call" | custom-call | flops 13421772 | bytes 1024 | tf_op jit(solution)/shard_map/far_tasks/pallas_call | solution.py:299
  26.0 0.6 %collective-permute-start.6 = (bf16[384,256]{1,0:T(8,128)(2,1)S(1)}, bf16[384,256]{1,0:T(8,128)(2,1)S(1)}, u32[]{:S(2)}, u32[]{:S(2)}) collective-permute-start(bf16[384,256]{1,0:T(8,128)(2,1)S(1)} %slice.14), channel_id=1, source_target_pairs={{0,1},{1,0},{2,3},{3,2},{4,5},{5,4},{6,7},{7,6},{8,9},{9,8},{10,11... | collective-permute-start | bytes 589832 | tf_op jit(solution)/shard_map/ppermute | solution.py:243
  26.7 0.4 collective-permute-start.9
  27.1 0.7 %collective-permute-done.6.refs_0_ = bf16[384,256]{1,0:T(8,128)(2,1)S(1)} collective-permute-done((bf16[384,256]{1,0:T(8,128)(2,1)S(1)}, bf16[384,256]{1,0:T(8,128)(2,1)S(1)}, u32[]{:S(2)}, u32[]{:S(2)}) %collective-permute-start.6) | collective-permute-done | bytes 196640 | tf_op jit(solution)/shard_map/ppermute | solution.py:243
  27.8 1.9 %far_tasks.6 = (f32[384,256]{1,0:T(8,128)S(1)}, f32[384,256]{1,0:T(8,128)S(1)}, f32[768,256]{1,0:T(8,128)S(1)}) custom-call(s32[16,5]{1,0:T(8,128)S(1)} %copy.15.keep_ref, s32[1]{0:T(128)} %bitcast.place_ref, bf16[816,256]{1,0:T(8,128)(2,1)S(1)} %collective-permute-done.1.x_ref, bf16[384,256]{1,0:T(8,128)(2,1)S(1)} %collective-permute-done.6.refs_0_, ...), custom_call_target="tpu_custom_call" | custom-call | flops 13421772 | bytes 1024 | tf_op jit(solution)/shard_map/far_tasks/pallas_call | solution.py:299
  29.8 1.2 %collective-permute-done.8.refs_2_ = bf16[768,256]{1,0:T(8,128)(2,1)} collective-permute-done((bf16[768,256]{1,0:T(8,128)(2,1)S(1)}, bf16[768,256]{1,0:T(8,128)(2,1)}, u32[]{:S(2)}, u32[]{:S(2)}) %collective-permute-start.8) | collective-permute-done | bytes 393248 | tf_op jit(solution)/shard_map/ppermute | solution.py:243
  31.0 2.3 %far_tasks.7 = (bf16[384,256]{1,0:T(8,128)(2,1)S(1)}, bf16[384,256]{1,0:T(8,128)(2,1)S(1)}, bf16[768,256]{1,0:T(8,128)(2,1)S(1)}) custom-call(s32[16,5]{1,0:T(8,128)S(1)} %copy.15.keep_ref, s32[1]{0:T(128)} %bitcast.place_ref, bf16[816,256]{1,0:T(8,128)(2,1)S(1)} %collective-permute-done.1.x_ref, bf16[384,256]{1,0:T(8,128)(2,1)S(1)} %collective-permute-done.6.refs_0_, ...), custom_call_target="tpu_custom_call" | custom-call | flops 13421772 | bytes 1024 | tf_op jit(solution)/shard_map/far_tasks/pallas_call | solution.py:299
  33.4 1.6 %collective-permute-start.13 = (bf16[384,256]{1,0:T(8,128)(2,1)S(1)}, bf16[384,256]{1,0:T(8,128)(2,1)S(1)}, u32[]{:S(2)}, u32[]{:S(2)}) collective-permute-start(bf16[384,256]{1,0:T(8,128)(2,1)S(1)} %add_convert_fusion.1), channel_id=1, source_target_pairs={{0,2},{1,3},{2,0},{3,1},{4,6},{5,7},{6,4},{7,5},{8,10},{9,11},{10,... | collective-permute-start | bytes 589832 | tf_op jit(solution)/shard_map/ppermute | solution.py:243
  35.5 1.0 %near_tasks.2 = (bf16[384,256]{1,0:T(8,128)(2,1)S(1)}, f32[768,256]{1,0:T(8,128)S(1)}, bf16[384,256]{1,0:T(8,128)(2,1)S(1)}, f32[768,256]{1,0:T(8,128)S(1)}) custom-call(s32[16,5]{1,0:T(8,128)S(1)} %copy.15.keep_ref, s32[1]{0:T(128)} %bitcast.place_ref, bf16[816,256]{1,0:T(8,128)(2,1)S(1)} %collective-permute-done.refs_0_, ...), custom_call_target="tpu_custom_call" | custom-call | flops 26843544 | bytes 1024 | tf_op jit(solution)/shard_map/near_tasks/pallas_call | solution.py:285
  36.5 1.8 %collective-permute-start.14 = (bf16[384,256]{1,0:T(8,128)(2,1)S(1)}, bf16[384,256]{1,0:T(8,128)(2,1)S(1)}, u32[]{:S(2)}, u32[]{:S(2)}) collective-permute-start(bf16[384,256]{1,0:T(8,128)(2,1)S(1)} %get-tuple-element.61), channel_id=1, source_target_pairs={{0,1},{1,0},{2,3},{3,2},{4,5},{5,4},{6,7},{7,6},{8,9},{9,8},{10,11... | collective-permute-start | bytes 589832 | tf_op jit(solution)/shard_map/ppermute | solution.py:243
  38.5 3.0 %collective-permute-done.10.refs_6_ = bf16[768,256]{1,0:T(8,128)(2,1)S(1)} collective-permute-done((bf16[768,256]{1,0:T(8,128)(2,1)S(1)}, bf16[768,256]{1,0:T(8,128)(2,1)S(1)}, u32[]{:S(2)}, u32[]{:S(2)}) %collective-permute-start.10) | collective-permute-done | bytes 393248 | tf_op jit(solution)/shard_map/ppermute | solution.py:243
  41.5 1.0 %collective-permute-start.16 = (bf16[384,256]{1,0:T(8,128)(2,1)S(1)}, bf16[384,256]{1,0:T(8,128)(2,1)S(1)}, u32[]{:S(2)}, u32[]{:S(2)}) collective-permute-start(bf16[384,256]{1,0:T(8,128)(2,1)S(1)} %add_convert_fusion), channel_id=1, source_target_pairs={{0,2},{1,3},{2,0},{3,1},{4,6},{5,7},{6,4},{7,5},{8,10},{9,11},{10,... | collective-permute-start | bytes 589832 | tf_op jit(solution)/shard_map/ppermute | solution.py:243
  42.5 2.8 %near_tasks.3 = (f32[384,256]{1,0:T(8,128)S(1)}, f32[768,256]{1,0:T(8,128)S(1)}, f32[384,256]{1,0:T(8,128)S(1)}, f32[768,256]{1,0:T(8,128)S(1)}) custom-call(s32[16,5]{1,0:T(8,128)S(1)} %copy.15.keep_ref, s32[1]{0:T(128)} %bitcast.place_ref, bf16[816,256]{1,0:T(8,128)(2,1)S(1)} %get-tuple-element.53.refs_0_, bf16[816,256]{1,0:T(8,128)(2,1)S(1)} %get-tuple-element.54.refs_1_, ...), custom_call_target="tpu_custom_call" | custom-call | flops 26843544 | bytes 1024 | tf_op jit(solution)/shard_map/near_tasks/pallas_call | solution.py:285
  45.3 2.4 %collective-permute-done.16.refs_9_ = bf16[384,256]{1,0:T(8,128)(2,1)S(1)} collective-permute-done((bf16[384,256]{1,0:T(8,128)(2,1)S(1)}, bf16[384,256]{1,0:T(8,128)(2,1)S(1)}, u32[]{:S(2)}, u32[]{:S(2)}) %collective-permute-start.16) | collective-permute-done | bytes 196640 | tf_op jit(solution)/shard_map/ppermute | solution.py:243
  47.6 1.6 %collective-permute-done.17.refs_13_ = bf16[768,256]{1,0:T(8,128)(2,1)S(1)} collective-permute-done((bf16[768,256]{1,0:T(8,128)(2,1)S(1)}, bf16[768,256]{1,0:T(8,128)(2,1)S(1)}, u32[]{:S(2)}, u32[]{:S(2)}) %collective-permute-start.17) | collective-permute-done | bytes 393248 | tf_op jit(solution)/shard_map/ppermute | solution.py:243
  49.3 1.5 %finish.1 = (bf16[256,768]{1,0:T(8,128)(2,1)}, bf16[256,768]{1,0:T(8,128)(2,1)}, bf16[256,768]{1,0:T(8,128)(2,1)}) custom-call(f32[384,256]{1,0:T(8,128)S(1)} %get-tuple-element.55.refs_0_, bf16[384,256]{1,0:T(8,128)(2,1)S(1)} %collective-permute-done.11.refs_1_, bf16[384,256]{1,0:T(8,128)(2,1)S(1)} %collective-permute-done.13.refs_2_, ...), custom_call_target="tpu_custom_call" | custom-call | tf_op jit(solution)/shard_map/finish/pallas_call | solution.py:338
  (29 shorter events, 1.3 us)
Async XLA Ops:
  2.6 13.5 %collective-permute-start.2 = (bf16[816,256]{1,0:T(8,128)(2,1)S(1)}, bf16[816,256]{1,0:T(8,128)(2,1)S(1)}, u32[]{:S(2)}, u32[]{:S(2)}) collective-permute-start(bf16[816,256]{1,0:T(8,128)(2,1)S(1)} %get-tuple-element.53.refs_0_), channel_id=1, source_target_pairs={{0,2},{1,3},{2,0},{3,1},{4,6},{5,7},{6,4},{7,5},{8,10},{9,11},{10,... | collective-permute-start | bytes 1253384 | tf_op jit(solution)/shard_map/ppermute | solution.py:243
  5.6 10.5 %collective-permute-start = (bf16[816,256]{1,0:T(8,128)(2,1)S(1)}, bf16[816,256]{1,0:T(8,128)(2,1)S(1)}, u32[]{:S(2)}, u32[]{:S(2)}) collective-permute-start(bf16[816,256]{1,0:T(8,128)(2,1)S(1)} %get-tuple-element.53.refs_0_), channel_id=1, source_target_pairs={{0,1},{1,0},{2,3},{3,2},{4,5},{5,4},{6,7},{7,6},{8,9},{9,8},{10,11... | collective-permute-start | bytes 1253384 | tf_op jit(solution)/shard_map/ppermute | solution.py:243
  5.6 20.3 %collective-permute-start.1 = (bf16[816,256]{1,0:T(8,128)(2,1)S(1)}, bf16[816,256]{1,0:T(8,128)(2,1)S(1)}, u32[]{:S(2)}, u32[]{:S(2)}) collective-permute-start(bf16[816,256]{1,0:T(8,128)(2,1)S(1)} %get-tuple-element.54.refs_1_), channel_id=1, source_target_pairs={{0,2},{1,3},{2,0},{3,1},{4,6},{5,7},{6,4},{7,5},{8,10},{9,11},{10,... | collective-permute-start | bytes 1253384 | tf_op jit(solution)/shard_map/ppermute | solution.py:243
  5.7 17.9 %collective-permute-start.5 = (bf16[768,256]{1,0:T(8,128)(2,1)S(1)}, bf16[768,256]{1,0:T(8,128)(2,1)}, u32[]{:S(2)}, u32[]{:S(2)}) collective-permute-start(bf16[768,256]{1,0:T(8,128)(2,1)S(1)} %get-tuple-element.38.refs_2_), channel_id=1, source_target_pairs={{0,12},{1,13},{2,6},{3,7},{4,0},{5,1},{6,10},{7,11},{8,4},{9,5},{1... | collective-permute-start | bytes 1179656 | tf_op jit(solution)/shard_map/ppermute | solution.py:243
  16.1 5.5 %collective-permute-start.4 = (bf16[432,256]{1,0:T(8,128)(2,1)S(1)}, bf16[432,256]{1,0:T(8,128)(2,1)S(1)}, u32[]{:S(2)}, u32[]{:S(2)}) collective-permute-start(bf16[432,256]{1,0:T(8,128)(2,1)S(1)} %slice.13), channel_id=1, source_target_pairs={{0,1},{1,0},{2,3},{3,2},{4,5},{5,4},{6,7},{7,6},{8,9},{9,8},{10,11... | collective-permute-start | bytes 663560 | tf_op jit(solution)/shard_map/ppermute | solution.py:243
  16.8 4.7 %copy-start = (s32[16,5]{0,1:T(8,128)S(1)}, s32[16,5]{0,1:T(8,128)}, u32[]{:S(2)}) copy-start(s32[16,5]{0,1:T(8,128)} %param.13) | copy-start | bytes 964
  16.8 4.8 %collective-permute-start.3 = (bf16[384,256]{1,0:T(8,128)(2,1)}, bf16[384,256]{1,0:T(8,128)(2,1)S(1)}, u32[]{:S(2)}, u32[]{:S(2)}) collective-permute-start(bf16[384,256]{1,0:T(8,128)(2,1)} %slice.12), channel_id=1, source_target_pairs={{0,1},{1,0},{2,3},{3,2},{4,5},{5,4},{6,7},{7,6},{8,9},{9,8},{10,11... | collective-permute-start | bytes 589832 | tf_op jit(solution)/shard_map/ppermute | solution.py:243
  17.3 13.7 %collective-permute-start.8 = (bf16[768,256]{1,0:T(8,128)(2,1)S(1)}, bf16[768,256]{1,0:T(8,128)(2,1)}, u32[]{:S(2)}, u32[]{:S(2)}) collective-permute-start(bf16[768,256]{1,0:T(8,128)(2,1)S(1)} %get-tuple-element.44.refs_2_.refs_3_), channel_id=1, source_target_pairs={{0,12},{1,13},{2,6},{3,7},{4,0},{5,1},{6,10},{7,11},{8,4},{9,5},{1... | collective-permute-start | bytes 1179656 | tf_op jit(solution)/shard_map/ppermute | solution.py:243
  25.9 1.9 %collective-permute-start.7 = (bf16[432,256]{1,0:T(8,128)(2,1)S(1)}, bf16[432,256]{1,0:T(8,128)(2,1)S(1)}, u32[]{:S(2)}, u32[]{:S(2)}) collective-permute-start(bf16[432,256]{1,0:T(8,128)(2,1)S(1)} %slice.15), channel_id=1, source_target_pairs={{0,1},{1,0},{2,3},{3,2},{4,5},{5,4},{6,7},{7,6},{8,9},{9,8},{10,11... | collective-permute-start | bytes 663560 | tf_op jit(solution)/shard_map/ppermute | solution.py:243
  26.0 1.7 %collective-permute-start.6 = (bf16[384,256]{1,0:T(8,128)(2,1)S(1)}, bf16[384,256]{1,0:T(8,128)(2,1)S(1)}, u32[]{:S(2)}, u32[]{:S(2)}) collective-permute-start(bf16[384,256]{1,0:T(8,128)(2,1)S(1)} %slice.14), channel_id=1, source_target_pairs={{0,1},{1,0},{2,3},{3,2},{4,5},{5,4},{6,7},{7,6},{8,9},{9,8},{10,11... | collective-permute-start | bytes 589832 | tf_op jit(solution)/shard_map/ppermute | solution.py:243
  26.6 6.8 %collective-permute-start.12 = (bf16[384,256]{1,0:T(8,128)(2,1)S(1)}, bf16[384,256]{1,0:T(8,128)(2,1)S(1)}, u32[]{:S(2)}, u32[]{:S(2)}) collective-permute-start(bf16[384,256]{1,0:T(8,128)(2,1)S(1)} %get-tuple-element.56), channel_id=1, source_target_pairs={{0,1},{1,0},{2,3},{3,2},{4,5},{5,4},{6,7},{7,6},{8,9},{9,8},{10,11... | collective-permute-start | bytes 589832 | tf_op jit(solution)/shard_map/ppermute | solution.py:243
  26.7 8.4 %collective-permute-start.9 = (bf16[816,256]{1,0:T(8,128)(2,1)S(1)}, bf16[816,256]{1,0:T(8,128)(2,1)S(1)}, u32[]{:S(2)}, u32[]{:S(2)}) collective-permute-start(bf16[816,256]{1,0:T(8,128)(2,1)S(1)} %get-tuple-element.54.refs_1_), channel_id=1, source_target_pairs={{0,1},{1,0},{2,3},{3,2},{4,5},{5,4},{6,7},{7,6},{8,9},{9,8},{10,11... | collective-permute-start | bytes 1253384 | tf_op jit(solution)/shard_map/ppermute | solution.py:243
  27.8 13.7 %collective-permute-start.10 = (bf16[768,256]{1,0:T(8,128)(2,1)S(1)}, bf16[768,256]{1,0:T(8,128)(2,1)S(1)}, u32[]{:S(2)}, u32[]{:S(2)}) collective-permute-start(bf16[768,256]{1,0:T(8,128)(2,1)S(1)} %get-tuple-element.52), channel_id=1, source_target_pairs={{0,4},{1,5},{2,14},{3,15},{4,8},{5,9},{6,2},{7,3},{8,12},{9,13},{1... | collective-permute-start | bytes 1179656 | tf_op jit(solution)/shard_map/ppermute | solution.py:243
  33.3 5.0 %collective-permute-start.15 = (bf16[384,256]{1,0:T(8,128)(2,1)S(1)}, bf16[384,256]{1,0:T(8,128)(2,1)S(1)}, u32[]{:S(2)}, u32[]{:S(2)}) collective-permute-start(bf16[384,256]{1,0:T(8,128)(2,1)S(1)} %get-tuple-element.62), channel_id=1, source_target_pairs={{0,1},{1,0},{2,3},{3,2},{4,5},{5,4},{6,7},{7,6},{8,9},{9,8},{10,11... | collective-permute-start | bytes 589832 | tf_op jit(solution)/shard_map/ppermute | solution.py:243
  33.4 11.8 %collective-permute-start.13 = (bf16[384,256]{1,0:T(8,128)(2,1)S(1)}, bf16[384,256]{1,0:T(8,128)(2,1)S(1)}, u32[]{:S(2)}, u32[]{:S(2)}) collective-permute-start(bf16[384,256]{1,0:T(8,128)(2,1)S(1)} %add_convert_fusion.1), channel_id=1, source_target_pairs={{0,2},{1,3},{2,0},{3,1},{4,6},{5,7},{6,4},{7,5},{8,10},{9,11},{10,... | collective-permute-start | bytes 589832 | tf_op jit(solution)/shard_map/ppermute | solution.py:243
  35.1 14.2 %collective-permute-start.17 = (bf16[768,256]{1,0:T(8,128)(2,1)S(1)}, bf16[768,256]{1,0:T(8,128)(2,1)S(1)}, u32[]{:S(2)}, u32[]{:S(2)}) collective-permute-start(bf16[768,256]{1,0:T(8,128)(2,1)S(1)} %get-tuple-element.66), channel_id=1, source_target_pairs={{0,4},{1,5},{2,14},{3,15},{4,8},{5,9},{6,2},{7,3},{8,12},{9,13},{1... | collective-permute-start | bytes 1179656 | tf_op jit(solution)/shard_map/ppermute | solution.py:243
  36.5 8.8 %collective-permute-start.14 = (bf16[384,256]{1,0:T(8,128)(2,1)S(1)}, bf16[384,256]{1,0:T(8,128)(2,1)S(1)}, u32[]{:S(2)}, u32[]{:S(2)}) collective-permute-start(bf16[384,256]{1,0:T(8,128)(2,1)S(1)} %get-tuple-element.61), channel_id=1, source_target_pairs={{0,1},{1,0},{2,3},{3,2},{4,5},{5,4},{6,7},{7,6},{8,9},{9,8},{10,11... | collective-permute-start | bytes 589832 | tf_op jit(solution)/shard_map/ppermute | solution.py:243
  38.3 6.9 %collective-permute-start.11 = (bf16[384,256]{1,0:T(8,128)(2,1)S(1)}, bf16[384,256]{1,0:T(8,128)(2,1)S(1)}, u32[]{:S(2)}, u32[]{:S(2)}) collective-permute-start(bf16[384,256]{1,0:T(8,128)(2,1)S(1)} %get-tuple-element.51), channel_id=1, source_target_pairs={{0,1},{1,0},{2,3},{3,2},{4,5},{5,4},{6,7},{7,6},{8,9},{9,8},{10,11... | collective-permute-start | bytes 589832 | tf_op jit(solution)/shard_map/ppermute | solution.py:243
  41.5 6.1 %collective-permute-start.16 = (bf16[384,256]{1,0:T(8,128)(2,1)S(1)}, bf16[384,256]{1,0:T(8,128)(2,1)S(1)}, u32[]{:S(2)}, u32[]{:S(2)}) collective-permute-start(bf16[384,256]{1,0:T(8,128)(2,1)S(1)} %add_convert_fusion), channel_id=1, source_target_pairs={{0,2},{1,3},{2,0},{3,1},{4,6},{5,7},{6,4},{7,5},{8,10},{9,11},{10,... | collective-permute-start | bytes 589832 | tf_op jit(solution)/shard_map/ppermute | solution.py:243

commit v6 on v5

--- a/solution.py
+++ b/solution.py
@@ -34,7 +34,7 @@
     return jnp.concatenate(parts, axis=0)
 
 
-def params(mib=24):
+def params(mib=16):
     return pltpu.CompilerParams(vmem_limit_bytes=mib * 1024 * 1024)
 
 
@@ -59,41 +59,41 @@
     return -(-2 * PARTS * heads // 16) * 16
 
 
-def pack_kernel(chunks, head_dim, q_hbm, do_hbm, o_hbm, lse_hbm, k_hbm, v_hbm, *rest):
-    count = len(chunks)
-    x_refs, kv_refs = rest[:count], rest[count : 2 * count]
-    q_ref, do_ref, o_ref, lse_ref, k_ref, v_ref, sems = rest[2 * count :]
-    sources = (q_hbm, do_hbm, o_hbm, lse_hbm, k_hbm, v_hbm)
-    targets = (q_ref, do_ref, o_ref, lse_ref, k_ref, v_ref)
+def fetch(sources, targets, sems):
     copies = [
         pltpu.make_async_copy(source, target, sems.at[i])
         for i, (source, target) in enumerate(zip(sources, targets))
     ]
     for copy in copies:
         copy.start()
-    for copy in copies[:4]:
+    for copy in copies:
         copy.wait()
-    lse = lse_ref[...] * LOG2E
-    first = 0
-    for heads, out_ref in zip(chunks, x_refs):
-        rows = heads * head_dim
-        span = slice(first * head_dim, first * head_dim + rows)
-        do_t = do_ref[:, span].T
-        out_ref[:rows] = q_ref[:, span].T
-        out_ref[rows : 2 * rows] = do_t
-        product = do_t.astype(F32) * o_ref[:, span].T.astype(F32)
-        delta = [
-            jnp.sum(product[h * head_dim : (h + 1) * head_dim], axis=0, keepdims=True)
-            for h in range(heads)
-        ]
-        pieces = split_parts(join([lse[first : first + heads]] + delta))
-        pad = extra_rows(heads) - 2 * PARTS * heads
-        if pad:
-            pieces.append(jnp.zeros((pad, lse.shape[1]), BF16))
-        out_ref[2 * rows :] = join([piece.astype(F32) for piece in pieces]).astype(BF16)
-        first += heads
-    for copy in copies[4:]:
-        copy.wait()
+
+
+def pack_queries(first, heads, head_dim, q_hbm, do_hbm, o_hbm, lse_hbm, *rest):
+    out_ref, q_ref, do_ref, o_ref, lse_ref, sems = rest[-6:]
+    rows = heads * head_dim
+    span = pl.ds(first * head_dim, rows)
+    sources = [ref.at[:, span] for ref in (q_hbm, do_hbm, o_hbm)] + [lse_hbm]
+    fetch(sources, (q_ref, do_ref, o_ref, lse_ref), sems)
+    do_t = do_ref[...].T
+    out_ref[:rows] = q_ref[...].T
+    out_ref[rows : 2 * rows] = do_t
+    product = do_t.astype(F32) * o_ref[...].T.astype(F32)
+    delta = [
+        jnp.sum(product[h * head_dim : (h + 1) * head_dim], axis=0, keepdims=True)
+        for h in range(heads)
+    ]
+    pieces = split_parts(join([lse_ref[first : first + heads] * LOG2E] + delta))
+    pad = extra_rows(heads) - 2 * PARTS * heads
+    if pad:
+        pieces.append(jnp.zeros((pad, out_ref.shape[1]), BF16))
+    out_ref[2 * rows :] = join([piece.astype(F32) for piece in pieces]).astype(BF16)
+
+
+def pack_keys(chunks, head_dim, k_hbm, v_hbm, token_ref, *rest):
+    kv_refs, (k_ref, v_ref, sems) = rest[: len(chunks)], rest[len(chunks) :]
+    fetch((k_hbm, v_hbm), (k_ref, v_ref), sems)
     first = 0
     for heads, out_ref in zip(chunks, kv_refs):
         rows = heads * head_dim
@@ -154,6 +154,13 @@
     return inside & (value > 0)
 
 
+def split_kernel(x_ref, *out_refs):
+    first = 0
+    for out_ref in out_refs:
+        out_ref[...] = x_ref[first : first + out_ref.shape[0]]
+        first += out_ref.shape[0]
+
+
 def partner_of(place):
     return place + 1 - 2 * lax.rem(place, 2)
 
@@ -214,20 +221,21 @@
     dkv_ref[...] = acc_ref[...].astype(dkv_ref.dtype)
 
 
-def finish_kernel(chunks, head_dim, scale, *refs):
-    ins, outs = refs[:-3], refs[-3:]
-    groups = [ins[i * 7 : (i + 1) * 7] for i in range(len(chunks))]
-    dq_all, dk_all, dv_all = [], [], []
-    for heads, group in zip(chunks, groups):
-        dq_own, dq_core, dq_far, dkv_own, dkv_core, dkv_far, zdkv = group
-        rows = heads * head_dim
-        dq = dq_own[...] + dq_core[...].astype(F32) + dq_far[...].astype(F32)
-        total = dkv_own[...] + dkv_core[...] + dkv_far[...] + zdkv[...].astype(F32)
-        dq_all.append((dq * scale).astype(BF16))
-        dk_all.append((total[:rows] * scale).astype(BF16))
-        dv_all.append(total[rows:].astype(BF16))
-    for parts, ref in zip((dq_all, dk_all, dv_all), outs):
-        ref[...] = join(parts).T
+def finish_kernel(first, heads, head_dim, scale, *refs):
+    dq_own, dq_core, dq_far, dkv_own, dkv_core, dkv_far, zdkv = refs[:7]
+    outs, held, sems = refs[-7:-4], refs[-4:-1], refs[-1]
+    rows = heads * head_dim
+    dq = dq_own[...] + dq_core[...].astype(F32) + dq_far[...].astype(F32)
+    total = dkv_own[...] + dkv_core[...] + dkv_far[...] + zdkv[...].astype(F32)
+    values = (dq * scale, total[:rows] * scale, total[rows:])
+    copies = []
+    for i, (value, ref, out) in enumerate(zip(values, held, outs)):
+        ref[...] = value.astype(BF16).T
+        span = pl.ds(first * head_dim, rows)
+        copies.append(pltpu.make_async_copy(ref, out.at[:, span], sems.at[i]))
+        copies[-1].start()
+    for copy in copies:
+        copy.wait()
 
 
 def per_device(query_rows, key_rows, value_rows, out_rows, grad_out, normalizer, keep_tasks):
@@ -252,24 +260,32 @@
         return jax.ShapeDtypeStruct((rows, tokens), dtype)
 
     x_rows = [2 * h * head_dim + extra_rows(h) for h in chunks]
-    packed = pl.pallas_call(
-        functools.partial(pack_kernel, chunks, head_dim),
-        out_shape=[shape(n, BF16) for n in x_rows] + [shape(2 * h * head_dim, BF16) for h in chunks],
-        in_specs=[pl.BlockSpec(memory_space=pltpu.HBM)] * 6,
-        out_specs=[VMEM] * (2 * len(chunks)),
-        scratch_shapes=[pltpu.VMEM((tokens, width), BF16)] * 3
-        + [pltpu.VMEM((HEADS, tokens), F32)]
-        + [pltpu.VMEM((tokens, width), BF16)] * 2
-        + [pltpu.SemaphoreType.DMA((6,))],
+    hbm = pl.BlockSpec(memory_space=pltpu.HBM)
+    fixed = lambda *values: [pltpu.with_memory_space_constraint(v, pltpu.HBM) for v in values]
+    x_own = []
+    for c, heads in enumerate(chunks):
+        rows = heads * head_dim
+        x_own.append(
+            pl.pallas_call(
+                functools.partial(pack_queries, sum(chunks[:c]), heads, head_dim),
+                out_shape=shape(x_rows[c], BF16),
+                in_specs=[hbm] * 4 + [pl.BlockSpec(memory_space=pl.ANY)] * c,
+                out_specs=VMEM,
+                scratch_shapes=[pltpu.VMEM((tokens, rows), BF16)] * 3
+                + [pltpu.VMEM((HEADS, tokens), F32), pltpu.SemaphoreType.DMA((4,))],
+                compiler_params=params(),
+                name="pack_queries",
+            )(*fixed(query_rows, grad_out, out_rows, normalizer), *x_own)
+        )
+    kv_own = pl.pallas_call(
+        functools.partial(pack_keys, chunks, head_dim),
+        out_shape=[shape(2 * h * head_dim, BF16) for h in chunks],
+        in_specs=[hbm] * 2 + [pl.BlockSpec(memory_space=pl.ANY)],
+        out_specs=[VMEM] * len(chunks),
+        scratch_shapes=[pltpu.VMEM((tokens, width), BF16)] * 2 + [pltpu.SemaphoreType.DMA((2,))],
         compiler_params=params(),
-        name="pack",
-    )(
-        *[
-            pltpu.with_memory_space_constraint(value, pltpu.HBM)
-            for value in (query_rows, grad_out, out_rows, normalizer, key_rows, value_rows)
-        ]
-    )
-    x_own, kv_own = packed[: len(chunks)], packed[len(chunks) :]
+        name="pack_keys",
+    )(*fixed(key_rows, value_rows), x_own[-1])
     x_far = [send(x, across) for x in x_own]
     kv_level = [send(kv, level_in) for kv in kv_own]
     x_core = [send(x, core) for x in x_own]
@@ -311,9 +327,18 @@
     far_out = []
     for c in range(len(chunks)):
         x = after(x_far[c], done)
-        cuts = [2 * chunks[c] * i // HOPS * head_dim for i in range(HOPS)] + [x.shape[0]]
-        cuts = [-(-cut // head_dim) * head_dim for cut in cuts]
-        hop = [send(x[i:j], core) for i, j in zip(cuts, cuts[1:])]
+        hop = [send(piece, core) for piece in pl.pallas_call(
+            split_kernel,
+            out_shape=[
+                pltpu.VMEM((chunks[c] * head_dim, tokens), BF16),
+                pltpu.VMEM((x.shape[0] - chunks[c] * head_dim, tokens), BF16),
+            ],
+            in_specs=[VMEM],
+            out_specs=[VMEM] * HOPS,
+            compiler_params=params(),
+            cost_estimate=cost(1024, 1024),
+            name="split",
+        )(x)]
         dq_x, dq_c, dkv_far = far(c, False, x, hop, kv_own[c], ())
         z = after(kv_level[c], dq_x)
         dq_x, dq_c, zdkv = far(c, True, x, hop, z, (dq_x, dq_c))
@@ -323,27 +348,24 @@
     dq_core, dkv_core = near(True, [after(value, done) for value in x_core], BF16, CORE_COST)
     done = dq_core[0]
     dq_own, dkv_own = near(False, [after(x, done, far_out[0][2]) for x in x_own], F32, SELF_COST)
-    finish_args = []
-    for c in range(len(chunks)):
+    out = ()
+    any_space = pl.BlockSpec(memory_space=pl.ANY)
+    for c, heads in enumerate(chunks):
+        rows = heads * head_dim
         dq_far, dkv_far, zdkv = far_out[c]
-        finish_args += [
-            dq_own[c],
-            send(dq_core[c], core),
-            dq_far,
-            dkv_own[c],
-            dkv_core[c],
-            dkv_far,
-            zdkv,
-        ]
-    grad_query, grad_key, grad_value = pl.pallas_call(
-        functools.partial(finish_kernel, chunks, head_dim, scale),
-        out_shape=[jax.ShapeDtypeStruct((tokens, width), BF16)] * 3,
-        in_specs=[VMEM] * len(finish_args),
-        out_specs=[VMEM] * 3,
-        compiler_params=params(),
-        name="finish",
-    )(*finish_args)
-    return grad_query, grad_key, grad_value
+        args = (dq_own[c], send(dq_core[c], core), dq_far, dkv_own[c], dkv_core[c], dkv_far, zdkv)
+        out = pl.pallas_call(
+            functools.partial(finish_kernel, sum(chunks[:c]), heads, head_dim, scale),
+            out_shape=[jax.ShapeDtypeStruct((tokens, width), BF16)] * 3,
+            in_specs=[VMEM] * 7 + [any_space] * len(out),
+            out_specs=[any_space] * 3,
+            scratch_shapes=[pltpu.VMEM((tokens, rows), BF16)] * 3 + [pltpu.SemaphoreType.DMA((3,))],
+            input_output_aliases={7 + i: i for i in range(len(out))},
+            compiler_params=params(),
+            cost_estimate=cost(1024, 1024),
+            name="finish",
+        )(*args, *out)
+    return tuple(out)
 
 
 def solution(mesh):

time: 50.3 us -> 51.2 us (1.018); the launches traced: 50.7 us -> 51 us
  Pallas kernels: 15.6 us -> 23.5 us
  starting transfers between devices: 18.1 us -> 14 us
  waiting for transfers between devices: 15.3 us -> 12.3 us
  local copies, waits for them, and re-layouts: 0.82 us -> 0.09 us
    ppermute x18, starting transfers between devices: 18.1 us -> 14 us  [send(): return lax.ppermute(value, 'tok', [(a, b % count) for a, b in pairs])]
    pallas_call x2 -> x7, Pallas kernels: 3.41 us -> 7.05 us  [the longest x2 2.77 us: per_device(): pl.pallas_call(functools.partial(pack_queries, sum(chunks[:c]), heads, he...]
    ppermute x18, waiting for transfers between devices: 15.3 us -> 12.3 us  [send(): return lax.ppermute(value, 'tok', [(a, b % count) for a, b in pairs])]
    pallas_call x4, Pallas kernels: 8.49 us -> 10.8 us  [far(): pl.pallas_call(functools.partial(far_kernel, chunks[c], head_dim, factor,...]
    pallas_call x2, Pallas kernels: 3.75 us -> 5.72 us  [near(): pl.pallas_call(functools.partial(near_kernel, chunks, head_dim, factor, c...]
    slice x4 -> x0, local copies, waits for them, and re-layouts: 0.74 us -> none  [per_device(): hop = [send(x[i:j], core) for i, j in zip(cuts, cuts[1:])]]
  transfers between devices with their start and end apart: 18 -> 18, of which waited for: 6 -> 5; matrix products, arithmetic and copies ran while one was open for 2% -> 0% of each run, Pallas kernels for 24% -> 41%
where the time goes in v6:
time: 51.2 us; the launch traced here: 51 us
  Pallas kernels  23.5 us (46%)
  starting transfers between devices  14 us (27%)
  waiting for transfers between devices  12.3 us (24%)
  between operations  0.96 us (2%)
    ppermute x18, starting transfers between devices, send(): return lax.ppermute(value, 'tok', [(a, b % count) for a, b in pairs])  14 us
    ppermute x18, waiting for transfers between devices, send(): return lax.ppermute(value, 'tok', [(a, b % count) for a, b in pairs])  12.3 us
    pallas_call x4, Pallas kernels, far(): pl.pallas_call(functools.partial(far_kernel, chunks[c], head_dim, factor,...  10.8 us
    pallas_call x2, Pallas kernels, near(): pl.pallas_call(functools.partial(near_kernel, chunks, head_dim, factor, c...  5.72 us
    pallas_call x2, Pallas kernels, per_device(): pl.pallas_call(functools.partial(pack_queries, sum(chunks[:c]), heads, he...  2.77 us
    pallas_call x2, Pallas kernels, per_device(): pl.pallas_call(functools.partial(finish_kernel, sum(chunks[:c]), heads, h...  2.16 us
    pallas_call x1, Pallas kernels, per_device(): pl.pallas_call(functools.partial(pack_keys, chunks, head_dim), out_shape=...  1.39 us
  transfers between devices with their start and end apart: 18, of which 5 were waited for; matrix products, arithmetic and copies ran while one was open for 0% of the time, Pallas kernels for 41%

profile of v6, /device:TPU:0, one launch (start us, length us, event | category | flops | bytes accessed | tf_op | source)
XLA Modules:
  0.0 51.0 jit_solution(16671808667181366003)
XLA Ops:
  0.6 1.4 %pack_queries.2.rest_0_.refs_0_ = bf16[816,256]{1,0:T(8,128)(2,1)S(1)} custom-call(bf16[256,768]{1,0:T(8,128)(2,1)} %q_hbm.3, bf16[256,768]{1,0:T(8,128)(2,1)} %do_hbm.3, bf16[256,768]{1,0:T(8,128)(2,1)} %o_hbm.3, f32[16,256]{1,0:T(8,128)} %lse_hbm.3), custom_call_target="tpu_custom_call" | custom-call | tf_op jit(solution)/shard_map/pack_queries/pallas_call | solution.py:269
  2.0 3.0 %collective-permute-start.2 = (bf16[816,256]{1,0:T(8,128)(2,1)S(1)}, bf16[816,256]{1,0:T(8,128)(2,1)S(1)}, u32[]{:S(2)}, u32[]{:S(2)}) collective-permute-start(bf16[816,256]{1,0:T(8,128)(2,1)S(1)} %pack_queries.2.rest_0_.refs_0_), channel_id=1, source_target_pairs={{0,2},{1,3},{2,0},{3,1},{4,6},{5,7},{6,4},{7,5},{8,10},{9,11},{10,... | collective-permute-start | bytes 1253384 | tf_op jit(solution)/shard_map/ppermute | solution.py:251
  5.0 1.4 %pack_queries.3.token_ref.refs_1_ = bf16[816,256]{1,0:T(8,128)(2,1)S(1)} custom-call(bf16[256,768]{1,0:T(8,128)(2,1)} %q_hbm.3, bf16[256,768]{1,0:T(8,128)(2,1)} %do_hbm.3, bf16[256,768]{1,0:T(8,128)(2,1)} %o_hbm.3, f32[16,256]{1,0:T(8,128)} %lse_hbm.3, bf16[816,256]{1,0:T(8,128)(2,1)S(1)} %pack_queries.2.rest_0_.refs_0_), custom_call_target="tpu_custom_call" | custom-call | tf_op jit(solution)/shard_map/pack_queries/pallas_call | solution.py:269
  6.6 1.4 %pack_keys.1 = (bf16[768,256]{1,0:T(8,128)(2,1)S(1)}, bf16[768,256]{1,0:T(8,128)(2,1)S(1)}) custom-call(bf16[256,768]{1,0:T(8,128)(2,1)} %k_hbm.1, bf16[256,768]{1,0:T(8,128)(2,1)} %v_hbm.1, bf16[816,256]{1,0:T(8,128)(2,1)S(1)} %pack_queries.3.token_ref.refs_1_), custom_call_target="tpu_custom_call" | custom-call | tf_op jit(solution)/shard_map/pack_keys/pallas_call | solution.py:280
  8.0 4.1 %collective-permute-start.5 = (bf16[768,256]{1,0:T(8,128)(2,1)S(1)}, bf16[768,256]{1,0:T(8,128)(2,1)}, u32[]{:S(2)}, u32[]{:S(2)}) collective-permute-start(bf16[768,256]{1,0:T(8,128)(2,1)S(1)} %get-tuple-element.43.refs_2_), channel_id=1, source_target_pairs={{0,12},{1,13},{2,6},{3,7},{4,0},{5,1},{6,10},{7,11},{8,4},{9,5},{1... | collective-permute-start | bytes 1179656 | tf_op jit(solution)/shard_map/ppermute | solution.py:251
  12.1 3.4 %collective-permute-done.2.x_ref = bf16[816,256]{1,0:T(8,128)(2,1)S(1)} collective-permute-done((bf16[816,256]{1,0:T(8,128)(2,1)S(1)}, bf16[816,256]{1,0:T(8,128)(2,1)S(1)}, u32[]{:S(2)}, u32[]{:S(2)}) %collective-permute-start.2) | collective-permute-done | bytes 417824 | tf_op jit(solution)/shard_map/ppermute | solution.py:251
  15.5 0.7 %split.2 = (bf16[384,256]{1,0:T(8,128)(2,1)}, bf16[432,256]{1,0:T(8,128)(2,1)S(1)}) custom-call(bf16[816,256]{1,0:T(8,128)(2,1)S(1)} %collective-permute-done.2.x_ref), custom_call_target="tpu_custom_call" | custom-call | flops 1024 | bytes 1024 | tf_op jit(solution)/shard_map/split/pallas_call | solution.py:330
  16.2 0.5 collective-permute-start.3
  16.7 4.2 %collective-permute-start.8 = (bf16[768,256]{1,0:T(8,128)(2,1)S(1)}, bf16[768,256]{1,0:T(8,128)(2,1)}, u32[]{:S(2)}, u32[]{:S(2)}) collective-permute-start(bf16[768,256]{1,0:T(8,128)(2,1)S(1)} %get-tuple-element.51.refs_2_.refs_3_), channel_id=1, source_target_pairs={{0,12},{1,13},{2,6},{3,7},{4,0},{5,1},{6,10},{7,11},{8,4},{9,5},{1... | collective-permute-start | bytes 1179656 | tf_op jit(solution)/shard_map/ppermute | solution.py:251
  21.0 2.0 %far_tasks.4 = (f32[384,256]{1,0:T(8,128)S(1)}, f32[384,256]{1,0:T(8,128)S(1)}, f32[768,256]{1,0:T(8,128)S(1)}) custom-call(s32[16,5]{1,0:T(8,128)S(1)} %copy.18.keep_ref, s32[1]{0:T(128)} %bitcast.place_ref, bf16[816,256]{1,0:T(8,128)(2,1)S(1)} %collective-permute-done.2.x_ref, bf16[384,256]{1,0:T(8,128)(2,1)S(1)} %collective-permute-done.3.refs_0_, ...), custom_call_target="tpu_custom_call" | custom-call | flops 13421772 | bytes 1024 | tf_op jit(solution)/shard_map/far_tasks/pallas_call | solution.py:315
  23.0 3.4 %far_tasks.5 = (bf16[384,256]{1,0:T(8,128)(2,1)S(1)}, bf16[384,256]{1,0:T(8,128)(2,1)S(1)}, bf16[768,256]{1,0:T(8,128)(2,1)S(1)}) custom-call(s32[16,5]{1,0:T(8,128)S(1)} %copy.18.keep_ref, s32[1]{0:T(128)} %bitcast.place_ref, bf16[816,256]{1,0:T(8,128)(2,1)S(1)} %collective-permute-done.2.x_ref, bf16[384,256]{1,0:T(8,128)(2,1)S(1)} %collective-permute-done.3.refs_0_, ...), custom_call_target="tpu_custom_call" | custom-call | flops 13421772 | bytes 1024 | tf_op jit(solution)/shard_map/far_tasks/pallas_call | solution.py:315
  26.6 0.5 collective-permute-start.6
  27.1 0.4 collective-permute-start.9
  27.6 0.7 %collective-permute-done.6.refs_0_ = bf16[384,256]{1,0:T(8,128)(2,1)S(1)} collective-permute-done((bf16[384,256]{1,0:T(8,128)(2,1)S(1)}, bf16[384,256]{1,0:T(8,128)(2,1)S(1)}, u32[]{:S(2)}, u32[]{:S(2)}) %collective-permute-start.6) | collective-permute-done | bytes 196640 | tf_op jit(solution)/shard_map/ppermute | solution.py:251
  28.3 1.9 %far_tasks.6 = (f32[384,256]{1,0:T(8,128)S(1)}, f32[384,256]{1,0:T(8,128)S(1)}, f32[768,256]{1,0:T(8,128)S(1)}) custom-call(s32[16,5]{1,0:T(8,128)S(1)} %copy.18.keep_ref, s32[1]{0:T(128)} %bitcast.place_ref, bf16[816,256]{1,0:T(8,128)(2,1)S(1)} %collective-permute-done.1.x_ref, bf16[384,256]{1,0:T(8,128)(2,1)S(1)} %collective-permute-done.6.refs_0_, ...), custom_call_target="tpu_custom_call" | custom-call | flops 13421772 | bytes 1024 | tf_op jit(solution)/shard_map/far_tasks/pallas_call | solution.py:315
  30.3 3.4 %far_tasks.7 = (bf16[384,256]{1,0:T(8,128)(2,1)S(1)}, bf16[384,256]{1,0:T(8,128)(2,1)S(1)}, bf16[768,256]{1,0:T(8,128)(2,1)S(1)}) custom-call(s32[16,5]{1,0:T(8,128)S(1)} %copy.18.keep_ref, s32[1]{0:T(128)} %bitcast.place_ref, bf16[816,256]{1,0:T(8,128)(2,1)S(1)} %collective-permute-done.1.x_ref, bf16[384,256]{1,0:T(8,128)(2,1)S(1)} %collective-permute-done.6.refs_0_, ...), custom_call_target="tpu_custom_call" | custom-call | flops 13421772 | bytes 1024 | tf_op jit(solution)/shard_map/far_tasks/pallas_call | solution.py:315
  34.2 3.0 %near_tasks.2 = (bf16[384,256]{1,0:T(8,128)(2,1)S(1)}, f32[768,256]{1,0:T(8,128)S(1)}, bf16[384,256]{1,0:T(8,128)(2,1)S(1)}, f32[768,256]{1,0:T(8,128)S(1)}) custom-call(s32[16,5]{1,0:T(8,128)S(1)} %copy.18.keep_ref, s32[1]{0:T(128)} %bitcast.place_ref, bf16[816,256]{1,0:T(8,128)(2,1)S(1)} %collective-permute-done.refs_0_, ...), custom_call_target="tpu_custom_call" | custom-call | flops 26843544 | bytes 1024 | tf_op jit(solution)/shard_map/near_tasks/pallas_call | solution.py:301
  37.1 0.4 collective-permute-start.11
  37.8 4.3 %collective-permute-done.10.refs_6_ = bf16[768,256]{1,0:T(8,128)(2,1)S(1)} collective-permute-done((bf16[768,256]{1,0:T(8,128)(2,1)S(1)}, bf16[768,256]{1,0:T(8,128)(2,1)S(1)}, u32[]{:S(2)}, u32[]{:S(2)}) %collective-permute-start.10) | collective-permute-done | bytes 393248 | tf_op jit(solution)/shard_map/ppermute | solution.py:251
  42.1 2.8 %near_tasks.3 = (f32[384,256]{1,0:T(8,128)S(1)}, f32[768,256]{1,0:T(8,128)S(1)}, f32[384,256]{1,0:T(8,128)S(1)}, f32[768,256]{1,0:T(8,128)S(1)}) custom-call(s32[16,5]{1,0:T(8,128)S(1)} %copy.18.keep_ref, s32[1]{0:T(128)} %bitcast.place_ref, bf16[816,256]{1,0:T(8,128)(2,1)S(1)} %pack_queries.2.rest_0_.refs_0_, ...), custom_call_target="tpu_custom_call" | custom-call | flops 26843544 | bytes 1024 | tf_op jit(solution)/shard_map/near_tasks/pallas_call | solution.py:301
  44.8 1.1 %finish.2 = (bf16[256,768]{1,0:T(8,128)(2,1)}, bf16[256,768]{1,0:T(8,128)(2,1)}, bf16[256,768]{1,0:T(8,128)(2,1)}) custom-call(f32[384,256]{1,0:T(8,128)S(1)} %get-tuple-element.69.refs_0_, bf16[384,256]{1,0:T(8,128)(2,1)S(1)} %collective-permute-done.15.refs_1_, bf16[384,256]{1,0:T(8,128)(2,1)S(1)} %collective-permute-done.17.refs_2_, ...), custom_call_target="tpu_custom_call" | custom-call | flops 1024 | bytes 1024 | tf_op jit(solution)/shard_map/finish/pallas_call | solution.py:357
  46.0 1.8 %collective-permute-done.13.refs_2_ = bf16[384,256]{1,0:T(8,128)(2,1)S(1)} collective-permute-done((bf16[384,256]{1,0:T(8,128)(2,1)S(1)}, bf16[384,256]{1,0:T(8,128)(2,1)S(1)}, u32[]{:S(2)}, u32[]{:S(2)}) %collective-permute-start.13) | collective-permute-done | bytes 196640 | tf_op jit(solution)/shard_map/ppermute | solution.py:251
  47.7 2.0 %collective-permute-done.14.refs_6_ = bf16[768,256]{1,0:T(8,128)(2,1)S(1)} collective-permute-done((bf16[768,256]{1,0:T(8,128)(2,1)S(1)}, bf16[768,256]{1,0:T(8,128)(2,1)S(1)}, u32[]{:S(2)}, u32[]{:S(2)}) %collective-permute-start.14) | collective-permute-done | bytes 393248 | tf_op jit(solution)/shard_map/ppermute | solution.py:251
  49.7 1.1 %finish.3 = (bf16[256,768]{1,0:T(8,128)(2,1)}, bf16[256,768]{1,0:T(8,128)(2,1)}, bf16[256,768]{1,0:T(8,128)(2,1)}) custom-call(f32[384,256]{1,0:T(8,128)S(1)} %get-tuple-element.62.refs_0_, bf16[384,256]{1,0:T(8,128)(2,1)S(1)} %collective-permute-done.11.refs_1_, ...), custom_call_target="tpu_custom_call", output_to_operand_aliasing={{0}: (7, {}), {1}: (8, {}), {2}: (9, {})} | custom-call | flops 1024 | bytes 1024 | tf_op jit(solution)/shard_map/finish/pallas_call | solution.py:357
  (30 shorter events, 1.2 us)
Async XLA Ops:
  2.0 13.5 %collective-permute-start.2 = (bf16[816,256]{1,0:T(8,128)(2,1)S(1)}, bf16[816,256]{1,0:T(8,128)(2,1)S(1)}, u32[]{:S(2)}, u32[]{:S(2)}) collective-permute-start(bf16[816,256]{1,0:T(8,128)(2,1)S(1)} %pack_queries.2.rest_0_.refs_0_), channel_id=1, source_target_pairs={{0,2},{1,3},{2,0},{3,1},{4,6},{5,7},{6,4},{7,5},{8,10},{9,11},{10,... | collective-permute-start | bytes 1253384 | tf_op jit(solution)/shard_map/ppermute | solution.py:251
  5.0 10.5 %collective-permute-start = (bf16[816,256]{1,0:T(8,128)(2,1)S(1)}, bf16[816,256]{1,0:T(8,128)(2,1)S(1)}, u32[]{:S(2)}, u32[]{:S(2)}) collective-permute-start(bf16[816,256]{1,0:T(8,128)(2,1)S(1)} %pack_queries.2.rest_0_.refs_0_), channel_id=1, source_target_pairs={{0,1},{1,0},{2,3},{3,2},{4,5},{5,4},{6,7},{7,6},{8,9},{9,8},{10,11... | collective-permute-start | bytes 1253384 | tf_op jit(solution)/shard_map/ppermute | solution.py:251
  6.4 20.0 %collective-permute-start.1 = (bf16[816,256]{1,0:T(8,128)(2,1)S(1)}, bf16[816,256]{1,0:T(8,128)(2,1)S(1)}, u32[]{:S(2)}, u32[]{:S(2)}) collective-permute-start(bf16[816,256]{1,0:T(8,128)(2,1)S(1)} %pack_queries.3.token_ref.refs_1_), channel_id=1, source_target_pairs={{0,2},{1,3},{2,0},{3,1},{4,6},{5,7},{6,4},{7,5},{8,10},{9,11},{10,... | collective-permute-start | bytes 1253384 | tf_op jit(solution)/shard_map/ppermute | solution.py:251
  8.0 15.0 %collective-permute-start.5 = (bf16[768,256]{1,0:T(8,128)(2,1)S(1)}, bf16[768,256]{1,0:T(8,128)(2,1)}, u32[]{:S(2)}, u32[]{:S(2)}) collective-permute-start(bf16[768,256]{1,0:T(8,128)(2,1)S(1)} %get-tuple-element.43.refs_2_), channel_id=1, source_target_pairs={{0,12},{1,13},{2,6},{3,7},{4,0},{5,1},{6,10},{7,11},{8,4},{9,5},{1... | collective-permute-start | bytes 1179656 | tf_op jit(solution)/shard_map/ppermute | solution.py:251
  16.2 4.8 %collective-permute-start.4 = (bf16[432,256]{1,0:T(8,128)(2,1)S(1)}, bf16[432,256]{1,0:T(8,128)(2,1)S(1)}, u32[]{:S(2)}, u32[]{:S(2)}) collective-permute-start(bf16[432,256]{1,0:T(8,128)(2,1)S(1)} %get-tuple-element.42), channel_id=1, source_target_pairs={{0,1},{1,0},{2,3},{3,2},{4,5},{5,4},{6,7},{7,6},{8,9},{9,8},{10,11... | collective-permute-start | bytes 663560 | tf_op jit(solution)/shard_map/ppermute | solution.py:251
  16.2 4.7 %copy-start = (s32[16,5]{0,1:T(8,128)S(1)}, s32[16,5]{0,1:T(8,128)}, u32[]{:S(2)}) copy-start(s32[16,5]{0,1:T(8,128)} %param.13) | copy-start | bytes 964
  16.2 4.8 %collective-permute-start.3 = (bf16[384,256]{1,0:T(8,128)(2,1)}, bf16[384,256]{1,0:T(8,128)(2,1)S(1)}, u32[]{:S(2)}, u32[]{:S(2)}) collective-permute-start(bf16[384,256]{1,0:T(8,128)(2,1)} %get-tuple-element.41), channel_id=1, source_target_pairs={{0,1},{1,0},{2,3},{3,2},{4,5},{5,4},{6,7},{7,6},{8,9},{9,8},{10,11... | collective-permute-start | bytes 589832 | tf_op jit(solution)/shard_map/ppermute | solution.py:251
  16.7 13.5 %collective-permute-start.8 = (bf16[768,256]{1,0:T(8,128)(2,1)S(1)}, bf16[768,256]{1,0:T(8,128)(2,1)}, u32[]{:S(2)}, u32[]{:S(2)}) collective-permute-start(bf16[768,256]{1,0:T(8,128)(2,1)S(1)} %get-tuple-element.51.refs_2_.refs_3_), channel_id=1, source_target_pairs={{0,12},{1,13},{2,6},{3,7},{4,0},{5,1},{6,10},{7,11},{8,4},{9,5},{1... | collective-permute-start | bytes 1179656 | tf_op jit(solution)/shard_map/ppermute | solution.py:251
  26.5 1.8 %collective-permute-start.7 = (bf16[432,256]{1,0:T(8,128)(2,1)S(1)}, bf16[432,256]{1,0:T(8,128)(2,1)S(1)}, u32[]{:S(2)}, u32[]{:S(2)}) collective-permute-start(bf16[432,256]{1,0:T(8,128)(2,1)S(1)} %get-tuple-element.50), channel_id=1, source_target_pairs={{0,1},{1,0},{2,3},{3,2},{4,5},{5,4},{6,7},{7,6},{8,9},{9,8},{10,11... | collective-permute-start | bytes 663560 | tf_op jit(solution)/shard_map/ppermute | solution.py:251
  26.6 1.7 %collective-permute-start.6 = (bf16[384,256]{1,0:T(8,128)(2,1)S(1)}, bf16[384,256]{1,0:T(8,128)(2,1)S(1)}, u32[]{:S(2)}, u32[]{:S(2)}) collective-permute-start(bf16[384,256]{1,0:T(8,128)(2,1)S(1)} %get-tuple-element.49), channel_id=1, source_target_pairs={{0,1},{1,0},{2,3},{3,2},{4,5},{5,4},{6,7},{7,6},{8,9},{9,8},{10,11... | collective-permute-start | bytes 589832 | tf_op jit(solution)/shard_map/ppermute | solution.py:251
  27.1 6.9 %collective-permute-start.16 = (bf16[384,256]{1,0:T(8,128)(2,1)S(1)}, bf16[384,256]{1,0:T(8,128)(2,1)S(1)}, u32[]{:S(2)}, u32[]{:S(2)}) collective-permute-start(bf16[384,256]{1,0:T(8,128)(2,1)S(1)} %get-tuple-element.70), channel_id=1, source_target_pairs={{0,1},{1,0},{2,3},{3,2},{4,5},{5,4},{6,7},{7,6},{8,9},{9,8},{10,11... | collective-permute-start | bytes 589832 | tf_op jit(solution)/shard_map/ppermute | solution.py:251
  27.1 7.0 %collective-permute-start.9 = (bf16[816,256]{1,0:T(8,128)(2,1)S(1)}, bf16[816,256]{1,0:T(8,128)(2,1)S(1)}, u32[]{:S(2)}, u32[]{:S(2)}) collective-permute-start(bf16[816,256]{1,0:T(8,128)(2,1)S(1)} %pack_queries.3.token_ref.refs_1_), channel_id=1, source_target_pairs={{0,1},{1,0},{2,3},{3,2},{4,5},{5,4},{6,7},{7,6},{8,9},{9,8},{10,11... | collective-permute-start | bytes 1253384 | tf_op jit(solution)/shard_map/ppermute | solution.py:251
  28.3 13.8 %collective-permute-start.10 = (bf16[768,256]{1,0:T(8,128)(2,1)S(1)}, bf16[768,256]{1,0:T(8,128)(2,1)S(1)}, u32[]{:S(2)}, u32[]{:S(2)}) collective-permute-start(bf16[768,256]{1,0:T(8,128)(2,1)S(1)} %get-tuple-element.59), channel_id=1, source_target_pairs={{0,4},{1,5},{2,14},{3,15},{4,8},{5,9},{6,2},{7,3},{8,12},{9,13},{1... | collective-permute-start | bytes 1179656 | tf_op jit(solution)/shard_map/ppermute | solution.py:251
  33.7 3.8 %collective-permute-start.12 = (bf16[384,256]{1,0:T(8,128)(2,1)S(1)}, bf16[384,256]{1,0:T(8,128)(2,1)S(1)}, u32[]{:S(2)}, u32[]{:S(2)}) collective-permute-start(bf16[384,256]{1,0:T(8,128)(2,1)S(1)} %get-tuple-element.64), channel_id=1, source_target_pairs={{0,1},{1,0},{2,3},{3,2},{4,5},{5,4},{6,7},{7,6},{8,9},{9,8},{10,11... | collective-permute-start | bytes 589832 | tf_op jit(solution)/shard_map/ppermute | solution.py:251
  34.0 10.8 %collective-permute-start.17 = (bf16[384,256]{1,0:T(8,128)(2,1)S(1)}, bf16[384,256]{1,0:T(8,128)(2,1)S(1)}, u32[]{:S(2)}, u32[]{:S(2)}) collective-permute-start(bf16[384,256]{1,0:T(8,128)(2,1)S(1)} %add_convert_fusion), channel_id=1, source_target_pairs={{0,2},{1,3},{2,0},{3,1},{4,6},{5,7},{6,4},{7,5},{8,10},{9,11},{10,... | collective-permute-start | bytes 589832 | tf_op jit(solution)/shard_map/ppermute | solution.py:251
  34.2 15.6 %collective-permute-start.14 = (bf16[768,256]{1,0:T(8,128)(2,1)S(1)}, bf16[768,256]{1,0:T(8,128)(2,1)S(1)}, u32[]{:S(2)}, u32[]{:S(2)}) collective-permute-start(bf16[768,256]{1,0:T(8,128)(2,1)S(1)} %get-tuple-element.68), channel_id=1, source_target_pairs={{0,4},{1,5},{2,14},{3,15},{4,8},{5,9},{6,2},{7,3},{8,12},{9,13},{1... | collective-permute-start | bytes 1179656 | tf_op jit(solution)/shard_map/ppermute | solution.py:251
  37.1 8.8 %collective-permute-start.11 = (bf16[384,256]{1,0:T(8,128)(2,1)S(1)}, bf16[384,256]{1,0:T(8,128)(2,1)S(1)}, u32[]{:S(2)}, u32[]{:S(2)}) collective-permute-start(bf16[384,256]{1,0:T(8,128)(2,1)S(1)} %get-tuple-element.63), channel_id=1, source_target_pairs={{0,1},{1,0},{2,3},{3,2},{4,5},{5,4},{6,7},{7,6},{8,9},{9,8},{10,11... | collective-permute-start | bytes 589832 | tf_op jit(solution)/shard_map/ppermute | solution.py:251
  37.5 7.3 %collective-permute-start.15 = (bf16[384,256]{1,0:T(8,128)(2,1)S(1)}, bf16[384,256]{1,0:T(8,128)(2,1)S(1)}, u32[]{:S(2)}, u32[]{:S(2)}) collective-permute-start(bf16[384,256]{1,0:T(8,128)(2,1)S(1)} %get-tuple-element.58), channel_id=1, source_target_pairs={{0,1},{1,0},{2,3},{3,2},{4,5},{5,4},{6,7},{7,6},{8,9},{9,8},{10,11... | collective-permute-start | bytes 589832 | tf_op jit(solution)/shard_map/ppermute | solution.py:251
  42.1 5.7 %collective-permute-start.13 = (bf16[384,256]{1,0:T(8,128)(2,1)S(1)}, bf16[384,256]{1,0:T(8,128)(2,1)S(1)}, u32[]{:S(2)}, u32[]{:S(2)}) collective-permute-start(bf16[384,256]{1,0:T(8,128)(2,1)S(1)} %add_convert_fusion.1), channel_id=1, source_target_pairs={{0,2},{1,3},{2,0},{3,1},{4,6},{5,7},{6,4},{7,5},{8,10},{9,11},{10,... | collective-permute-start | bytes 589832 | tf_op jit(solution)/shard_map/ppermute | solution.py:251

commit v7 on v6

--- a/solution.py
+++ b/solution.py
@@ -197,7 +197,7 @@
     place = place_ref[0]
     jump = jnp.where(lax.rem(place, 4) < 2, 2, -2)
     target = place + 2 * jump if level else place
-    acc_ref[...] = jnp.zeros_like(acc_ref)
+    sum_ref = acc_ref if level else dkv_ref
     slots = ((place + jump, (x_ref,), dq_ref), (partner_of(place) + jump, c_refs, cdq_ref))
     for i, (query, queries_ref, out_ref) in enumerate(slots):
         flag = flag_of(keep_ref, count, query, target)
@@ -209,16 +209,22 @@
             )
             total = join(dq) if first else earlier[i][...] + join(dq)
             out_ref[...] = total.astype(out_ref.dtype)
-            acc_ref[...] += join(dk + dv)
+            if i:
+                sum_ref[...] += join(dk + dv)
+            else:
+                sum_ref[...] = join(dk + dv)
 
         @pl.when(jnp.logical_not(flag))
         def _(i=i, out_ref=out_ref):
+            if not i:
+                sum_ref[...] = jnp.zeros_like(sum_ref)
             if first:
                 out_ref[...] = jnp.zeros_like(out_ref)
             else:
                 out_ref[...] = earlier[i][...].astype(out_ref.dtype)
 
-    dkv_ref[...] = acc_ref[...].astype(dkv_ref.dtype)
+    if level:
+        dkv_ref[...] = acc_ref[...].astype(dkv_ref.dtype)
 
 
 def finish_kernel(first, heads, head_dim, scale, *refs):

time: 51.2 us -> 50 us (0.977); the launches traced: 51 us -> 49.2 us
  Pallas kernels: 23.5 us -> 17 us
  starting transfers between devices: 14 us -> 18.5 us
    pallas_call x4, Pallas kernels: 10.8 us -> 6.2 us  [far(): pl.pallas_call(functools.partial(far_kernel, chunks[c], head_dim, factor,...]
    ppermute x18, starting transfers between devices: 14 us -> 18.5 us  [send(): return lax.ppermute(value, 'tok', [(a, b % count) for a, b in pairs])]
    pallas_call x2, Pallas kernels: 5.72 us -> 3.75 us  [near(): pl.pallas_call(functools.partial(near_kernel, chunks, head_dim, factor, c...]
  transfers between devices with their start and end apart: 18 -> 18, of which waited for: 5 -> 6; matrix products, arithmetic and copies ran while one was open for 0% -> 0% of each run, Pallas kernels for 41% -> 30%
where the time goes in v7:
time: 50 us; the launch traced here: 49.2 us
  starting transfers between devices  18.5 us (37%)
  Pallas kernels  17 us (34%)
  waiting for transfers between devices  12.5 us (25%)
  between operations  0.97 us (2%)
    ppermute x18, starting transfers between devices, send(): return lax.ppermute(value, 'tok', [(a, b % count) for a, b in pairs])  18.5 us
    ppermute x18, waiting for transfers between devices, send(): return lax.ppermute(value, 'tok', [(a, b % count) for a, b in pairs])  12.5 us
    pallas_call x4, Pallas kernels, far(): pl.pallas_call(functools.partial(far_kernel, chunks[c], head_dim, factor,...  6.2 us
    pallas_call x2, Pallas kernels, near(): pl.pallas_call(functools.partial(near_kernel, chunks, head_dim, factor, c...  3.75 us
    pallas_call x2, Pallas kernels, per_device(): pl.pallas_call(functools.partial(pack_queries, sum(chunks[:c]), heads, he...  2.77 us
    pallas_call x2, Pallas kernels, per_device(): pl.pallas_call(functools.partial(finish_kernel, sum(chunks[:c]), heads, h...  2.16 us
    pallas_call x1, Pallas kernels, per_device(): pl.pallas_call(functools.partial(pack_keys, chunks, head_dim), out_shape=...  1.39 us
  transfers between devices with their start and end apart: 18, of which 6 were waited for; matrix products, arithmetic and copies ran while one was open for 0% of the time, Pallas kernels for 30%

profile of v7, /device:TPU:0, one launch (start us, length us, event | category | flops | bytes accessed | tf_op | source)
XLA Modules:
  0.0 49.2 jit_solution(16877802244251302824)
XLA Ops:
  0.6 1.4 %pack_queries.2.rest_0_.refs_0_ = bf16[816,256]{1,0:T(8,128)(2,1)S(1)} custom-call(bf16[256,768]{1,0:T(8,128)(2,1)} %q_hbm.3, bf16[256,768]{1,0:T(8,128)(2,1)} %do_hbm.3, bf16[256,768]{1,0:T(8,128)(2,1)} %o_hbm.3, f32[16,256]{1,0:T(8,128)} %lse_hbm.3), custom_call_target="tpu_custom_call" | custom-call | tf_op jit(solution)/shard_map/pack_queries/pallas_call | solution.py:275
  2.0 3.0 %collective-permute-start.2 = (bf16[816,256]{1,0:T(8,128)(2,1)S(1)}, bf16[816,256]{1,0:T(8,128)(2,1)S(1)}, u32[]{:S(2)}, u32[]{:S(2)}) collective-permute-start(bf16[816,256]{1,0:T(8,128)(2,1)S(1)} %pack_queries.2.rest_0_.refs_0_), channel_id=1, source_target_pairs={{0,2},{1,3},{2,0},{3,1},{4,6},{5,7},{6,4},{7,5},{8,10},{9,11},{10,... | collective-permute-start | bytes 1253384 | tf_op jit(solution)/shard_map/ppermute | solution.py:257
  5.0 1.4 %pack_queries.3.token_ref.refs_1_ = bf16[816,256]{1,0:T(8,128)(2,1)S(1)} custom-call(bf16[256,768]{1,0:T(8,128)(2,1)} %q_hbm.3, bf16[256,768]{1,0:T(8,128)(2,1)} %do_hbm.3, bf16[256,768]{1,0:T(8,128)(2,1)} %o_hbm.3, f32[16,256]{1,0:T(8,128)} %lse_hbm.3, bf16[816,256]{1,0:T(8,128)(2,1)S(1)} %pack_queries.2.rest_0_.refs_0_), custom_call_target="tpu_custom_call" | custom-call | tf_op jit(solution)/shard_map/pack_queries/pallas_call | solution.py:275
  6.6 1.4 %pack_keys.1 = (bf16[768,256]{1,0:T(8,128)(2,1)S(1)}, bf16[768,256]{1,0:T(8,128)(2,1)S(1)}) custom-call(bf16[256,768]{1,0:T(8,128)(2,1)} %k_hbm.1, bf16[256,768]{1,0:T(8,128)(2,1)} %v_hbm.1, bf16[816,256]{1,0:T(8,128)(2,1)S(1)} %pack_queries.3.token_ref.refs_1_), custom_call_target="tpu_custom_call" | custom-call | tf_op jit(solution)/shard_map/pack_keys/pallas_call | solution.py:286
  8.0 4.1 %collective-permute-start.5 = (bf16[768,256]{1,0:T(8,128)(2,1)S(1)}, bf16[768,256]{1,0:T(8,128)(2,1)}, u32[]{:S(2)}, u32[]{:S(2)}) collective-permute-start(bf16[768,256]{1,0:T(8,128)(2,1)S(1)} %get-tuple-element.43.refs_2_), channel_id=1, source_target_pairs={{0,12},{1,13},{2,6},{3,7},{4,0},{5,1},{6,10},{7,11},{8,4},{9,5},{1... | collective-permute-start | bytes 1179656 | tf_op jit(solution)/shard_map/ppermute | solution.py:257
  12.1 3.4 %collective-permute-done.2.x_ref = bf16[816,256]{1,0:T(8,128)(2,1)S(1)} collective-permute-done((bf16[816,256]{1,0:T(8,128)(2,1)S(1)}, bf16[816,256]{1,0:T(8,128)(2,1)S(1)}, u32[]{:S(2)}, u32[]{:S(2)}) %collective-permute-start.2) | collective-permute-done | bytes 417824 | tf_op jit(solution)/shard_map/ppermute | solution.py:257
  16.7 4.2 %collective-permute-start.8 = (bf16[768,256]{1,0:T(8,128)(2,1)S(1)}, bf16[768,256]{1,0:T(8,128)(2,1)}, u32[]{:S(2)}, u32[]{:S(2)}) collective-permute-start(bf16[768,256]{1,0:T(8,128)(2,1)S(1)} %get-tuple-element.51.refs_2_.refs_3_), channel_id=1, source_target_pairs={{0,12},{1,13},{2,6},{3,7},{4,0},{5,1},{6,10},{7,11},{8,4},{9,5},{1... | collective-permute-start | bytes 1179656 | tf_op jit(solution)/shard_map/ppermute | solution.py:257
  21.0 0.8 %far_tasks.4 = (f32[384,256]{1,0:T(8,128)S(1)}, f32[384,256]{1,0:T(8,128)S(1)}, f32[768,256]{1,0:T(8,128)S(1)}) custom-call(s32[16,5]{1,0:T(8,128)S(1)} %copy.18.keep_ref, s32[1]{0:T(128)} %bitcast.place_ref, bf16[816,256]{1,0:T(8,128)(2,1)S(1)} %collective-permute-done.2.x_ref, bf16[384,256]{1,0:T(8,128)(2,1)S(1)} %collective-permute-done.3.refs_0_, ...), custom_call_target="tpu_custom_call" | custom-call | flops 13421772 | bytes 1024 | tf_op jit(solution)/shard_map/far_tasks/pallas_call | solution.py:321
  21.8 2.3 %far_tasks.5 = (bf16[384,256]{1,0:T(8,128)(2,1)S(1)}, bf16[384,256]{1,0:T(8,128)(2,1)S(1)}, bf16[768,256]{1,0:T(8,128)(2,1)S(1)}) custom-call(s32[16,5]{1,0:T(8,128)S(1)} %copy.18.keep_ref, s32[1]{0:T(128)} %bitcast.place_ref, bf16[816,256]{1,0:T(8,128)(2,1)S(1)} %collective-permute-done.2.x_ref, bf16[384,256]{1,0:T(8,128)(2,1)S(1)} %collective-permute-done.3.refs_0_, ...), custom_call_target="tpu_custom_call" | custom-call | flops 13421772 | bytes 1024 | tf_op jit(solution)/shard_map/far_tasks/pallas_call | solution.py:321
  24.2 0.8 %collective-permute-start.7 = (bf16[432,256]{1,0:T(8,128)(2,1)S(1)}, bf16[432,256]{1,0:T(8,128)(2,1)S(1)}, u32[]{:S(2)}, u32[]{:S(2)}) collective-permute-start(bf16[432,256]{1,0:T(8,128)(2,1)S(1)} %get-tuple-element.50), channel_id=1, source_target_pairs={{0,1},{1,0},{2,3},{3,2},{4,5},{5,4},{6,7},{7,6},{8,9},{9,8},{10,11... | collective-permute-start | bytes 663560 | tf_op jit(solution)/shard_map/ppermute | solution.py:257
  25.5 0.9 %collective-permute-done.6.refs_0_ = bf16[384,256]{1,0:T(8,128)(2,1)S(1)} collective-permute-done((bf16[384,256]{1,0:T(8,128)(2,1)S(1)}, bf16[384,256]{1,0:T(8,128)(2,1)S(1)}, u32[]{:S(2)}, u32[]{:S(2)}) %collective-permute-start.6) | collective-permute-done | bytes 196640 | tf_op jit(solution)/shard_map/ppermute | solution.py:257
  26.4 0.9 %collective-permute-start.10 = (bf16[768,256]{1,0:T(8,128)(2,1)S(1)}, bf16[768,256]{1,0:T(8,128)(2,1)S(1)}, u32[]{:S(2)}, u32[]{:S(2)}) collective-permute-start(bf16[768,256]{1,0:T(8,128)(2,1)S(1)} %get-tuple-element.59), channel_id=1, source_target_pairs={{0,4},{1,5},{2,14},{3,15},{4,8},{5,9},{6,2},{7,3},{8,12},{9,13},{1... | collective-permute-start | bytes 1179656 | tf_op jit(solution)/shard_map/ppermute | solution.py:257
  27.3 0.8 %far_tasks.6 = (f32[384,256]{1,0:T(8,128)S(1)}, f32[384,256]{1,0:T(8,128)S(1)}, f32[768,256]{1,0:T(8,128)S(1)}) custom-call(s32[16,5]{1,0:T(8,128)S(1)} %copy.18.keep_ref, s32[1]{0:T(128)} %bitcast.place_ref, bf16[816,256]{1,0:T(8,128)(2,1)S(1)} %collective-permute-done.1.x_ref, bf16[384,256]{1,0:T(8,128)(2,1)S(1)} %collective-permute-done.6.refs_0_, ...), custom_call_target="tpu_custom_call" | custom-call | flops 13421772 | bytes 1024 | tf_op jit(solution)/shard_map/far_tasks/pallas_call | solution.py:321
  28.1 2.2 %collective-permute-done.8.refs_2_ = bf16[768,256]{1,0:T(8,128)(2,1)} collective-permute-done((bf16[768,256]{1,0:T(8,128)(2,1)S(1)}, bf16[768,256]{1,0:T(8,128)(2,1)}, u32[]{:S(2)}, u32[]{:S(2)}) %collective-permute-start.8) | collective-permute-done | bytes 393248 | tf_op jit(solution)/shard_map/ppermute | solution.py:257
  30.4 2.3 %far_tasks.7 = (bf16[384,256]{1,0:T(8,128)(2,1)S(1)}, bf16[384,256]{1,0:T(8,128)(2,1)S(1)}, bf16[768,256]{1,0:T(8,128)(2,1)S(1)}) custom-call(s32[16,5]{1,0:T(8,128)S(1)} %copy.18.keep_ref, s32[1]{0:T(128)} %bitcast.place_ref, bf16[816,256]{1,0:T(8,128)(2,1)S(1)} %collective-permute-done.1.x_ref, bf16[384,256]{1,0:T(8,128)(2,1)S(1)} %collective-permute-done.6.refs_0_, ...), custom_call_target="tpu_custom_call" | custom-call | flops 13421772 | bytes 1024 | tf_op jit(solution)/shard_map/far_tasks/pallas_call | solution.py:321
  32.8 1.2 %collective-permute-start.17 = (bf16[384,256]{1,0:T(8,128)(2,1)S(1)}, bf16[384,256]{1,0:T(8,128)(2,1)S(1)}, u32[]{:S(2)}, u32[]{:S(2)}) collective-permute-start(bf16[384,256]{1,0:T(8,128)(2,1)S(1)} %add_convert_fusion), channel_id=1, source_target_pairs={{0,2},{1,3},{2,0},{3,1},{4,6},{5,7},{6,4},{7,5},{8,10},{9,11},{10,... | collective-permute-start | bytes 589832 | tf_op jit(solution)/shard_map/ppermute | solution.py:257
  34.7 1.0 %near_tasks.2 = (bf16[384,256]{1,0:T(8,128)(2,1)S(1)}, f32[768,256]{1,0:T(8,128)S(1)}, bf16[384,256]{1,0:T(8,128)(2,1)S(1)}, f32[768,256]{1,0:T(8,128)S(1)}) custom-call(s32[16,5]{1,0:T(8,128)S(1)} %copy.18.keep_ref, s32[1]{0:T(128)} %bitcast.place_ref, bf16[816,256]{1,0:T(8,128)(2,1)S(1)} %collective-permute-done.refs_0_, ...), custom_call_target="tpu_custom_call" | custom-call | flops 26843544 | bytes 1024 | tf_op jit(solution)/shard_map/near_tasks/pallas_call | solution.py:307
  36.3 3.8 %collective-permute-done.10.refs_6_ = bf16[768,256]{1,0:T(8,128)(2,1)S(1)} collective-permute-done((bf16[768,256]{1,0:T(8,128)(2,1)S(1)}, bf16[768,256]{1,0:T(8,128)(2,1)S(1)}, u32[]{:S(2)}, u32[]{:S(2)}) %collective-permute-start.10) | collective-permute-done | bytes 393248 | tf_op jit(solution)/shard_map/ppermute | solution.py:257
  40.1 1.7 %collective-permute-start.13 = (bf16[384,256]{1,0:T(8,128)(2,1)S(1)}, bf16[384,256]{1,0:T(8,128)(2,1)S(1)}, u32[]{:S(2)}, u32[]{:S(2)}) collective-permute-start(bf16[384,256]{1,0:T(8,128)(2,1)S(1)} %add_convert_fusion.1), channel_id=1, source_target_pairs={{0,2},{1,3},{2,0},{3,1},{4,6},{5,7},{6,4},{7,5},{8,10},{9,11},{10,... | collective-permute-start | bytes 589832 | tf_op jit(solution)/shard_map/ppermute | solution.py:257
  41.9 2.8 %near_tasks.3 = (f32[384,256]{1,0:T(8,128)S(1)}, f32[768,256]{1,0:T(8,128)S(1)}, f32[384,256]{1,0:T(8,128)S(1)}, f32[768,256]{1,0:T(8,128)S(1)}) custom-call(s32[16,5]{1,0:T(8,128)S(1)} %copy.18.keep_ref, s32[1]{0:T(128)} %bitcast.place_ref, bf16[816,256]{1,0:T(8,128)(2,1)S(1)} %pack_queries.2.rest_0_.refs_0_, ...), custom_call_target="tpu_custom_call" | custom-call | flops 26843544 | bytes 1024 | tf_op jit(solution)/shard_map/near_tasks/pallas_call | solution.py:307
  44.7 1.1 %finish.2 = (bf16[256,768]{1,0:T(8,128)(2,1)}, bf16[256,768]{1,0:T(8,128)(2,1)}, bf16[256,768]{1,0:T(8,128)(2,1)}) custom-call(f32[384,256]{1,0:T(8,128)S(1)} %get-tuple-element.69.refs_0_, bf16[384,256]{1,0:T(8,128)(2,1)S(1)} %collective-permute-done.15.refs_1_, bf16[384,256]{1,0:T(8,128)(2,1)S(1)} %collective-permute-done.17.refs_2_, ...), custom_call_target="tpu_custom_call" | custom-call | flops 1024 | bytes 1024 | tf_op jit(solution)/shard_map/finish/pallas_call | solution.py:363
  45.8 1.3 %collective-permute-done.13.refs_2_ = bf16[384,256]{1,0:T(8,128)(2,1)S(1)} collective-permute-done((bf16[384,256]{1,0:T(8,128)(2,1)S(1)}, bf16[384,256]{1,0:T(8,128)(2,1)S(1)}, u32[]{:S(2)}, u32[]{:S(2)}) %collective-permute-start.13) | collective-permute-done | bytes 196640 | tf_op jit(solution)/shard_map/ppermute | solution.py:257
  47.0 0.9 %collective-permute-done.14.refs_6_ = bf16[768,256]{1,0:T(8,128)(2,1)S(1)} collective-permute-done((bf16[768,256]{1,0:T(8,128)(2,1)S(1)}, bf16[768,256]{1,0:T(8,128)(2,1)S(1)}, u32[]{:S(2)}, u32[]{:S(2)}) %collective-permute-start.14) | collective-permute-done | bytes 393248 | tf_op jit(solution)/shard_map/ppermute | solution.py:257
  47.9 1.1 %finish.3 = (bf16[256,768]{1,0:T(8,128)(2,1)}, bf16[256,768]{1,0:T(8,128)(2,1)}, bf16[256,768]{1,0:T(8,128)(2,1)}) custom-call(f32[384,256]{1,0:T(8,128)S(1)} %get-tuple-element.62.refs_0_, bf16[384,256]{1,0:T(8,128)(2,1)S(1)} %collective-permute-done.11.refs_1_, ...), custom_call_target="tpu_custom_call", output_to_operand_aliasing={{0}: (7, {}), {1}: (8, {}), {2}: (9, {})} | custom-call | flops 1024 | bytes 1024 | tf_op jit(solution)/shard_map/finish/pallas_call | solution.py:363
  (30 shorter events, 3.5 us)
Async XLA Ops:
  2.0 13.5 %collective-permute-start.2 = (bf16[816,256]{1,0:T(8,128)(2,1)S(1)}, bf16[816,256]{1,0:T(8,128)(2,1)S(1)}, u32[]{:S(2)}, u32[]{:S(2)}) collective-permute-start(bf16[816,256]{1,0:T(8,128)(2,1)S(1)} %pack_queries.2.rest_0_.refs_0_), channel_id=1, source_target_pairs={{0,2},{1,3},{2,0},{3,1},{4,6},{5,7},{6,4},{7,5},{8,10},{9,11},{10,... | collective-permute-start | bytes 1253384 | tf_op jit(solution)/shard_map/ppermute | solution.py:257
  5.0 10.5 %collective-permute-start = (bf16[816,256]{1,0:T(8,128)(2,1)S(1)}, bf16[816,256]{1,0:T(8,128)(2,1)S(1)}, u32[]{:S(2)}, u32[]{:S(2)}) collective-permute-start(bf16[816,256]{1,0:T(8,128)(2,1)S(1)} %pack_queries.2.rest_0_.refs_0_), channel_id=1, source_target_pairs={{0,1},{1,0},{2,3},{3,2},{4,5},{5,4},{6,7},{7,6},{8,9},{9,8},{10,11... | collective-permute-start | bytes 1253384 | tf_op jit(solution)/shard_map/ppermute | solution.py:257
  6.4 17.7 %collective-permute-start.1 = (bf16[816,256]{1,0:T(8,128)(2,1)S(1)}, bf16[816,256]{1,0:T(8,128)(2,1)S(1)}, u32[]{:S(2)}, u32[]{:S(2)}) collective-permute-start(bf16[816,256]{1,0:T(8,128)(2,1)S(1)} %pack_queries.3.token_ref.refs_1_), channel_id=1, source_target_pairs={{0,2},{1,3},{2,0},{3,1},{4,6},{5,7},{6,4},{7,5},{8,10},{9,11},{10,... | collective-permute-start | bytes 1253384 | tf_op jit(solution)/shard_map/ppermute | solution.py:257
  8.0 13.8 %collective-permute-start.5 = (bf16[768,256]{1,0:T(8,128)(2,1)S(1)}, bf16[768,256]{1,0:T(8,128)(2,1)}, u32[]{:S(2)}, u32[]{:S(2)}) collective-permute-start(bf16[768,256]{1,0:T(8,128)(2,1)S(1)} %get-tuple-element.43.refs_2_), channel_id=1, source_target_pairs={{0,12},{1,13},{2,6},{3,7},{4,0},{5,1},{6,10},{7,11},{8,4},{9,5},{1... | collective-permute-start | bytes 1179656 | tf_op jit(solution)/shard_map/ppermute | solution.py:257
  16.2 4.8 %collective-permute-start.4 = (bf16[432,256]{1,0:T(8,128)(2,1)S(1)}, bf16[432,256]{1,0:T(8,128)(2,1)S(1)}, u32[]{:S(2)}, u32[]{:S(2)}) collective-permute-start(bf16[432,256]{1,0:T(8,128)(2,1)S(1)} %get-tuple-element.42), channel_id=1, source_target_pairs={{0,1},{1,0},{2,3},{3,2},{4,5},{5,4},{6,7},{7,6},{8,9},{9,8},{10,11... | collective-permute-start | bytes 663560 | tf_op jit(solution)/shard_map/ppermute | solution.py:257
  16.2 4.7 %copy-start = (s32[16,5]{0,1:T(8,128)S(1)}, s32[16,5]{0,1:T(8,128)}, u32[]{:S(2)}) copy-start(s32[16,5]{0,1:T(8,128)} %param.13) | copy-start | bytes 964
  16.2 4.8 %collective-permute-start.3 = (bf16[384,256]{1,0:T(8,128)(2,1)}, bf16[384,256]{1,0:T(8,128)(2,1)S(1)}, u32[]{:S(2)}, u32[]{:S(2)}) collective-permute-start(bf16[384,256]{1,0:T(8,128)(2,1)} %get-tuple-element.41), channel_id=1, source_target_pairs={{0,1},{1,0},{2,3},{3,2},{4,5},{5,4},{6,7},{7,6},{8,9},{9,8},{10,11... | collective-permute-start | bytes 589832 | tf_op jit(solution)/shard_map/ppermute | solution.py:257
  16.7 13.7 %collective-permute-start.8 = (bf16[768,256]{1,0:T(8,128)(2,1)S(1)}, bf16[768,256]{1,0:T(8,128)(2,1)}, u32[]{:S(2)}, u32[]{:S(2)}) collective-permute-start(bf16[768,256]{1,0:T(8,128)(2,1)S(1)} %get-tuple-element.51.refs_2_.refs_3_), channel_id=1, source_target_pairs={{0,12},{1,13},{2,6},{3,7},{4,0},{5,1},{6,10},{7,11},{8,4},{9,5},{1... | collective-permute-start | bytes 1179656 | tf_op jit(solution)/shard_map/ppermute | solution.py:257
  24.2 3.2 %collective-permute-start.7 = (bf16[432,256]{1,0:T(8,128)(2,1)S(1)}, bf16[432,256]{1,0:T(8,128)(2,1)S(1)}, u32[]{:S(2)}, u32[]{:S(2)}) collective-permute-start(bf16[432,256]{1,0:T(8,128)(2,1)S(1)} %get-tuple-element.50), channel_id=1, source_target_pairs={{0,1},{1,0},{2,3},{3,2},{4,5},{5,4},{6,7},{7,6},{8,9},{9,8},{10,11... | collective-permute-start | bytes 663560 | tf_op jit(solution)/shard_map/ppermute | solution.py:257
  24.9 1.4 %collective-permute-start.6 = (bf16[384,256]{1,0:T(8,128)(2,1)S(1)}, bf16[384,256]{1,0:T(8,128)(2,1)S(1)}, u32[]{:S(2)}, u32[]{:S(2)}) collective-permute-start(bf16[384,256]{1,0:T(8,128)(2,1)S(1)} %get-tuple-element.49), channel_id=1, source_target_pairs={{0,1},{1,0},{2,3},{3,2},{4,5},{5,4},{6,7},{7,6},{8,9},{9,8},{10,11... | collective-permute-start | bytes 589832 | tf_op jit(solution)/shard_map/ppermute | solution.py:257
  25.0 7.8 %collective-permute-start.16 = (bf16[384,256]{1,0:T(8,128)(2,1)S(1)}, bf16[384,256]{1,0:T(8,128)(2,1)S(1)}, u32[]{:S(2)}, u32[]{:S(2)}) collective-permute-start(bf16[384,256]{1,0:T(8,128)(2,1)S(1)} %get-tuple-element.70), channel_id=1, source_target_pairs={{0,1},{1,0},{2,3},{3,2},{4,5},{5,4},{6,7},{7,6},{8,9},{9,8},{10,11... | collective-permute-start | bytes 589832 | tf_op jit(solution)/shard_map/ppermute | solution.py:257
  25.5 8.6 %collective-permute-start.9 = (bf16[816,256]{1,0:T(8,128)(2,1)S(1)}, bf16[816,256]{1,0:T(8,128)(2,1)S(1)}, u32[]{:S(2)}, u32[]{:S(2)}) collective-permute-start(bf16[816,256]{1,0:T(8,128)(2,1)S(1)} %pack_queries.3.token_ref.refs_1_), channel_id=1, source_target_pairs={{0,1},{1,0},{2,3},{3,2},{4,5},{5,4},{6,7},{7,6},{8,9},{9,8},{10,11... | collective-permute-start | bytes 1253384 | tf_op jit(solution)/shard_map/ppermute | solution.py:257
  26.4 13.7 %collective-permute-start.10 = (bf16[768,256]{1,0:T(8,128)(2,1)S(1)}, bf16[768,256]{1,0:T(8,128)(2,1)S(1)}, u32[]{:S(2)}, u32[]{:S(2)}) collective-permute-start(bf16[768,256]{1,0:T(8,128)(2,1)S(1)} %get-tuple-element.59), channel_id=1, source_target_pairs={{0,4},{1,5},{2,14},{3,15},{4,8},{5,9},{6,2},{7,3},{8,12},{9,13},{1... | collective-permute-start | bytes 1179656 | tf_op jit(solution)/shard_map/ppermute | solution.py:257
  32.7 3.1 %collective-permute-start.12 = (bf16[384,256]{1,0:T(8,128)(2,1)S(1)}, bf16[384,256]{1,0:T(8,128)(2,1)S(1)}, u32[]{:S(2)}, u32[]{:S(2)}) collective-permute-start(bf16[384,256]{1,0:T(8,128)(2,1)S(1)} %get-tuple-element.64), channel_id=1, source_target_pairs={{0,1},{1,0},{2,3},{3,2},{4,5},{5,4},{6,7},{7,6},{8,9},{9,8},{10,11... | collective-permute-start | bytes 589832 | tf_op jit(solution)/shard_map/ppermute | solution.py:257
  32.8 11.8 %collective-permute-start.17 = (bf16[384,256]{1,0:T(8,128)(2,1)S(1)}, bf16[384,256]{1,0:T(8,128)(2,1)S(1)}, u32[]{:S(2)}, u32[]{:S(2)}) collective-permute-start(bf16[384,256]{1,0:T(8,128)(2,1)S(1)} %add_convert_fusion), channel_id=1, source_target_pairs={{0,2},{1,3},{2,0},{3,1},{4,6},{5,7},{6,4},{7,5},{8,10},{9,11},{10,... | collective-permute-start | bytes 589832 | tf_op jit(solution)/shard_map/ppermute | solution.py:257
  34.1 13.9 %collective-permute-start.14 = (bf16[768,256]{1,0:T(8,128)(2,1)S(1)}, bf16[768,256]{1,0:T(8,128)(2,1)S(1)}, u32[]{:S(2)}, u32[]{:S(2)}) collective-permute-start(bf16[768,256]{1,0:T(8,128)(2,1)S(1)} %get-tuple-element.68), channel_id=1, source_target_pairs={{0,4},{1,5},{2,14},{3,15},{4,8},{5,9},{6,2},{7,3},{8,12},{9,13},{1... | collective-permute-start | bytes 1179656 | tf_op jit(solution)/shard_map/ppermute | solution.py:257
  35.7 10.1 %collective-permute-start.11 = (bf16[384,256]{1,0:T(8,128)(2,1)S(1)}, bf16[384,256]{1,0:T(8,128)(2,1)S(1)}, u32[]{:S(2)}, u32[]{:S(2)}) collective-permute-start(bf16[384,256]{1,0:T(8,128)(2,1)S(1)} %get-tuple-element.63), channel_id=1, source_target_pairs={{0,1},{1,0},{2,3},{3,2},{4,5},{5,4},{6,7},{7,6},{8,9},{9,8},{10,11... | collective-permute-start | bytes 589832 | tf_op jit(solution)/shard_map/ppermute | solution.py:257
  35.8 8.9 %collective-permute-start.15 = (bf16[384,256]{1,0:T(8,128)(2,1)S(1)}, bf16[384,256]{1,0:T(8,128)(2,1)S(1)}, u32[]{:S(2)}, u32[]{:S(2)}) collective-permute-start(bf16[384,256]{1,0:T(8,128)(2,1)S(1)} %get-tuple-element.58), channel_id=1, source_target_pairs={{0,1},{1,0},{2,3},{3,2},{4,5},{5,4},{6,7},{7,6},{8,9},{9,8},{10,11... | collective-permute-start | bytes 589832 | tf_op jit(solution)/shard_map/ppermute | solution.py:257
  40.1 6.9 %collective-permute-start.13 = (bf16[384,256]{1,0:T(8,128)(2,1)S(1)}, bf16[384,256]{1,0:T(8,128)(2,1)S(1)}, u32[]{:S(2)}, u32[]{:S(2)}) collective-permute-start(bf16[384,256]{1,0:T(8,128)(2,1)S(1)} %add_convert_fusion.1), channel_id=1, source_target_pairs={{0,2},{1,3},{2,0},{3,1},{4,6},{5,7},{6,4},{7,5},{8,10},{9,11},{10,... | collective-permute-start | bytes 589832 | tf_op jit(solution)/shard_map/ppermute | solution.py:257

commit v8 on v7

--- a/solution.py
+++ b/solution.py
@@ -268,21 +268,20 @@
     x_rows = [2 * h * head_dim + extra_rows(h) for h in chunks]
     hbm = pl.BlockSpec(memory_space=pltpu.HBM)
     fixed = lambda *values: [pltpu.with_memory_space_constraint(v, pltpu.HBM) for v in values]
-    x_own = []
-    for c, heads in enumerate(chunks):
+    def queries_of(c, heads, *token):
         rows = heads * head_dim
-        x_own.append(
-            pl.pallas_call(
-                functools.partial(pack_queries, sum(chunks[:c]), heads, head_dim),
+        return pl.pallas_call(
+            functools.partial(pack_queries, sum(chunks[:c]), heads, head_dim),
                 out_shape=shape(x_rows[c], BF16),
-                in_specs=[hbm] * 4 + [pl.BlockSpec(memory_space=pl.ANY)] * c,
+                in_specs=[hbm] * 4 + [pl.BlockSpec(memory_space=pl.ANY)] * len(token),
                 out_specs=VMEM,
                 scratch_shapes=[pltpu.VMEM((tokens, rows), BF16)] * 3
                 + [pltpu.VMEM((HEADS, tokens), F32), pltpu.SemaphoreType.DMA((4,))],
                 compiler_params=params(),
                 name="pack_queries",
-            )(*fixed(query_rows, grad_out, out_rows, normalizer), *x_own)
-        )
+            )(*fixed(query_rows, grad_out, out_rows, normalizer), *token)
+
+    x_own = [queries_of(0, chunks[0])]
     kv_own = pl.pallas_call(
         functools.partial(pack_keys, chunks, head_dim),
         out_shape=[shape(2 * h * head_dim, BF16) for h in chunks],
@@ -291,7 +290,8 @@
         scratch_shapes=[pltpu.VMEM((tokens, width), BF16)] * 2 + [pltpu.SemaphoreType.DMA((2,))],
         compiler_params=params(),
         name="pack_keys",
-    )(*fixed(key_rows, value_rows), x_own[-1])
+    )(*fixed(key_rows, value_rows), x_own[0])
+    x_own += [queries_of(c, chunks[c], kv_own[0]) for c in range(1, len(chunks))]
     x_far = [send(x, across) for x in x_own]
     kv_level = [send(kv, level_in) for kv in kv_own]
     x_core = [send(x, core) for x in x_own]

time: 50 us -> 49.6 us (level); the launches traced: 49.2 us -> 49.5 us
  starting transfers between devices: 18.5 us -> 20.4 us
  waiting for transfers between devices: 12.5 us -> 11.2 us
    pallas_call x4, Pallas kernels: 6.2 us -> 3.94 us  [far(): pl.pallas_call(functools.partial(far_kernel, chunks[c], head_dim, factor,...]
    pallas_call x2, Pallas kernels: 3.75 us -> 5.73 us  [near(): pl.pallas_call(functools.partial(near_kernel, chunks, head_dim, factor, c...]
    ppermute x18, starting transfers between devices: 18.5 us -> 20.4 us  [send(): return lax.ppermute(value, 'tok', [(a, b % count) for a, b in pairs])]
    ppermute x18, waiting for transfers between devices: 12.5 us -> 11.2 us  [send(): return lax.ppermute(value, 'tok', [(a, b % count) for a, b in pairs])]
  transfers between devices with their start and end apart: 18 -> 18, of which waited for: 6 -> 6; matrix products, arithmetic and copies ran while one was open for 0% -> 0% of each run, Pallas kernels for 30% -> 29%
where the time goes in v8:
time: 49.6 us; the launch traced here: 49.5 us
  starting transfers between devices  20.4 us (41%)
  Pallas kernels  16.7 us (34%)
  waiting for transfers between devices  11.2 us (23%)
  between operations  0.98 us (2%)
    ppermute x18, starting transfers between devices, send(): return lax.ppermute(value, 'tok', [(a, b % count) for a, b in pairs])  20.4 us
    ppermute x18, waiting for transfers between devices, send(): return lax.ppermute(value, 'tok', [(a, b % count) for a, b in pairs])  11.2 us
    pallas_call x2, Pallas kernels, near(): pl.pallas_call(functools.partial(near_kernel, chunks, head_dim, factor, c...  5.73 us
    pallas_call x4, Pallas kernels, far(): pl.pallas_call(functools.partial(far_kernel, chunks[c], head_dim, factor,...  3.94 us
    pallas_call x2, Pallas kernels, queries_of(): pl.pallas_call(functools.partial(pack_queries, sum(chunks[:c]), heads, he...  2.78 us
    pallas_call x2, Pallas kernels, per_device(): pl.pallas_call(functools.partial(finish_kernel, sum(chunks[:c]), heads, h...  2.18 us
    pallas_call x1, Pallas kernels, per_device(): pl.pallas_call(functools.partial(pack_keys, chunks, head_dim), out_shape=...  1.39 us
  transfers between devices with their start and end apart: 18, of which 6 were waited for; matrix products, arithmetic and copies ran while one was open for 0% of the time, Pallas kernels for 29%

profile of v8, /device:TPU:0, one launch (start us, length us, event | category | flops | bytes accessed | tf_op | source)
XLA Modules:
  0.0 49.5 jit_solution(11387111228970956773)
XLA Ops:
  0.6 1.4 %pack_queries.2.token_ref.refs_0_ = bf16[816,256]{1,0:T(8,128)(2,1)S(1)} custom-call(bf16[256,768]{1,0:T(8,128)(2,1)} %q_hbm.3, bf16[256,768]{1,0:T(8,128)(2,1)} %do_hbm.3, bf16[256,768]{1,0:T(8,128)(2,1)} %o_hbm.3, f32[16,256]{1,0:T(8,128)} %lse_hbm.3), custom_call_target="tpu_custom_call" | custom-call | tf_op jit(solution)/shard_map/pack_queries/pallas_call | solution.py:273
  2.0 3.0 %collective-permute-start.2 = (bf16[816,256]{1,0:T(8,128)(2,1)S(1)}, bf16[816,256]{1,0:T(8,128)(2,1)S(1)}, u32[]{:S(2)}, u32[]{:S(2)}) collective-permute-start(bf16[816,256]{1,0:T(8,128)(2,1)S(1)} %pack_queries.2.token_ref.refs_0_), channel_id=1, source_target_pairs={{0,2},{1,3},{2,0},{3,1},{4,6},{5,7},{6,4},{7,5},{8,10},{9,11},{10,... | collective-permute-start | bytes 1253384 | tf_op jit(solution)/shard_map/ppermute | solution.py:257
  5.0 1.4 %pack_keys.1 = (bf16[768,256]{1,0:T(8,128)(2,1)S(1)}, bf16[768,256]{1,0:T(8,128)(2,1)S(1)}) custom-call(bf16[256,768]{1,0:T(8,128)(2,1)} %k_hbm.1, bf16[256,768]{1,0:T(8,128)(2,1)} %v_hbm.1, bf16[816,256]{1,0:T(8,128)(2,1)S(1)} %pack_queries.2.token_ref.refs_0_), custom_call_target="tpu_custom_call" | custom-call | tf_op jit(solution)/shard_map/pack_keys/pallas_call | solution.py:285
  6.4 1.4 %pack_queries.3.refs_1_ = bf16[816,256]{1,0:T(8,128)(2,1)S(1)} custom-call(bf16[256,768]{1,0:T(8,128)(2,1)} %q_hbm.3, bf16[256,768]{1,0:T(8,128)(2,1)} %do_hbm.3, bf16[256,768]{1,0:T(8,128)(2,1)} %o_hbm.3, f32[16,256]{1,0:T(8,128)} %lse_hbm.3, bf16[768,256]{1,0:T(8,128)(2,1)S(1)} %get-tuple-element.40.rest_0_.refs_2_), custom_call_target="tpu_custom_call" | custom-call | tf_op jit(solution)/shard_map/pack_queries/pallas_call | solution.py:273
  8.0 4.0 %collective-permute-start.5 = (bf16[768,256]{1,0:T(8,128)(2,1)S(1)}, bf16[768,256]{1,0:T(8,128)(2,1)}, u32[]{:S(2)}, u32[]{:S(2)}) collective-permute-start(bf16[768,256]{1,0:T(8,128)(2,1)S(1)} %get-tuple-element.40.rest_0_.refs_2_), channel_id=1, source_target_pairs={{0,12},{1,13},{2,6},{3,7},{4,0},{5,1},{6,10},{7,11},{8,4},{9,5},{1... | collective-permute-start | bytes 1179656 | tf_op jit(solution)/shard_map/ppermute | solution.py:257
  12.0 3.5 %collective-permute-done.2.x_ref = bf16[816,256]{1,0:T(8,128)(2,1)S(1)} collective-permute-done((bf16[816,256]{1,0:T(8,128)(2,1)S(1)}, bf16[816,256]{1,0:T(8,128)(2,1)S(1)}, u32[]{:S(2)}, u32[]{:S(2)}) %collective-permute-start.2) | collective-permute-done | bytes 417824 | tf_op jit(solution)/shard_map/ppermute | solution.py:257
  15.5 0.7 %split.2 = (bf16[384,256]{1,0:T(8,128)(2,1)}, bf16[432,256]{1,0:T(8,128)(2,1)S(1)}) custom-call(bf16[816,256]{1,0:T(8,128)(2,1)S(1)} %collective-permute-done.2.x_ref), custom_call_target="tpu_custom_call" | custom-call | flops 1024 | bytes 1024 | tf_op jit(solution)/shard_map/split/pallas_call | solution.py:336
  16.7 4.2 %collective-permute-start.8 = (bf16[768,256]{1,0:T(8,128)(2,1)S(1)}, bf16[768,256]{1,0:T(8,128)(2,1)}, u32[]{:S(2)}, u32[]{:S(2)}) collective-permute-start(bf16[768,256]{1,0:T(8,128)(2,1)S(1)} %get-tuple-element.51.refs_2_.refs_3_), channel_id=1, source_target_pairs={{0,12},{1,13},{2,6},{3,7},{4,0},{5,1},{6,10},{7,11},{8,4},{9,5},{1... | collective-permute-start | bytes 1179656 | tf_op jit(solution)/shard_map/ppermute | solution.py:257
  21.0 0.8 %far_tasks.4 = (f32[384,256]{1,0:T(8,128)S(1)}, f32[384,256]{1,0:T(8,128)S(1)}, f32[768,256]{1,0:T(8,128)S(1)}) custom-call(s32[16,5]{1,0:T(8,128)S(1)} %copy.18.keep_ref, s32[1]{0:T(128)} %bitcast.place_ref, bf16[816,256]{1,0:T(8,128)(2,1)S(1)} %collective-permute-done.2.x_ref, bf16[384,256]{1,0:T(8,128)(2,1)S(1)} %collective-permute-done.3.refs_0_, ...), custom_call_target="tpu_custom_call" | custom-call | flops 13421772 | bytes 1024 | tf_op jit(solution)/shard_map/far_tasks/pallas_call | solution.py:321
  21.8 1.2 %far_tasks.5 = (bf16[384,256]{1,0:T(8,128)(2,1)S(1)}, bf16[384,256]{1,0:T(8,128)(2,1)S(1)}, bf16[768,256]{1,0:T(8,128)(2,1)S(1)}) custom-call(s32[16,5]{1,0:T(8,128)S(1)} %copy.18.keep_ref, s32[1]{0:T(128)} %bitcast.place_ref, bf16[816,256]{1,0:T(8,128)(2,1)S(1)} %collective-permute-done.2.x_ref, bf16[384,256]{1,0:T(8,128)(2,1)S(1)} %collective-permute-done.3.refs_0_, ...), custom_call_target="tpu_custom_call" | custom-call | flops 13421772 | bytes 1024 | tf_op jit(solution)/shard_map/far_tasks/pallas_call | solution.py:321
  23.0 0.6 %collective-permute-done.1.x_ref = bf16[816,256]{1,0:T(8,128)(2,1)S(1)} collective-permute-done((bf16[816,256]{1,0:T(8,128)(2,1)S(1)}, bf16[816,256]{1,0:T(8,128)(2,1)S(1)}, u32[]{:S(2)}, u32[]{:S(2)}) %collective-permute-start.1) | collective-permute-done | bytes 417824 | tf_op jit(solution)/shard_map/ppermute | solution.py:257
  24.7 0.7 %collective-permute-done.6.refs_0_ = bf16[384,256]{1,0:T(8,128)(2,1)S(1)} collective-permute-done((bf16[384,256]{1,0:T(8,128)(2,1)S(1)}, bf16[384,256]{1,0:T(8,128)(2,1)S(1)}, u32[]{:S(2)}, u32[]{:S(2)}) %collective-permute-start.6) | collective-permute-done | bytes 196640 | tf_op jit(solution)/shard_map/ppermute | solution.py:257
  25.5 1.8 %collective-permute-start.10 = (bf16[768,256]{1,0:T(8,128)(2,1)S(1)}, bf16[768,256]{1,0:T(8,128)(2,1)S(1)}, u32[]{:S(2)}, u32[]{:S(2)}) collective-permute-start(bf16[768,256]{1,0:T(8,128)(2,1)S(1)} %get-tuple-element.59), channel_id=1, source_target_pairs={{0,4},{1,5},{2,14},{3,15},{4,8},{5,9},{6,2},{7,3},{8,12},{9,13},{1... | collective-permute-start | bytes 1179656 | tf_op jit(solution)/shard_map/ppermute | solution.py:257
  27.3 0.8 %far_tasks.6 = (f32[384,256]{1,0:T(8,128)S(1)}, f32[384,256]{1,0:T(8,128)S(1)}, f32[768,256]{1,0:T(8,128)S(1)}) custom-call(s32[16,5]{1,0:T(8,128)S(1)} %copy.18.keep_ref, s32[1]{0:T(128)} %bitcast.place_ref, bf16[816,256]{1,0:T(8,128)(2,1)S(1)} %collective-permute-done.1.x_ref, bf16[384,256]{1,0:T(8,128)(2,1)S(1)} %collective-permute-done.6.refs_0_, ...), custom_call_target="tpu_custom_call" | custom-call | flops 13421772 | bytes 1024 | tf_op jit(solution)/shard_map/far_tasks/pallas_call | solution.py:321
  28.1 2.3 %collective-permute-done.8.refs_2_ = bf16[768,256]{1,0:T(8,128)(2,1)} collective-permute-done((bf16[768,256]{1,0:T(8,128)(2,1)S(1)}, bf16[768,256]{1,0:T(8,128)(2,1)}, u32[]{:S(2)}, u32[]{:S(2)}) %collective-permute-start.8) | collective-permute-done | bytes 393248 | tf_op jit(solution)/shard_map/ppermute | solution.py:257
  30.4 1.2 %far_tasks.7 = (bf16[384,256]{1,0:T(8,128)(2,1)S(1)}, bf16[384,256]{1,0:T(8,128)(2,1)S(1)}, bf16[768,256]{1,0:T(8,128)(2,1)S(1)}) custom-call(s32[16,5]{1,0:T(8,128)S(1)} %copy.18.keep_ref, s32[1]{0:T(128)} %bitcast.place_ref, bf16[816,256]{1,0:T(8,128)(2,1)S(1)} %collective-permute-done.1.x_ref, bf16[384,256]{1,0:T(8,128)(2,1)S(1)} %collective-permute-done.6.refs_0_, ...), custom_call_target="tpu_custom_call" | custom-call | flops 13421772 | bytes 1024 | tf_op jit(solution)/shard_map/far_tasks/pallas_call | solution.py:321
  31.7 3.5 %collective-permute-start.17 = (bf16[384,256]{1,0:T(8,128)(2,1)S(1)}, bf16[384,256]{1,0:T(8,128)(2,1)S(1)}, u32[]{:S(2)}, u32[]{:S(2)}) collective-permute-start(bf16[384,256]{1,0:T(8,128)(2,1)S(1)} %add_convert_fusion), channel_id=1, source_target_pairs={{0,2},{1,3},{2,0},{3,1},{4,6},{5,7},{6,4},{7,5},{8,10},{9,11},{10,... | collective-permute-start | bytes 589832 | tf_op jit(solution)/shard_map/ppermute | solution.py:257
  35.2 3.0 %near_tasks.2 = (bf16[384,256]{1,0:T(8,128)(2,1)S(1)}, f32[768,256]{1,0:T(8,128)S(1)}, bf16[384,256]{1,0:T(8,128)(2,1)S(1)}, f32[768,256]{1,0:T(8,128)S(1)}) custom-call(s32[16,5]{1,0:T(8,128)S(1)} %copy.18.keep_ref, s32[1]{0:T(128)} %bitcast.place_ref, bf16[816,256]{1,0:T(8,128)(2,1)S(1)} %collective-permute-done.refs_0_, ...), custom_call_target="tpu_custom_call" | custom-call | flops 26843544 | bytes 1024 | tf_op jit(solution)/shard_map/near_tasks/pallas_call | solution.py:307
  38.8 1.5 %collective-permute-start.13 = (bf16[384,256]{1,0:T(8,128)(2,1)S(1)}, bf16[384,256]{1,0:T(8,128)(2,1)S(1)}, u32[]{:S(2)}, u32[]{:S(2)}) collective-permute-start(bf16[384,256]{1,0:T(8,128)(2,1)S(1)} %add_convert_fusion.1), channel_id=1, source_target_pairs={{0,2},{1,3},{2,0},{3,1},{4,6},{5,7},{6,4},{7,5},{8,10},{9,11},{10,... | collective-permute-start | bytes 589832 | tf_op jit(solution)/shard_map/ppermute | solution.py:257
  40.3 2.8 %near_tasks.3 = (f32[384,256]{1,0:T(8,128)S(1)}, f32[768,256]{1,0:T(8,128)S(1)}, f32[384,256]{1,0:T(8,128)S(1)}, f32[768,256]{1,0:T(8,128)S(1)}) custom-call(s32[16,5]{1,0:T(8,128)S(1)} %copy.18.keep_ref, s32[1]{0:T(128)} %bitcast.place_ref, bf16[816,256]{1,0:T(8,128)(2,1)S(1)} %pack_queries.2.token_ref.refs_0_, bf16[816,256]{1,0:T(8,128)(2,1)S(1)} %pack_queries.3.refs_1_, ...), custom_call_target="tpu_custom_call" | custom-call | flops 26843544 | bytes 1024 | tf_op jit(solution)/shard_map/near_tasks/pallas_call | solution.py:307
  43.1 1.1 %finish.2 = (bf16[256,768]{1,0:T(8,128)(2,1)}, bf16[256,768]{1,0:T(8,128)(2,1)}, bf16[256,768]{1,0:T(8,128)(2,1)}) custom-call(f32[384,256]{1,0:T(8,128)S(1)} %get-tuple-element.69.refs_0_, bf16[384,256]{1,0:T(8,128)(2,1)S(1)} %collective-permute-done.15.refs_1_, bf16[384,256]{1,0:T(8,128)(2,1)S(1)} %collective-permute-done.17.refs_2_, ...), custom_call_target="tpu_custom_call" | custom-call | flops 1024 | bytes 1024 | tf_op jit(solution)/shard_map/finish/pallas_call | solution.py:363
  44.2 1.6 %collective-permute-done.13.refs_2_ = bf16[384,256]{1,0:T(8,128)(2,1)S(1)} collective-permute-done((bf16[384,256]{1,0:T(8,128)(2,1)S(1)}, bf16[384,256]{1,0:T(8,128)(2,1)S(1)}, u32[]{:S(2)}, u32[]{:S(2)}) %collective-permute-start.13) | collective-permute-done | bytes 196640 | tf_op jit(solution)/shard_map/ppermute | solution.py:257
  45.8 2.5 %collective-permute-done.14.refs_6_ = bf16[768,256]{1,0:T(8,128)(2,1)S(1)} collective-permute-done((bf16[768,256]{1,0:T(8,128)(2,1)S(1)}, bf16[768,256]{1,0:T(8,128)(2,1)S(1)}, u32[]{:S(2)}, u32[]{:S(2)}) %collective-permute-start.14) | collective-permute-done | bytes 393248 | tf_op jit(solution)/shard_map/ppermute | solution.py:257
  48.2 1.1 %finish.3 = (bf16[256,768]{1,0:T(8,128)(2,1)}, bf16[256,768]{1,0:T(8,128)(2,1)}, bf16[256,768]{1,0:T(8,128)(2,1)}) custom-call(f32[384,256]{1,0:T(8,128)S(1)} %get-tuple-element.62.refs_0_, bf16[384,256]{1,0:T(8,128)(2,1)S(1)} %collective-permute-done.11.refs_1_, ...), custom_call_target="tpu_custom_call", output_to_operand_aliasing={{0}: (7, {}), {1}: (8, {}), {2}: (9, {})} | custom-call | flops 1024 | bytes 1024 | tf_op jit(solution)/shard_map/finish/pallas_call | solution.py:363
  (30 shorter events, 2.6 us)
Async XLA Ops:
  2.0 13.5 %collective-permute-start.2 = (bf16[816,256]{1,0:T(8,128)(2,1)S(1)}, bf16[816,256]{1,0:T(8,128)(2,1)S(1)}, u32[]{:S(2)}, u32[]{:S(2)}) collective-permute-start(bf16[816,256]{1,0:T(8,128)(2,1)S(1)} %pack_queries.2.token_ref.refs_0_), channel_id=1, source_target_pairs={{0,2},{1,3},{2,0},{3,1},{4,6},{5,7},{6,4},{7,5},{8,10},{9,11},{10,... | collective-permute-start | bytes 1253384 | tf_op jit(solution)/shard_map/ppermute | solution.py:257
  5.0 10.5 %collective-permute-start = (bf16[816,256]{1,0:T(8,128)(2,1)S(1)}, bf16[816,256]{1,0:T(8,128)(2,1)S(1)}, u32[]{:S(2)}, u32[]{:S(2)}) collective-permute-start(bf16[816,256]{1,0:T(8,128)(2,1)S(1)} %pack_queries.2.token_ref.refs_0_), channel_id=1, source_target_pairs={{0,1},{1,0},{2,3},{3,2},{4,5},{5,4},{6,7},{7,6},{8,9},{9,8},{10,11... | collective-permute-start | bytes 1253384 | tf_op jit(solution)/shard_map/ppermute | solution.py:257
  7.8 15.8 %collective-permute-start.1 = (bf16[816,256]{1,0:T(8,128)(2,1)S(1)}, bf16[816,256]{1,0:T(8,128)(2,1)S(1)}, u32[]{:S(2)}, u32[]{:S(2)}) collective-permute-start(bf16[816,256]{1,0:T(8,128)(2,1)S(1)} %pack_queries.3.refs_1_), channel_id=1, source_target_pairs={{0,2},{1,3},{2,0},{3,1},{4,6},{5,7},{6,4},{7,5},{8,10},{9,11},{10,... | collective-permute-start | bytes 1253384 | tf_op jit(solution)/shard_map/ppermute | solution.py:257
  8.0 13.8 %collective-permute-start.5 = (bf16[768,256]{1,0:T(8,128)(2,1)S(1)}, bf16[768,256]{1,0:T(8,128)(2,1)}, u32[]{:S(2)}, u32[]{:S(2)}) collective-permute-start(bf16[768,256]{1,0:T(8,128)(2,1)S(1)} %get-tuple-element.40.rest_0_.refs_2_), channel_id=1, source_target_pairs={{0,12},{1,13},{2,6},{3,7},{4,0},{5,1},{6,10},{7,11},{8,4},{9,5},{1... | collective-permute-start | bytes 1179656 | tf_op jit(solution)/shard_map/ppermute | solution.py:257
  16.2 4.8 %collective-permute-start.4 = (bf16[432,256]{1,0:T(8,128)(2,1)S(1)}, bf16[432,256]{1,0:T(8,128)(2,1)S(1)}, u32[]{:S(2)}, u32[]{:S(2)}) collective-permute-start(bf16[432,256]{1,0:T(8,128)(2,1)S(1)} %get-tuple-element.43), channel_id=1, source_target_pairs={{0,1},{1,0},{2,3},{3,2},{4,5},{5,4},{6,7},{7,6},{8,9},{9,8},{10,11... | collective-permute-start | bytes 663560 | tf_op jit(solution)/shard_map/ppermute | solution.py:257
  16.2 4.7 %copy-start = (s32[16,5]{0,1:T(8,128)S(1)}, s32[16,5]{0,1:T(8,128)}, u32[]{:S(2)}) copy-start(s32[16,5]{0,1:T(8,128)} %param.13) | copy-start | bytes 964
  16.2 4.8 %collective-permute-start.3 = (bf16[384,256]{1,0:T(8,128)(2,1)}, bf16[384,256]{1,0:T(8,128)(2,1)S(1)}, u32[]{:S(2)}, u32[]{:S(2)}) collective-permute-start(bf16[384,256]{1,0:T(8,128)(2,1)} %get-tuple-element.42), channel_id=1, source_target_pairs={{0,1},{1,0},{2,3},{3,2},{4,5},{5,4},{6,7},{7,6},{8,9},{9,8},{10,11... | collective-permute-start | bytes 589832 | tf_op jit(solution)/shard_map/ppermute | solution.py:257
  16.7 13.7 %collective-permute-start.8 = (bf16[768,256]{1,0:T(8,128)(2,1)S(1)}, bf16[768,256]{1,0:T(8,128)(2,1)}, u32[]{:S(2)}, u32[]{:S(2)}) collective-permute-start(bf16[768,256]{1,0:T(8,128)(2,1)S(1)} %get-tuple-element.51.refs_2_.refs_3_), channel_id=1, source_target_pairs={{0,12},{1,13},{2,6},{3,7},{4,0},{5,1},{6,10},{7,11},{8,4},{9,5},{1... | collective-permute-start | bytes 1179656 | tf_op jit(solution)/shard_map/ppermute | solution.py:257
  23.7 3.7 %collective-permute-start.7 = (bf16[432,256]{1,0:T(8,128)(2,1)S(1)}, bf16[432,256]{1,0:T(8,128)(2,1)S(1)}, u32[]{:S(2)}, u32[]{:S(2)}) collective-permute-start(bf16[432,256]{1,0:T(8,128)(2,1)S(1)} %get-tuple-element.50), channel_id=1, source_target_pairs={{0,1},{1,0},{2,3},{3,2},{4,5},{5,4},{6,7},{7,6},{8,9},{9,8},{10,11... | collective-permute-start | bytes 663560 | tf_op jit(solution)/shard_map/ppermute | solution.py:257
  23.7 1.7 %collective-permute-start.6 = (bf16[384,256]{1,0:T(8,128)(2,1)S(1)}, bf16[384,256]{1,0:T(8,128)(2,1)S(1)}, u32[]{:S(2)}, u32[]{:S(2)}) collective-permute-start(bf16[384,256]{1,0:T(8,128)(2,1)S(1)} %get-tuple-element.49), channel_id=1, source_target_pairs={{0,1},{1,0},{2,3},{3,2},{4,5},{5,4},{6,7},{7,6},{8,9},{9,8},{10,11... | collective-permute-start | bytes 589832 | tf_op jit(solution)/shard_map/ppermute | solution.py:257
  24.2 7.4 %collective-permute-start.16 = (bf16[384,256]{1,0:T(8,128)(2,1)S(1)}, bf16[384,256]{1,0:T(8,128)(2,1)S(1)}, u32[]{:S(2)}, u32[]{:S(2)}) collective-permute-start(bf16[384,256]{1,0:T(8,128)(2,1)S(1)} %get-tuple-element.70), channel_id=1, source_target_pairs={{0,1},{1,0},{2,3},{3,2},{4,5},{5,4},{6,7},{7,6},{8,9},{9,8},{10,11... | collective-permute-start | bytes 589832 | tf_op jit(solution)/shard_map/ppermute | solution.py:257
  24.3 10.9 %collective-permute-start.9 = (bf16[816,256]{1,0:T(8,128)(2,1)S(1)}, bf16[816,256]{1,0:T(8,128)(2,1)S(1)}, u32[]{:S(2)}, u32[]{:S(2)}) collective-permute-start(bf16[816,256]{1,0:T(8,128)(2,1)S(1)} %pack_queries.3.refs_1_), channel_id=1, source_target_pairs={{0,1},{1,0},{2,3},{3,2},{4,5},{5,4},{6,7},{7,6},{8,9},{9,8},{10,11... | collective-permute-start | bytes 1253384 | tf_op jit(solution)/shard_map/ppermute | solution.py:257
  25.5 13.3 %collective-permute-start.10 = (bf16[768,256]{1,0:T(8,128)(2,1)S(1)}, bf16[768,256]{1,0:T(8,128)(2,1)S(1)}, u32[]{:S(2)}, u32[]{:S(2)}) collective-permute-start(bf16[768,256]{1,0:T(8,128)(2,1)S(1)} %get-tuple-element.59), channel_id=1, source_target_pairs={{0,4},{1,5},{2,14},{3,15},{4,8},{5,9},{6,2},{7,3},{8,12},{9,13},{1... | collective-permute-start | bytes 1179656 | tf_op jit(solution)/shard_map/ppermute | solution.py:257
  31.6 6.7 %collective-permute-start.12 = (bf16[384,256]{1,0:T(8,128)(2,1)S(1)}, bf16[384,256]{1,0:T(8,128)(2,1)S(1)}, u32[]{:S(2)}, u32[]{:S(2)}) collective-permute-start(bf16[384,256]{1,0:T(8,128)(2,1)S(1)} %get-tuple-element.64), channel_id=1, source_target_pairs={{0,1},{1,0},{2,3},{3,2},{4,5},{5,4},{6,7},{7,6},{8,9},{9,8},{10,11... | collective-permute-start | bytes 589832 | tf_op jit(solution)/shard_map/ppermute | solution.py:257
  31.7 11.4 %collective-permute-start.17 = (bf16[384,256]{1,0:T(8,128)(2,1)S(1)}, bf16[384,256]{1,0:T(8,128)(2,1)S(1)}, u32[]{:S(2)}, u32[]{:S(2)}) collective-permute-start(bf16[384,256]{1,0:T(8,128)(2,1)S(1)} %add_convert_fusion), channel_id=1, source_target_pairs={{0,2},{1,3},{2,0},{3,1},{4,6},{5,7},{6,4},{7,5},{8,10},{9,11},{10,... | collective-permute-start | bytes 589832 | tf_op jit(solution)/shard_map/ppermute | solution.py:257
  35.2 13.0 %collective-permute-start.14 = (bf16[768,256]{1,0:T(8,128)(2,1)S(1)}, bf16[768,256]{1,0:T(8,128)(2,1)S(1)}, u32[]{:S(2)}, u32[]{:S(2)}) collective-permute-start(bf16[768,256]{1,0:T(8,128)(2,1)S(1)} %get-tuple-element.68), channel_id=1, source_target_pairs={{0,4},{1,5},{2,14},{3,15},{4,8},{5,9},{6,2},{7,3},{8,12},{9,13},{1... | collective-permute-start | bytes 1179656 | tf_op jit(solution)/shard_map/ppermute | solution.py:257
  38.2 6.0 %collective-permute-start.11 = (bf16[384,256]{1,0:T(8,128)(2,1)S(1)}, bf16[384,256]{1,0:T(8,128)(2,1)S(1)}, u32[]{:S(2)}, u32[]{:S(2)}) collective-permute-start(bf16[384,256]{1,0:T(8,128)(2,1)S(1)} %get-tuple-element.63), channel_id=1, source_target_pairs={{0,1},{1,0},{2,3},{3,2},{4,5},{5,4},{6,7},{7,6},{8,9},{9,8},{10,11... | collective-permute-start | bytes 589832 | tf_op jit(solution)/shard_map/ppermute | solution.py:257
  38.3 4.8 %collective-permute-start.15 = (bf16[384,256]{1,0:T(8,128)(2,1)S(1)}, bf16[384,256]{1,0:T(8,128)(2,1)S(1)}, u32[]{:S(2)}, u32[]{:S(2)}) collective-permute-start(bf16[384,256]{1,0:T(8,128)(2,1)S(1)} %get-tuple-element.58), channel_id=1, source_target_pairs={{0,1},{1,0},{2,3},{3,2},{4,5},{5,4},{6,7},{7,6},{8,9},{9,8},{10,11... | collective-permute-start | bytes 589832 | tf_op jit(solution)/shard_map/ppermute | solution.py:257
  38.8 7.0 %collective-permute-start.13 = (bf16[384,256]{1,0:T(8,128)(2,1)S(1)}, bf16[384,256]{1,0:T(8,128)(2,1)S(1)}, u32[]{:S(2)}, u32[]{:S(2)}) collective-permute-start(bf16[384,256]{1,0:T(8,128)(2,1)S(1)} %add_convert_fusion.1), channel_id=1, source_target_pairs={{0,2},{1,3},{2,0},{3,1},{4,6},{5,7},{6,4},{7,5},{8,10},{9,11},{10,... | collective-permute-start | bytes 589832 | tf_op jit(solution)/shard_map/ppermute | solution.py:257
